TPU v7x, 256 devices: a whole 4x4x8 slice. The times are simulated.
256 devices in a mesh: table: 64 (over z, y, core), batch: 4 (over x).
Axes of the slice: x: 4, y: 4, z: 8, core: 2. Of those that a mesh axis runs over, the one named last changes fastest.
Arguments:
- embedding_table: bfloat16 [524288, 128], P('table'), may hold values from -6 to 6
- request_rows: int32 [256, 2048], P(('table', 'batch')), may hold values from -1 to 8191, as said below
- node_slots: int32 [262144, 2], P(('table', 'batch')), may hold values from 0 to 2047, as said below
- neighbours: int32 [262144, 8], P(('table', 'batch')), may hold values from 0 to 1023
- kept_edges: int32 [2, 262144, 8], P(None, ('table', 'batch')), may hold values 0 or 1
- weight_one: bfloat16 [128, 256], replicated, may hold values from -0.5 to 0.5
- weight_two: bfloat16 [256, 256], replicated, may hold values from -0.375 to 0.375
- proj_first: bfloat16 [256, 256], replicated, may hold values from -0.375 to 0.375
- proj_second: bfloat16 [256, 256], replicated, may hold values from -0.375 to 0.375
Outputs:
- table_grad: float32 [524288, 128], P(('table', 'batch'))
Inputs may be any that keep to these rules, and one draw needn't show every extreme that they name: `request_rows`: in each device's row, slab p (slots p * 32 to p * 32 + 31) lists rows of table index p, its used slots first and -1 in the rest. Every device fills some slab completely, and some table index receives a full slab from every device. `node_slots`: each entry names a used slot of its own device's request list, and every used slot is named by some node of that device.
All inputs are finite; a program needn't handle non-finite values. No bound on the sum of `kept_edges` on one device may be relied on, other than what follows from the above.
Results may differ from a plain program's by a relative error of at most 0.0095.
The roundings to bfloat16 on the way count: a program that leaves them out, or rounds other values in their place, can miss the bound.
Values may be sent and summed in bfloat16 or wider, within the bound.
No kernel may reach another device: no remote copies, remote signals or barrier semaphores. Data moves between devices by JAX's collectives and lax.ppermute only.
A program may use at most 128 MiB of HBM per device.

v0:
```python
import functools

import jax
import jax.numpy as jnp
from jax import lax
from jax.experimental import pallas as pl
from jax.experimental.pallas import tpu as pltpu
from jax.sharding import PartitionSpec as P

SEED_DEV = 256
TEMPER = 0.25
EPSILON = 1e-06
F32 = jnp.float32
BF16 = jnp.bfloat16
VMEM_BYTES = 48 * 1024 * 1024
VMEM = pl.BlockSpec(memory_space=pltpu.VMEM)


def nn(left, right):
    return lax.dot_general(left, right, (((1,), (0,)), ((), ())), preferred_element_type=F32)


def nt(left, right):
    return lax.dot_general(left, right, (((1,), (1,)), ((), ())), preferred_element_type=F32)


def tn(left, right):
    return lax.dot_general(left, right, (((0,), (0,)), ((), ())), preferred_element_type=F32)


def split(values):
    high = values.astype(BF16)
    low = (values - high.astype(F32)).astype(BF16)
    return jnp.concatenate([high, low], axis=0)


def call(kernel, outs, args, flops, moved, aliases=None):
    return pl.pallas_call(
        kernel,
        out_shape=outs,
        in_specs=[VMEM] * len(args),
        out_specs=[VMEM] * len(outs),
        input_output_aliases=aliases or {},
        compiler_params=pltpu.CompilerParams(vmem_limit_bytes=VMEM_BYTES),
        cost_estimate=pl.CostEstimate(flops=flops, bytes_accessed=moved, transcendentals=0),
    )(*args)


def edges_kernel(near_ref, counts_ref):
    views, slots, nodes = near_ref.shape
    rows = 32

    def step(block, carry):
        start = pl.multiple_of(block * rows, rows)
        ids = lax.broadcasted_iota(jnp.int32, (rows, nodes), 0) + start
        own = (ids == lax.broadcasted_iota(jnp.int32, (rows, nodes), 1)).astype(F32)
        for view in range(views):
            total = own
            for slot in range(slots):
                near = near_ref[view, slot : slot + 1, :]
                total = total + jnp.where(near == ids, 1.0, 0.0)
            counts_ref[view, pl.ds(start, rows), :] = total.astype(BF16)
        return carry

    lax.fori_loop(0, nodes // rows, step, 0)


def slots_kernel(slot_ref, counts_ref):
    hashes, nodes = slot_ref.shape
    rows = 32

    def step(block, carry):
        start = pl.multiple_of(block * rows, rows)
        ids = lax.broadcasted_iota(jnp.int32, (rows, nodes), 0) + start
        total = jnp.where(slot_ref[0:1, :] == ids, 1.0, 0.0)
        for which in range(1, hashes):
            total = total + jnp.where(slot_ref[which : which + 1, :] == ids, 1.0, 0.0)
        counts_ref[pl.ds(start, rows), :] = total.astype(BF16)
        return carry

    lax.fori_loop(0, counts_ref.shape[0] // rows, step, 0)


def forward_kernel(
    rows_ref, slots_ref, edges_ref, degree_ref, one_ref, two_ref, first_ref, second_ref,
    keys_ref, raw_ref, hidden_ref, inner_ref, slope_ref,
):
    seeds = SEED_DEV
    width = rows_ref.shape[1]
    features = split(tn(rows_ref[...], slots_ref[...]))
    for view in range(2):
        edges = edges_ref[view]
        degree = degree_ref[view : view + 1, :]
        summed = nn(features, edges)
        layer_in = ((summed[:width] + summed[width:]) / degree).astype(BF16)
        hidden = jnp.maximum(tn(one_ref[...], layer_in), 0.0).astype(BF16)
        hidden_ref[view] = hidden
        seed_in = (nn(hidden, edges[:, :seeds]) / degree[:, :seeds]).astype(BF16)
        inner = jnp.maximum(tn(two_ref[...], seed_in), 0.0).astype(BF16)
        before = tn(first_ref[...], inner)
        grown = jnp.exp(jnp.minimum(before, 0.0))
        near_zero = before * (1.0 + before * (0.5 + before * (1.0 / 6.0)))
        below = jnp.where(before > -0.01, near_zero, grown - 1.0)
        projected = jnp.where(before > 0.0, before, below).astype(BF16)
        raw = tn(second_ref[...], projected)
        scale = lax.rsqrt(jnp.sum(raw * raw, axis=0, keepdims=True) + EPSILON)
        span = slice(view * seeds, (view + 1) * seeds)
        keys_ref[:, span] = (raw * scale).astype(BF16)
        raw_ref[:, span] = raw
        inner_ref[:, span] = inner
        slope_ref[:, span] = jnp.where(before > 0.0, 1.0, grown)


def backward_kernel(
    key0_ref, key1_ref, key2_ref, key3_ref, raw_ref, hidden_ref, inner_ref, slope_ref,
    slots_ref, edges_ref, degree_ref, one_ref, two_ref, first_ref, second_ref,
    grads_ref, expo_ref,
):
    seeds = SEED_DEV
    keys_t = [ref[...] for ref in (key0_ref, key1_ref, key2_ref, key3_ref)]
    count = keys_t[0].shape[1]
    totals_own = jnp.zeros((1, count), F32)
    totals = []
    same = lax.broadcasted_iota(jnp.int32, (count, count), 0) == lax.broadcasted_iota(
        jnp.int32, (count, count), 1
    )
    for block in range(4):
        keys = keys_t[block].T
        total = jnp.zeros((count, 1), F32)
        for other in range(4):
            expo = jnp.exp(nn(keys, keys_t[other]) * (1.0 / TEMPER))
            if other == block:
                expo = jnp.where(same, 0.0, expo)
            total = total + jnp.sum(expo, axis=1, keepdims=True)
            if other == 0:
                expo_ref[block * count : (block + 1) * count, :] = expo
                totals_own = totals_own + jnp.sum(expo, axis=0, keepdims=True)
        totals.append(total)
    own_inverse = 1.0 / totals_own
    pulled = jnp.zeros((keys_t[0].shape[0], count), F32)
    for block in range(4):
        expo = expo_ref[block * count : (block + 1) * count, :]
        weights = (expo * (own_inverse + 1.0 / totals[block])).astype(BF16)
        pulled = pulled + nn(keys_t[block], weights)
    feature_grads = None
    for view in range(2):
        span = slice(view * seeds, (view + 1) * seeds)
        other = slice((1 - view) * seeds, (2 - view) * seeds)
        partner = key0_ref[:, other].astype(F32)
        key_grads = (pulled[:, span] - 2.0 * partner) * (1.0 / TEMPER)
        raw = raw_ref[:, span]
        scale = lax.rsqrt(jnp.sum(raw * raw, axis=0, keepdims=True) + EPSILON)
        along = jnp.sum(raw * key_grads, axis=0, keepdims=True) * (scale * scale)
        raw_grads = ((key_grads - raw * along) * scale).astype(BF16)
        grads = nn(second_ref[...], raw_grads).astype(BF16).astype(F32)
        grads = (grads * slope_ref[:, span]).astype(BF16)
        grads = nn(first_ref[...], grads).astype(BF16)
        grads = jnp.where(inner_ref[:, span] > 0, grads, jnp.zeros_like(grads))
        grads = nn(two_ref[...], grads).astype(BF16).astype(F32)
        degree = degree_ref[view : view + 1, :]
        wide = grads.shape[0]
        grads = nt(split(grads / degree[:, :seeds]), edges_ref[view, :, :seeds])
        grads = (grads[:wide] + grads[wide:]).astype(BF16)
        grads = jnp.where(hidden_ref[view] > 0, grads, jnp.zeros_like(grads))
        grads = nn(one_ref[...], grads).astype(BF16).astype(F32)
        grads = nt(split(grads / degree), edges_ref[view])
        feature_grads = grads if feature_grads is None else feature_grads + grads
    width = feature_grads.shape[0] // 2
    feature_grads = split(feature_grads[:width] + feature_grads[width:])
    slot_grads = nt(slots_ref[...], feature_grads)
    grads_ref[...] = (slot_grads[:, :width] + slot_grads[:, width:]).astype(BF16)


def scatter_kernel(row_ref, lane_ref, grads_ref, *rest, first):
    out_ref = rest[-1]
    count, width = grads_ref.shape
    parts = 4
    rows = out_ref.shape[0] // parts
    low = row_ref[...] & (rows - 1)
    hit = low == lax.broadcasted_iota(jnp.int32, (rows, count), 0)
    pick = jnp.where(hit, 1.0, 0.0).astype(BF16)
    grads = grads_ref[...].astype(F32)
    part_of = lane_ref[...]
    for part in range(parts):
        chosen = jnp.where(part_of == part, grads, 0.0).astype(BF16)
        added = nn(pick, chosen)
        span = slice(part * rows, (part + 1) * rows)
        if not first:
            added = added + rest[0][span, :]
        out_ref[span, :] = added


def body(
    embedding_table,
    request_rows,
    node_slots,
    neighbours,
    kept_edges,
    weight_one,
    weight_two,
    proj_first,
    proj_second,
):
    table_count = lax.axis_size("table")
    batch_count = lax.axis_size("batch")
    shard_rows, width = embedding_table.shape
    nodes = neighbours.shape[0]
    seeds = SEED_DEV
    requests = request_rows.reshape(table_count, -1)
    slot_count = requests.size

    def turn(value, by):
        return lax.ppermute(
            value, "batch", [(source, (source + by) % batch_count) for source in range(batch_count)]
        )

    def exchange(value):
        return [value] + [turn(value, by) for by in range(1, batch_count)]

    received = lax.all_to_all(requests, "table", split_axis=0, concat_axis=0, tiled=True)
    fetched = embedding_table[jnp.maximum(received, 0)]
    arrived = lax.all_to_all(fetched, "table", split_axis=0, concat_axis=0, tiled=True)
    rows = arrived.reshape(slot_count, width)

    near = jnp.where(kept_edges > 0, neighbours[None], -1).transpose(0, 2, 1)
    degree = 1.0 + jnp.sum(kept_edges, axis=2).astype(F32)
    (edges,) = call(
        edges_kernel,
        [jax.ShapeDtypeStruct((2, nodes, nodes), BF16)],
        [near],
        flops=60_000_000,
        moved=4 * nodes * nodes,
    )
    (slots,) = call(
        slots_kernel,
        [jax.ShapeDtypeStruct((slot_count, nodes), BF16)],
        [node_slots.T],
        flops=10_000_000,
        moved=2 * nodes * slot_count,
    )
    wide = weight_one.shape[1]
    keys, raw, hidden, inner, slope = call(
        forward_kernel,
        [
            jax.ShapeDtypeStruct((wide, 2 * seeds), BF16),
            jax.ShapeDtypeStruct((wide, 2 * seeds), F32),
            jax.ShapeDtypeStruct((2, wide, nodes), BF16),
            jax.ShapeDtypeStruct((wide, 2 * seeds), BF16),
            jax.ShapeDtypeStruct((wide, 2 * seeds), F32),
        ],
        [rows, slots, edges, degree, weight_one, weight_two, proj_first, proj_second],
        flops=2_400_000_000,
        moved=10_000_000,
    )
    group_keys = exchange(keys)
    grads = pl.pallas_call(
        backward_kernel,
        out_shape=jax.ShapeDtypeStruct((slot_count, width), BF16),
        in_specs=[VMEM] * 15,
        out_specs=VMEM,
        scratch_shapes=[pltpu.VMEM((2 * seeds * batch_count, 2 * seeds), F32)],
        compiler_params=pltpu.CompilerParams(vmem_limit_bytes=VMEM_BYTES),
        cost_estimate=pl.CostEstimate(
            flops=8_000_000_000, bytes_accessed=12_000_000, transcendentals=4_000_000
        ),
    )(
        *group_keys, raw, hidden, inner, slope, slots, edges, degree,
        weight_one, weight_two, proj_first, proj_second,
    )
    returned = lax.all_to_all(
        grads.reshape(table_count, -1, width), "table", split_axis=0, concat_axis=0, tiled=True
    ).reshape(slot_count, width)

    out_rows = shard_rows // batch_count
    part_rows = out_rows // 4
    offset = lax.axis_index("batch") * out_rows
    owned = exchange(received)
    parts = exchange(returned)
    total = None
    for index, piece in zip(owned, parts):
        index = index.reshape(-1) - offset
        lanes = jnp.broadcast_to((index // part_rows)[:, None], (slot_count, width))
        args = [index[None, :], lanes, piece] + ([] if total is None else [total])
        (total,) = call(
            functools.partial(scatter_kernel, first=total is None),
            [jax.ShapeDtypeStruct((out_rows, width), F32)],
            args,
            flops=1_000_000_000,
            moved=4_000_000,
            aliases={} if total is None else {3: 0},
        )
    return total


def solution(mesh):
    in_specs = (
        P("table", None),
        P(("table", "batch"), None),
        P(("table", "batch"), None),
        P(("table", "batch"), None),
        P(None, ("table", "batch"), None),
        P(),
        P(),
        P(),
        P(),
    )
    out_specs = P(("table", "batch"), None)
    return jax.shard_map(body, mesh=mesh, in_specs=in_specs, out_specs=out_specs, check_vma=False)
```

profile of v0, /device:TPU:1, one launch (start us, length us, event | category | flops | bytes accessed | tf_op | source)
XLA Modules:
  0.0 161.3 jit_solution(2039608553542212299)
XLA Ops:
  0.5 1.5 reduce.12
  2.7 13.2 %all-to-all-start = ((s32[64,1,32]{2,1,0:T(1,128)}), s32[64,1,32]{2,1,0:T(1,128)S(1)}, u32[]{:S(2)}, u32[]{:S(2)}) async-start(s32[64,1,32]{2,1,0:T(1,128)} %bitcast), calls=%async_computation | async-start | bytes 65536 | tf_op jit(solution)/shard_map/all_to_all | solution.py:220
  15.9 9.3 %all-to-all-done = s32[64,1,32]{2,1,0:T(1,128)S(1)} async-done(((s32[64,1,32]{2,1,0:T(1,128)}), s32[64,1,32]{2,1,0:T(1,128)S(1)}, u32[]{:S(2)}, u32[]{:S(2)}) %all-to-all-start) | async-done | bytes 8224 | tf_op jit(solution)/shard_map/all_to_all | solution.py:220
  26.1 8.1 %gather_fusion = bf16[2048,128]{1,0:T(8,128)(2,1)} fusion(bf16[8192,128]{1,0:T(8,128)(2,1)S(1)} %copy-done, s32[2048]{0:T(1024)S(1)} %broadcast_clamp_fusion), kind=kCustom, calls=%fused_computation | custom fusion | bytes 1056768 | tf_op jit(solution)/shard_map/gather | solution.py:221
  34.1 4.7 %all-to-all-start.1 = ((bf16[64,32,128]{2,1,0:T(8,128)(2,1)}), bf16[64,32,128]{2,1,0:T(8,128)(2,1)S(1)}, u32[]{:S(2)}, u32[]{:S(2)}) async-start(bf16[64,32,128]{2,1,0:T(8,128)(2,1)} %bitcast.16), calls=%async_computation.1 | async-start | bytes 1048576 | tf_op jit(solution)/shard_map/all_to_all | solution.py:222
  38.9 1.9 %shard_map.91.slots_ref = bf16[2048,1024]{1,0:T(8,128)(2,1)S(1)} custom-call(s32[2,1024]{1,0:T(2,128)S(1)} %bitcast.15), custom_call_target="tpu_custom_call" | custom-call | flops 10000000 | bytes 4194304 | tf_op jit(solution)/shard_map/pallas_call | solution.py:38
  40.8 1.9 %copy-done.1 = bf16[2048,1024]{1,0:T(8,128)(2,1)} copy-done((bf16[2048,1024]{1,0:T(8,128)(2,1)}, bf16[2048,1024]{1,0:T(8,128)(2,1)S(1)}, u32[]{:S(2)}) %copy-start.1) | copy-done | bytes 4194328
  42.8 7.8 %shard_map.92.edges_ref = bf16[2,1024,1024]{2,1,0:T(8,128)(2,1)S(1)} custom-call(s32[2,8,1024]{2,1,0:T(8,128)S(1)} %get-tuple-element.18.near_ref), custom_call_target="tpu_custom_call" | custom-call | flops 60000000 | bytes 4194304 | tf_op jit(solution)/shard_map/pallas_call | solution.py:38
  50.7 2.0 %copy-done.2 = bf16[2,1024,1024]{2,1,0:T(8,128)(2,1)} copy-done((bf16[2,1024,1024]{2,1,0:T(8,128)(2,1)}, bf16[2,1024,1024]{2,1,0:T(8,128)(2,1)S(1)}, u32[]{:S(2)}) %copy-start.2) | copy-done | bytes 4194328
  52.7 4.0 %all-to-all-done.1 = bf16[64,32,128]{2,1,0:T(8,128)(2,1)S(1)} async-done(((bf16[64,32,128]{2,1,0:T(8,128)(2,1)}), bf16[64,32,128]{2,1,0:T(8,128)(2,1)S(1)}, u32[]{:S(2)}, u32[]{:S(2)}) %all-to-all-start.1) | async-done | bytes 524320 | tf_op jit(solution)/shard_map/all_to_all | solution.py:222
  56.7 7.5 %shard_map.93 = (bf16[256,512]{1,0:T(8,128)(2,1)S(1)}, f32[256,512]{1,0:T(8,128)S(1)}, bf16[2,256,1024]{2,1,0:T(8,128)(2,1)S(1)}, bf16[256,512]{1,0:T(8,128)(2,1)S(1)}, f32[256,512]{1,0:T(8,128)S(1)}) custom-call(bf16[2048,128]{1,0:T(8,128)(2,1)S(1)} %bitcast.10, bf16[2048,1024]{1,0:T(8,128)(2,1)} %copy-done.1, bf16[2,1024,1024]{2,1,0:T(8,128)(2,1)} %copy-done.2, ...), custom_call_target="tpu_custom_call" | custom-call | flops 2400000000 | bytes 10000000 | tf_op jit(solution)/shard_map/pallas_call | solution.py:38
  67.6 1.2 collective-permute-start.1
  68.8 2.5 %collective-permute-start.2 = (bf16[256,512]{1,0:T(8,128)(2,1)S(1)}, bf16[256,512]{1,0:T(8,128)(2,1)S(1)}, u32[]{:S(2)}, u32[]{:S(2)}) collective-permute-start(bf16[256,512]{1,0:T(8,128)(2,1)S(1)} %get-tuple-element.10.key0_ref), channel_id=1, source_target_pairs={{0,2},{1,3},{2,0},{3,1},{4,6},{5,7},{6,4},{7,5},{8,10},{9,11},{10,... | collective-permute-start | bytes 786440 | tf_op jit(solution)/shard_map/ppermute | solution.py:213
  71.3 1.2 collective-permute-start.3
  73.7 2.6 %collective-permute-done.1.key1_ref = bf16[256,512]{1,0:T(8,128)(2,1)S(1)} collective-permute-done((bf16[256,512]{1,0:T(8,128)(2,1)S(1)}, bf16[256,512]{1,0:T(8,128)(2,1)S(1)}, u32[]{:S(2)}, u32[]{:S(2)}) %collective-permute-start.1) | collective-permute-done | bytes 262176 | tf_op jit(solution)/shard_map/ppermute | solution.py:213
  76.3 1.3 collective-permute-start
  77.6 5.3 %collective-permute-done.2.key2_ref = bf16[256,512]{1,0:T(8,128)(2,1)S(1)} collective-permute-done((bf16[256,512]{1,0:T(8,128)(2,1)S(1)}, bf16[256,512]{1,0:T(8,128)(2,1)S(1)}, u32[]{:S(2)}, u32[]{:S(2)}) %collective-permute-start.2) | collective-permute-done | bytes 262176 | tf_op jit(solution)/shard_map/ppermute | solution.py:213
  82.9 1.2 copy-done.9
  84.1 1.0 copy-done.11
  85.2 1.0 copy-done.13
  87.2 12.6 %shard_map.94 = bf16[2048,128]{1,0:T(8,128)(2,1)} custom-call(bf16[256,512]{1,0:T(8,128)(2,1)S(1)} %get-tuple-element.10.key0_ref, bf16[256,512]{1,0:T(8,128)(2,1)S(1)} %collective-permute-done.1.key1_ref, bf16[256,512]{1,0:T(8,128)(2,1)S(1)} %collective-permute-done.2.key2_ref, bf16[256,512]{1,0:T(8,128)(2,1)} %collective-permute-done.3.key3_ref, ...), custom_call_target="tpu_custom_call" | custom-call | flops 8000000000 | bytes 12000000 | tf_op jit(solution)/shard_map/pallas_call | solution.py:256
  99.7 7.9 %all-to-all-start.2 = ((bf16[64,32,128]{2,1,0:T(8,128)(2,1)}), bf16[64,32,128]{2,1,0:T(8,128)(2,1)S(1)}, u32[]{:S(2)}, u32[]{:S(2)}) async-start(bf16[64,32,128]{2,1,0:T(8,128)(2,1)} %bitcast.6), calls=%async_computation.2 | async-start | bytes 1048576 | tf_op jit(solution)/shard_map/all_to_all | solution.py:270
  108.8 16.7 %all-to-all-done.2 = bf16[64,32,128]{2,1,0:T(8,128)(2,1)S(1)} async-done(((bf16[64,32,128]{2,1,0:T(8,128)(2,1)}), bf16[64,32,128]{2,1,0:T(8,128)(2,1)S(1)}, u32[]{:S(2)}, u32[]{:S(2)}) %all-to-all-start.2) | async-done | bytes 524320 | tf_op jit(solution)/shard_map/all_to_all | solution.py:270
  125.4 1.2 collective-permute-start.8
  126.6 1.9 %collective-permute-start.6 = (bf16[2048,128]{1,0:T(8,128)(2,1)S(1)}, bf16[2048,128]{1,0:T(8,128)(2,1)}, u32[]{:S(2)}, u32[]{:S(2)}) collective-permute-start(bf16[2048,128]{1,0:T(8,128)(2,1)S(1)} %bitcast.12), channel_id=1, source_target_pairs={{0,2},{1,3},{2,0},{3,1},{4,6},{5,7},{6,4},{7,5},{8,10},{9,11},{10,... | collective-permute-start | bytes 1572872 | tf_op jit(solution)/shard_map/ppermute | solution.py:213
  128.4 1.5 collective-permute-start.4
  130.7 3.3 %shard_map.95.rest_0_ = f32[2048,128]{1,0:T(8,128)} custom-call(s32[1,2048]{1,0:T(1,128)S(1)} %sub.121.row_ref, s32[2048,128]{1,0:T(8,128)S(1)} %broadcast_in_dim.25.lane_ref, bf16[2048,128]{1,0:T(8,128)(2,1)S(1)} %bitcast.14), custom_call_target="tpu_custom_call" | custom-call | flops 1000000000 | bytes 4000000 | tf_op jit(solution)/shard_map/pallas_call | solution.py:38
  134.0 5.9 %collective-permute-done.8.grads_ref = bf16[2048,128]{1,0:T(8,128)(2,1)} collective-permute-done((bf16[2048,128]{1,0:T(8,128)(2,1)S(1)}, bf16[2048,128]{1,0:T(8,128)(2,1)}, u32[]{:S(2)}, u32[]{:S(2)}) %collective-permute-start.8) | collective-permute-done | bytes 524320 | tf_op jit(solution)/shard_map/ppermute | solution.py:213
  140.2 4.7 %shard_map.96.rest_0_ = f32[2048,128]{1,0:T(8,128)} custom-call(s32[1,2048]{1,0:T(1,128)S(1)} %sub.116.row_ref, s32[2048,128]{1,0:T(8,128)S(1)} %broadcast_in_dim.24.lane_ref, bf16[2048,128]{1,0:T(8,128)(2,1)} %collective-permute-done.8.grads_ref, f32[2048,128]{1,0:T(8,128)} %shard_map.95.rest_0_), custom_call_target="tpu_custom_call", output_to_operand_aliasing={{}: (3, {})} | custom-call | flops 1000000000 | bytes 4000000 | tf_op jit(solution)/shard_map/pallas_call | solution.py:38
  144.9 6.6 %collective-permute-done.6.grads_ref = bf16[2048,128]{1,0:T(8,128)(2,1)} collective-permute-done((bf16[2048,128]{1,0:T(8,128)(2,1)S(1)}, bf16[2048,128]{1,0:T(8,128)(2,1)}, u32[]{:S(2)}, u32[]{:S(2)}) %collective-permute-start.6) | collective-permute-done | bytes 524320 | tf_op jit(solution)/shard_map/ppermute | solution.py:213
  151.8 4.7 %shard_map.97.rest_0_ = f32[2048,128]{1,0:T(8,128)} custom-call(s32[1,2048]{1,0:T(1,128)S(1)} %sub.112.row_ref, s32[2048,128]{1,0:T(8,128)S(1)} %broadcast_in_dim.23.lane_ref, bf16[2048,128]{1,0:T(8,128)(2,1)} %collective-permute-done.6.grads_ref, f32[2048,128]{1,0:T(8,128)} %shard_map.96.rest_0_), custom_call_target="tpu_custom_call", output_to_operand_aliasing={{}: (3, {})} | custom-call | flops 1000000000 | bytes 4000000 | tf_op jit(solution)/shard_map/pallas_call | solution.py:38
  156.8 4.5 %shard_map.98 = f32[2048,128]{1,0:T(8,128)} custom-call(s32[1,2048]{1,0:T(1,128)S(1)} %sub.108.row_ref, s32[2048,128]{1,0:T(8,128)S(1)} %broadcast_in_dim.20.lane_ref, bf16[2048,128]{1,0:T(8,128)(2,1)S(1)} %collective-permute-done.4.grads_ref, f32[2048,128]{1,0:T(8,128)} %shard_map.97.rest_0_), custom_call_target="tpu_custom_call", output_to_operand_aliasing={{}: (3, {})} | custom-call | flops 1000000000 | bytes 4000000 | tf_op jit(solution)/shard_map/pallas_call | solution.py:38
  (64 shorter events, 10.4 us)
Async XLA Ops:
  0.0 26.0 %copy-start = (bf16[8192,128]{1,0:T(8,128)(2,1)S(1)}, bf16[8192,128]{1,0:T(8,128)(2,1)}, u32[]{:S(2)}) copy-start(bf16[8192,128]{1,0:T(8,128)(2,1)} %param.9) | copy-start | bytes 6291460
  0.0 38.9 %copy-start.7 = (s32[1024,2]{0,1:T(2,128)S(1)}, s32[1024,2]{0,1:T(2,128)}, u32[]{:S(2)}) copy-start(s32[1024,2]{0,1:T(2,128)} %param.11) | copy-start | bytes 24580
  2.7 22.5 %all-to-all-start = ((s32[64,1,32]{2,1,0:T(1,128)}), s32[64,1,32]{2,1,0:T(1,128)S(1)}, u32[]{:S(2)}, u32[]{:S(2)}) async-start(s32[64,1,32]{2,1,0:T(1,128)} %bitcast), calls=%async_computation | async-start | bytes 65536 | tf_op jit(solution)/shard_map/all_to_all | solution.py:220
  26.0 16.7 %copy-start.16 = (s32[2,1024,8]{1,2,0:T(8,128)S(1)}, s32[2,1024,8]{1,2,0:T(8,128)}, u32[]{:S(2)}) copy-start(s32[2,1024,8]{1,2,0:T(8,128)} %param.13) | copy-start | bytes 196612
  26.1 16.7 %copy-start.17 = (s32[1024,8]{0,1:T(8,128)S(1)}, s32[1024,8]{0,1:T(8,128)}, u32[]{:S(2)}) copy-start(s32[1024,8]{0,1:T(8,128)} %param.12) | copy-start | bytes 98308
  34.1 22.6 %all-to-all-start.1 = ((bf16[64,32,128]{2,1,0:T(8,128)(2,1)}), bf16[64,32,128]{2,1,0:T(8,128)(2,1)S(1)}, u32[]{:S(2)}, u32[]{:S(2)}) async-start(bf16[64,32,128]{2,1,0:T(8,128)(2,1)} %bitcast.16), calls=%async_computation.1 | async-start | bytes 1048576 | tf_op jit(solution)/shard_map/all_to_all | solution.py:222
  38.9 17.8 %copy-start.3 = (bf16[256,256]{1,0:T(8,128)(2,1)S(1)}, bf16[256,256]{1,0:T(8,128)(2,1)}, u32[]{:S(2)}) copy-start(bf16[256,256]{1,0:T(8,128)(2,1)} %two_ref.3) | copy-start | bytes 393220
  38.9 17.8 %copy-start.4 = (bf16[256,256]{1,0:T(8,128)(2,1)S(1)}, bf16[256,256]{1,0:T(8,128)(2,1)}, u32[]{:S(2)}) copy-start(bf16[256,256]{1,0:T(8,128)(2,1)} %first_ref.3) | copy-start | bytes 393220
  38.9 17.8 %copy-start.5 = (bf16[256,256]{1,0:T(8,128)(2,1)S(1)}, bf16[256,256]{1,0:T(8,128)(2,1)}, u32[]{:S(2)}) copy-start(bf16[256,256]{1,0:T(8,128)(2,1)} %second_ref.3) | copy-start | bytes 393220
  38.9 17.8 %copy-start.6 = (bf16[128,256]{1,0:T(8,128)(2,1)S(1)}, bf16[128,256]{1,0:T(8,128)(2,1)}, u32[]{:S(2)}) copy-start(bf16[128,256]{1,0:T(8,128)(2,1)} %one_ref.3) | copy-start | bytes 196612
  40.8 1.9 %copy-start.1 = (bf16[2048,1024]{1,0:T(8,128)(2,1)}, bf16[2048,1024]{1,0:T(8,128)(2,1)S(1)}, u32[]{:S(2)}) copy-start(bf16[2048,1024]{1,0:T(8,128)(2,1)S(1)} %shard_map.91.slots_ref) | copy-start | bytes 12582916
  50.7 2.0 %copy-start.2 = (bf16[2,1024,1024]{2,1,0:T(8,128)(2,1)}, bf16[2,1024,1024]{2,1,0:T(8,128)(2,1)S(1)}, u32[]{:S(2)}) copy-start(bf16[2,1024,1024]{2,1,0:T(8,128)(2,1)S(1)} %shard_map.92.edges_ref) | copy-start | bytes 12582916
  64.3 1.0 copy-start.8
  65.2 0.9 copy-start.10
  66.1 0.8 copy-start.12
  66.9 0.7 copy-start.14
  67.6 8.7 %collective-permute-start.1 = (bf16[256,512]{1,0:T(8,128)(2,1)S(1)}, bf16[256,512]{1,0:T(8,128)(2,1)S(1)}, u32[]{:S(2)}, u32[]{:S(2)}) collective-permute-start(bf16[256,512]{1,0:T(8,128)(2,1)S(1)} %get-tuple-element.10.key0_ref), channel_id=1, source_target_pairs={{0,1},{1,2},{2,3},{3,0},{4,5},{5,6},{6,7},{7,4},{8,9},{9,10},{10,1... | collective-permute-start | bytes 786440 | tf_op jit(solution)/shard_map/ppermute | solution.py:213
  68.8 14.1 %collective-permute-start.2 = (bf16[256,512]{1,0:T(8,128)(2,1)S(1)}, bf16[256,512]{1,0:T(8,128)(2,1)S(1)}, u32[]{:S(2)}, u32[]{:S(2)}) collective-permute-start(bf16[256,512]{1,0:T(8,128)(2,1)S(1)} %get-tuple-element.10.key0_ref), channel_id=1, source_target_pairs={{0,2},{1,3},{2,0},{3,1},{4,6},{5,7},{6,4},{7,5},{8,10},{9,11},{10,... | collective-permute-start | bytes 786440 | tf_op jit(solution)/shard_map/ppermute | solution.py:213
  71.3 11.7 %collective-permute-start.3 = (bf16[256,512]{1,0:T(8,128)(2,1)S(1)}, bf16[256,512]{1,0:T(8,128)(2,1)}, u32[]{:S(2)}, u32[]{:S(2)}) collective-permute-start(bf16[256,512]{1,0:T(8,128)(2,1)S(1)} %get-tuple-element.10.key0_ref), channel_id=1, source_target_pairs={{0,3},{1,0},{2,1},{3,2},{4,7},{5,4},{6,5},{7,6},{8,11},{9,8},{10,9... | collective-permute-start | bytes 786440 | tf_op jit(solution)/shard_map/ppermute | solution.py:213
  72.4 35.4 %collective-permute-start.7 = (s32[64,32]{1,0:T(8,128)S(1)}, s32[64,32]{1,0:T(8,128)}, u32[]{:S(2)}, u32[]{:S(2)}) collective-permute-start(s32[64,32]{1,0:T(8,128)S(1)} %bitcast.18), channel_id=1, source_target_pairs={{0,1},{1,2},{2,3},{3,0},{4,5},{5,6},{6,7},{7,4},{8,9},{9,10},{10,1... | collective-permute-start | bytes 24584 | tf_op jit(solution)/shard_map/ppermute | solution.py:213
  72.7 35.9 %collective-permute-start.5 = (s32[64,32]{1,0:T(8,128)S(1)}, s32[64,32]{1,0:T(8,128)S(1)}, u32[]{:S(2)}, u32[]{:S(2)}) collective-permute-start(s32[64,32]{1,0:T(8,128)S(1)} %bitcast.19), channel_id=1, source_target_pairs={{0,2},{1,3},{2,0},{3,1},{4,6},{5,7},{6,4},{7,5},{8,10},{9,11},{10,... | collective-permute-start | bytes 24584 | tf_op jit(solution)/shard_map/ppermute | solution.py:213
  76.3 32.4 %collective-permute-start = (s32[64,32]{1,0:T(8,128)S(1)}, s32[64,32]{1,0:T(8,128)S(1)}, u32[]{:S(2)}, u32[]{:S(2)}) collective-permute-start(s32[64,32]{1,0:T(8,128)S(1)} %bitcast.20), channel_id=1, source_target_pairs={{0,3},{1,0},{2,1},{3,2},{4,7},{5,4},{6,5},{7,6},{8,11},{9,8},{10,9... | collective-permute-start | bytes 24584 | tf_op jit(solution)/shard_map/ppermute | solution.py:213
  82.9 1.2 copy-start.9
  84.1 1.0 copy-start.11
  85.2 1.0 copy-start.13
  86.2 0.9 copy-start.15
  99.7 25.7 %all-to-all-start.2 = ((bf16[64,32,128]{2,1,0:T(8,128)(2,1)}), bf16[64,32,128]{2,1,0:T(8,128)(2,1)S(1)}, u32[]{:S(2)}, u32[]{:S(2)}) async-start(bf16[64,32,128]{2,1,0:T(8,128)(2,1)} %bitcast.6), calls=%async_computation.2 | async-start | bytes 1048576 | tf_op jit(solution)/shard_map/all_to_all | solution.py:270
  125.4 14.4 %collective-permute-start.8 = (bf16[2048,128]{1,0:T(8,128)(2,1)S(1)}, bf16[2048,128]{1,0:T(8,128)(2,1)}, u32[]{:S(2)}, u32[]{:S(2)}) collective-permute-start(bf16[2048,128]{1,0:T(8,128)(2,1)S(1)} %bitcast.11), channel_id=1, source_target_pairs={{0,1},{1,2},{2,3},{3,0},{4,5},{5,6},{6,7},{7,4},{8,9},{9,10},{10,1... | collective-permute-start | bytes 1572872 | tf_op jit(solution)/shard_map/ppermute | solution.py:213
  126.6 24.9 %collective-permute-start.6 = (bf16[2048,128]{1,0:T(8,128)(2,1)S(1)}, bf16[2048,128]{1,0:T(8,128)(2,1)}, u32[]{:S(2)}, u32[]{:S(2)}) collective-permute-start(bf16[2048,128]{1,0:T(8,128)(2,1)S(1)} %bitcast.12), channel_id=1, source_target_pairs={{0,2},{1,3},{2,0},{3,1},{4,6},{5,7},{6,4},{7,5},{8,10},{9,11},{10,... | collective-permute-start | bytes 1572872 | tf_op jit(solution)/shard_map/ppermute | solution.py:213
  128.4 28.0 %collective-permute-start.4 = (bf16[2048,128]{1,0:T(8,128)(2,1)S(1)}, bf16[2048,128]{1,0:T(8,128)(2,1)S(1)}, u32[]{:S(2)}, u32[]{:S(2)}) collective-permute-start(bf16[2048,128]{1,0:T(8,128)(2,1)S(1)} %bitcast.13), channel_id=1, source_target_pairs={{0,3},{1,0},{2,1},{3,2},{4,7},{5,4},{6,5},{7,6},{8,11},{9,8},{10,9... | collective-permute-start | bytes 1572872 | tf_op jit(solution)/shard_map/ppermute | solution.py:213
where the time goes:
time: 162 us; the launch traced here: 161 us
  waiting for transfers between devices  50.4 us (31%)
  Pallas kernels  47 us (29%)
  starting transfers between devices  37.7 us (23%)
  local copies, waits for them, and re-layouts  22.8 us (14%)
  other arithmetic  3.13 us (2%)
    pallas_call x7, Pallas kernels, call(): pl.pallas_call(kernel, out_shape=outs, in_specs=[VMEM] * len(args), out_s...  34.5 us
    ppermute x9, waiting for transfers between devices, turn(): lax.ppermute(value, 'batch', [(source, (source + by) % batch_count) for s...  20.4 us
    all_to_all x1, waiting for transfers between devices, body(): lax.all_to_all(grads.reshape(table_count, -1, width), 'table', split_axis...  16.7 us
    all_to_all x1, starting transfers between devices, body(): lax.all_to_all(requests, 'table', split_axis=0, concat_axis=0, tiled=True)  13.2 us
    pallas_call x1, Pallas kernels, body(): pl.pallas_call(backward_kernel, out_shape=jax.ShapeDtypeStruct((slot_coun...  12.6 us
    unnamed x37, local copies, waits for them, and re-layouts  12.1 us
    ppermute x9, starting transfers between devices, turn(): lax.ppermute(value, 'batch', [(source, (source + by) % batch_count) for s...  11.9 us
    all_to_all x1, waiting for transfers between devices, body(): lax.all_to_all(requests, 'table', split_axis=0, concat_axis=0, tiled=True)  9.3 us
  transfers between devices with their start and end apart: 12, of which 7 were waited for; matrix products, arithmetic and copies ran while one was open for 2% of the time, Pallas kernels for 22%

commit v1 on v0

v1 whole, which is shorter than its diff:
```python
import functools

import jax
import jax.numpy as jnp
from jax import lax
from jax.experimental import pallas as pl
from jax.experimental.pallas import tpu as pltpu
from jax.sharding import PartitionSpec as P

SEED_DEV = 256
TEMPER = 0.25
EPSILON = 1e-06
F32 = jnp.float32
BF16 = jnp.bfloat16
VMEM = pl.BlockSpec(memory_space=pltpu.VMEM)
HBM = pl.BlockSpec(memory_space=pltpu.HBM)


def nn(left, right):
    return lax.dot_general(left, right, (((1,), (0,)), ((), ())), preferred_element_type=F32)


def nt(left, right):
    return lax.dot_general(left, right, (((1,), (1,)), ((), ())), preferred_element_type=F32)


def tn(left, right):
    return lax.dot_general(left, right, (((0,), (0,)), ((), ())), preferred_element_type=F32)


def split(values):
    high = values.astype(BF16)
    low = (values - high.astype(F32)).astype(BF16)
    return jnp.concatenate([high, low], axis=0)


def call(kernel, outs, args, flops, moved, mib, scratch=(), far=(), far_outs=()):
    return pl.pallas_call(
        kernel,
        out_shape=outs,
        in_specs=[
            HBM if place in far else VMEM for place in range(len(args))
        ],
        out_specs=[HBM if place in far_outs else VMEM for place in range(len(outs))],
        scratch_shapes=list(scratch),
        compiler_params=pltpu.CompilerParams(vmem_limit_bytes=mib * 1024 * 1024),
        cost_estimate=pl.CostEstimate(flops=flops, bytes_accessed=moved, transcendentals=0),
    )(*args)


TILE, LANES, ROWS = 16, 128, 64


def spread(row, kind):
    return jnp.broadcast_to(row, (TILE, LANES)).astype(kind)


def places(axis):
    return lax.broadcasted_iota(jnp.int32, (TILE, LANES), axis)


def edges_kernel(near_ref, kept_ref, edges_far, edges_ref, sem):
    views, degree, nodes = kept_ref.shape
    none = jnp.zeros((), BF16)
    copies = []
    for part in range(nodes // LANES):
        span = slice(part * LANES, (part + 1) * LANES)
        nears = [spread(near_ref[slot : slot + 1, span], jnp.int16) for slot in range(degree)]
        kept = [
            [spread(kept_ref[view, slot : slot + 1, span], BF16) for slot in range(degree)]
            for view in range(views)
        ]

        def step(block, carry):
            for tile in range(ROWS // TILE):
                start = pl.multiple_of(block * ROWS + tile * TILE, TILE)
                ids = places(0) + start
                own = jnp.where(ids == places(1) + part * LANES, 1.0, 0.0).astype(BF16)
                ids = ids.astype(jnp.int16)
                totals = [own] * views
                for slot in range(degree):
                    hit = nears[slot] == ids
                    for view in range(views):
                        totals[view] = totals[view] + jnp.where(hit, kept[view][slot], none)
                for view in range(views):
                    edges_ref[view, pl.ds(start, TILE), span] = totals[view]
            return carry

        lax.fori_loop(0, nodes // ROWS, step, 0)
        copies.append(
            pltpu.make_async_copy(edges_ref.at[:, :, span], edges_far.at[:, :, span], sem.at[part])
        )
        copies[-1].start()
    for copy in copies:
        copy.wait()


def slots_kernel(slot_ref, slots_far, slots_ref, sem):
    hashes, nodes = slot_ref.shape
    one, none = jnp.ones((), BF16), jnp.zeros((), BF16)
    copies = []
    for part in range(nodes // LANES):
        span = slice(part * LANES, (part + 1) * LANES)
        named = [spread(slot_ref[which : which + 1, span], jnp.int16) for which in range(hashes)]

        def step(block, carry):
            for tile in range(ROWS // TILE):
                start = pl.multiple_of(block * ROWS + tile * TILE, TILE)
                ids = (places(0) + start).astype(jnp.int16)
                total = jnp.where(named[0] == ids, one, none)
                for which in range(1, hashes):
                    total = total + jnp.where(named[which] == ids, one, none)
                slots_ref[pl.ds(start, TILE), span] = total
            return carry

        lax.fori_loop(0, slots_ref.shape[0] // ROWS, step, 0)
        copies.append(
            pltpu.make_async_copy(slots_ref.at[:, span], slots_far.at[:, span], sem.at[part])
        )
        copies[-1].start()
    for copy in copies:
        copy.wait()


def slot_parts(source, target, sems):
    count = sems.shape[0]
    part = target.shape[0] // count
    spans = [pl.ds(place * part, part) for place in range(count)]
    return [
        pltpu.make_async_copy(source.at[span], target.at[span], sems.at[place])
        for place, span in enumerate(spans)
    ]


def forward_kernel(
    rows_ref, slots_ref, edges_ref, degree_ref, one_ref, two_ref, first_ref, second_ref,
    keys_ref, raw_ref, hidden_ref, inner_ref, slope_ref,
):
    seeds = SEED_DEV
    width = rows_ref.shape[1]
    features = split(tn(rows_ref[...], slots_ref[...]))
    for view in range(2):
        edges = edges_ref[view]
        degree = degree_ref[view : view + 1, :]
        summed = nn(features, edges)
        layer_in = ((summed[:width] + summed[width:]) / degree).astype(BF16)
        hidden = jnp.maximum(tn(one_ref[...], layer_in), 0.0).astype(BF16)
        hidden_ref[view] = hidden
        seed_in = (nn(hidden, edges[:, :seeds]) / degree[:, :seeds]).astype(BF16)
        inner = jnp.maximum(tn(two_ref[...], seed_in), 0.0).astype(BF16)
        before = tn(first_ref[...], inner)
        grown = jnp.exp(jnp.minimum(before, 0.0))
        near_zero = before * (1.0 + before * (0.5 + before * (1.0 / 6.0)))
        below = jnp.where(before > -0.01, near_zero, grown - 1.0)
        projected = jnp.where(before > 0.0, before, below).astype(BF16)
        raw = tn(second_ref[...], projected)
        scale = lax.rsqrt(jnp.sum(raw * raw, axis=0, keepdims=True) + EPSILON)
        span = slice(view * seeds, (view + 1) * seeds)
        keys_ref[:, span] = (raw * scale).astype(BF16)
        raw_ref[:, span] = raw
        inner_ref[:, span] = inner
        slope_ref[:, span] = jnp.where(before > 0.0, 1.0, grown)


def flip(row):
    return jnp.broadcast_to(row, (128, row.shape[1])).T[:, :1]


def pair_expo(left, right_t, same=None):
    expo = jnp.exp(nn(left, right_t) * (1.0 / TEMPER))
    return expo if same is None else jnp.where(same, 0.0, expo)


def diagonal(count):
    down = lax.broadcasted_iota(jnp.int32, (count, count), 0)
    return down == lax.broadcasted_iota(jnp.int32, (count, count), 1)


def down_sum(expo):
    return jnp.sum(expo, axis=0, keepdims=True)


def across_sum(expo):
    return jnp.sum(expo, axis=1, keepdims=True)


def early_kernel(key0_ref, key1_ref, key3_ref, expo_ref, total0_ref, totals_ref):
    own, ahead, behind = key0_ref[...], key1_ref[...], key3_ref[...]
    count = own.shape[1]
    same = diagonal(count)
    expo = pair_expo(own.T, own, same)
    expo_ref[:count, :] = expo
    total0 = down_sum(expo)
    left = ahead.T
    expo = pair_expo(left, own)
    expo_ref[count : 2 * count, :] = expo
    total0 = total0 + down_sum(expo)
    total1 = across_sum(expo) + across_sum(pair_expo(left, ahead, same))
    left = behind.T
    expo = pair_expo(left, own)
    expo_ref[2 * count :, :] = expo
    total0 = total0 + down_sum(expo)
    total3 = across_sum(expo) + across_sum(pair_expo(left, behind, same))
    expo = pair_expo(left, ahead)
    total3 = total3 + across_sum(expo)
    total1 = total1 + flip(down_sum(expo))
    total0_ref[...] = total0
    totals_ref[:count, :] = total1
    totals_ref[count:, :] = total3


def backward_kernel(
    key0_ref, key1_ref, key3_ref, key2_ref, expo_ref, total0_ref, totals_ref,
    raw_ref, hidden_ref, inner_ref, slope_ref,
    slots_ref, edges_ref, degree_ref, one_ref, two_ref, first_ref, second_ref,
    grads_ref,
):
    seeds = SEED_DEV
    far = key2_ref[...]
    count = far.shape[1]
    left = far.T
    last = pair_expo(left, key0_ref[...])
    total0 = total0_ref[...] + down_sum(last)
    total2 = across_sum(last) + across_sum(pair_expo(left, far, diagonal(count)))
    expo = pair_expo(left, key1_ref[...])
    total2 = total2 + across_sum(expo)
    total1 = totals_ref[:count, :] + flip(down_sum(expo))
    expo = pair_expo(left, key3_ref[...])
    total2 = total2 + across_sum(expo)
    total3 = totals_ref[count:, :] + flip(down_sum(expo))
    own_inverse = 1.0 / total0
    pulled = jnp.zeros(far.shape, F32)
    blocks = (
        (key0_ref, expo_ref[:count, :], flip(total0)),
        (key1_ref, expo_ref[count : 2 * count, :], total1),
        (key3_ref, expo_ref[2 * count :, :], total3),
        (key2_ref, last, total2),
    )
    for key_ref, expo, total in blocks:
        weights = (expo * (own_inverse + 1.0 / total)).astype(BF16)
        pulled = pulled + nn(key_ref[...], weights)
    feature_grads = None
    for view in range(2):
        span = slice(view * seeds, (view + 1) * seeds)
        other = slice((1 - view) * seeds, (2 - view) * seeds)
        partner = key0_ref[:, other].astype(F32)
        key_grads = (pulled[:, span] - 2.0 * partner) * (1.0 / TEMPER)
        raw = raw_ref[:, span]
        scale = lax.rsqrt(jnp.sum(raw * raw, axis=0, keepdims=True) + EPSILON)
        along = jnp.sum(raw * key_grads, axis=0, keepdims=True) * (scale * scale)
        raw_grads = ((key_grads - raw * along) * scale).astype(BF16)
        grads = nn(second_ref[...], raw_grads).astype(BF16).astype(F32)
        grads = (grads * slope_ref[:, span]).astype(BF16)
        grads = nn(first_ref[...], grads).astype(BF16)
        grads = jnp.where(inner_ref[:, span] > 0, grads, jnp.zeros_like(grads))
        grads = nn(two_ref[...], grads).astype(BF16).astype(F32)
        degree = degree_ref[view : view + 1, :]
        wide = grads.shape[0]
        grads = nt(split(grads / degree[:, :seeds]), edges_ref[view, :, :seeds])
        grads = (grads[:wide] + grads[wide:]).astype(BF16)
        grads = jnp.where(hidden_ref[view] > 0, grads, jnp.zeros_like(grads))
        grads = nn(one_ref[...], grads).astype(BF16).astype(F32)
        grads = nt(split(grads / degree), edges_ref[view])
        feature_grads = grads if feature_grads is None else feature_grads + grads
    width = feature_grads.shape[0] // 2
    feature_grads = split(feature_grads[:width] + feature_grads[width:])
    slot_grads = nt(slots_ref[...], feature_grads)
    grads_ref[...] = (slot_grads[:, :width] + slot_grads[:, width:]).astype(BF16)


def slabs_kernel(flat_ref, out_ref):
    slabs, slots = out_ref.shape
    for slab in range(slabs):
        out_ref[slab : slab + 1, :] = flat_ref[:, slab * slots : (slab + 1) * slots]


def fetch_kernel(
    asked_ref, table_far, out_ref, table_ref, wide_ref, rows_ref, index_ref, sem, table_sem
):
    slabs, slots = index_ref.shape
    copy = pltpu.make_async_copy(asked_ref, index_ref, sem)
    copy.start()
    table_copies = slot_parts(table_far, table_ref, table_sem)
    for table_copy in table_copies:
        table_copy.start()
    part = table_ref.shape[0] // len(table_copies)
    for place, table_copy in enumerate(table_copies):
        table_copy.wait()
        span = slice(place * part, (place + 1) * part)
        wide_ref[span, :] = table_ref[span, :].astype(F32)
    copy.wait()

    def step(slab, carry):
        start = pl.multiple_of(slab * slots, slots)
        for slot in range(slots):
            row = jnp.maximum(index_ref[slab, slot], 0)
            rows_ref[pl.ds(start + slot, 1), :] = wide_ref[pl.ds(row, 1), :]
        return carry

    lax.fori_loop(0, slabs, step, 0)
    out_ref[...] = rows_ref[...].astype(BF16).reshape(out_ref.shape)


def scatter_kernel(*refs, spans, first):
    out_ref = refs[-1]
    parts = 4
    rows = out_ref.shape[0] // parts
    picks, pieces = [], []
    for place, span in enumerate(spans):
        row_ref, lane_ref, grads_ref = refs[3 * place : 3 * place + 3]
        low = row_ref[:, span] & (rows - 1)
        hit = low == lax.broadcasted_iota(jnp.int32, (rows, low.shape[1]), 0)
        pick = jnp.where(hit, 1.0, 0.0).astype(BF16)
        grads = grads_ref[...]
        part_of = lane_ref[span, :]
        zero = jnp.zeros_like(grads)
        chosen = [jnp.where(part_of == part, grads, zero) for part in range(parts)]
        picks.append(pick)
        pieces.append(jnp.concatenate(chosen, axis=1))
    added = sum(nn(pick, chosen) for pick, chosen in zip(picks, pieces))
    width = out_ref.shape[1]
    for part in range(parts):
        span = slice(part * rows, (part + 1) * rows)
        value = added[:, part * width : (part + 1) * width]
        out_ref[span, :] = value if first else value + refs[-2][span, :]


def body(
    embedding_table,
    request_rows,
    node_slots,
    neighbours,
    kept_edges,
    weight_one,
    weight_two,
    proj_first,
    proj_second,
):
    table_count = lax.axis_size("table")
    batch_count = lax.axis_size("batch")
    shard_rows, width = embedding_table.shape
    nodes = neighbours.shape[0]
    seeds = SEED_DEV
    slot_count = request_rows.size
    (requests,) = call(
        slabs_kernel,
        [jax.ShapeDtypeStruct((table_count, slot_count // table_count), jnp.int32)],
        [request_rows],
        flops=1000,
        moved=50_000,
        mib=2,
    )

    def turn(value, by):
        return lax.ppermute(
            value, "batch", [(source, (source + by) % batch_count) for source in range(batch_count)]
        )

    received = lax.all_to_all(requests, "table", split_axis=0, concat_axis=0, tiled=True)
    (fetched,) = call(
        fetch_kernel,
        [jax.ShapeDtypeStruct(requests.shape + (width,), BF16)],
        [received, embedding_table],
        flops=1_000_000,
        moved=6_000_000,
        mib=60,
        scratch=[
            pltpu.VMEM((shard_rows, width), BF16),
            pltpu.VMEM((shard_rows, width), F32),
            pltpu.VMEM((slot_count, width), F32),
            pltpu.SMEM(requests.shape, jnp.int32),
            pltpu.SemaphoreType.DMA,
            pltpu.SemaphoreType.DMA((8,)),
        ],
        far=(1,),
    )
    arrived = lax.all_to_all(fetched, "table", split_axis=0, concat_axis=0, tiled=True)

    (slots,) = call(
        slots_kernel,
        [jax.ShapeDtypeStruct((slot_count, nodes), BF16)],
        [node_slots.T],
        flops=10_000_000,
        moved=2 * nodes * slot_count,
        mib=60,
        scratch=[
            pltpu.VMEM((slot_count, nodes), BF16),
            pltpu.SemaphoreType.DMA((nodes // LANES,)),
        ],
        far_outs=(0,),
    )
    kept = kept_edges.transpose(0, 2, 1).astype(F32)
    degree = 1.0 + jnp.sum(kept, axis=1)
    fetched, received, near, kept = lax.optimization_barrier(
        (fetched, received, neighbours.T, kept)
    )
    (edges,) = call(
        edges_kernel,
        [jax.ShapeDtypeStruct((2, nodes, nodes), BF16)],
        [near, kept],
        flops=60_000_000,
        moved=4 * nodes * nodes,
        mib=60,
        scratch=[
            pltpu.VMEM((2, nodes, nodes), BF16),
            pltpu.SemaphoreType.DMA((nodes // LANES,)),
        ],
        far_outs=(0,),
    )
    out_rows = shard_rows // batch_count
    part_rows = out_rows // 4
    offset = lax.axis_index("batch") * out_rows
    owned = []
    for by in range(batch_count):
        index = (received if by == 0 else turn(received, by)).reshape(-1) - offset
        part_of = jnp.where(index < 0, -1, index // part_rows).astype(BF16)
        owned.append((index[None, :], part_of))
    arrived, owned, edges, slots, degree = lax.optimization_barrier(
        (arrived, owned, edges, slots, degree)
    )
    rows = arrived.reshape(slot_count, width)

    wide = weight_one.shape[1]
    keys, raw, hidden, inner, slope = call(
        forward_kernel,
        [
            jax.ShapeDtypeStruct((wide, 2 * seeds), BF16),
            jax.ShapeDtypeStruct((wide, 2 * seeds), F32),
            jax.ShapeDtypeStruct((2, wide, nodes), BF16),
            jax.ShapeDtypeStruct((wide, 2 * seeds), BF16),
            jax.ShapeDtypeStruct((wide, 2 * seeds), F32),
        ],
        [rows, slots, edges, degree, weight_one, weight_two, proj_first, proj_second],
        flops=2_400_000_000,
        moved=10_000_000,
        mib=24,
    )
    ahead, far, behind = [turn(keys, by) for by in (1, 2, 3)]
    keys, owned = lax.optimization_barrier((keys, owned))
    lanes = [jnp.broadcast_to(part_of[:, None], (slot_count, width)) for _, part_of in owned]
    ahead, behind, lanes = lax.optimization_barrier((ahead, behind, lanes))
    owned = [(index, lane) for (index, _), lane in zip(owned, lanes)]
    expo, total0, totals = call(
        early_kernel,
        [
            jax.ShapeDtypeStruct((6 * seeds, 2 * seeds), F32),
            jax.ShapeDtypeStruct((1, 2 * seeds), F32),
            jax.ShapeDtypeStruct((4 * seeds, 1), F32),
        ],
        [keys, ahead, behind],
        flops=800_000_000,
        moved=4_000_000,
        mib=16,
    )
    (grads,) = call(
        backward_kernel,
        [jax.ShapeDtypeStruct((slot_count, width), BF16)],
        [
            keys, ahead, behind, far, expo, total0, totals, raw, hidden, inner, slope,
            slots, edges, degree, weight_one, weight_two, proj_first, proj_second,
        ],
        flops=8_000_000_000,
        moved=12_000_000,
        mib=32,
    )
    returned = lax.all_to_all(
        grads.reshape(table_count, -1, width), "table", split_axis=0, concat_axis=0, tiled=True
    ).reshape(slot_count, width)

    half = slot_count // 2
    upper, lower = slice(0, half), slice(half, slot_count)
    from_left = [turn(returned[upper], 1)]
    from_right = [turn(returned[lower], 3)]
    from_left.append(turn(returned[lower], 1))
    from_right.append(turn(returned[upper], 3))
    from_far = [turn(from_left[0], 1), turn(from_right[0], 3)]
    rounds = (
        ((0, slice(0, slot_count), returned),),
        ((1, upper, from_left[0]), (3, lower, from_right[0])),
        ((1, lower, from_left[1]), (3, upper, from_right[1])),
        ((2, upper, from_far[0]), (2, lower, from_far[1])),
    )
    total = None
    for pieces in rounds:
        args = []
        for source, span, piece in pieces:
            args += [*owned[source], piece]
        args += [] if total is None else [total]
        (total,) = call(
            functools.partial(
                scatter_kernel, spans=[span for _, span, _ in pieces], first=total is None
            ),
            [jax.ShapeDtypeStruct((out_rows, width), F32)],
            args,
            flops=1_000_000_000,
            moved=4_000_000,
            mib=16,
        )
    return total


def solution(mesh):
    in_specs = (
        P("table", None),
        P(("table", "batch"), None),
        P(("table", "batch"), None),
        P(("table", "batch"), None),
        P(None, ("table", "batch"), None),
        P(),
        P(),
        P(),
        P(),
    )
    out_specs = P(("table", "batch"), None)
    return jax.shard_map(body, mesh=mesh, in_specs=in_specs, out_specs=out_specs, check_vma=False)
```

time: 162 us -> 138 us (0.85)
  blocking collectives: 0 us -> 27.3 us
  waiting for transfers between devices: 50.4 us -> 27.1 us
  local copies, waits for them, and re-layouts: 22.8 us -> 7.69 us
  Pallas kernels: 47 us -> 35.6 us
  starting transfers between devices: 37.7 us -> 35.8 us
    all_to_all x0 -> x1, blocking collectives: none -> 27.3 us  [body(): lax.all_to_all(grads.reshape(table_count, -1, width), 'table', split_axis...]
    all_to_all x1 -> x0, waiting for transfers between devices: 16.7 us -> none  [body(): lax.all_to_all(grads.reshape(table_count, -1, width), 'table', split_axis...]
    pallas_call x8 -> x11, Pallas kernels: 47 us -> 35.6 us  [call(): pl.pallas_call(kernel, out_shape=outs, in_specs=[HBM if place in far else...]
    gather x1 -> x0, local copies, waits for them, and re-layouts: 8.05 us -> none  [body(): fetched = embedding_table[jnp.maximum(received, 0)]]
    all_to_all x1 -> x0, starting transfers between devices: 7.95 us -> none  [body(): lax.all_to_all(grads.reshape(table_count, -1, width), 'table', split_axis...]
    all_to_all x1, waiting for transfers between devices: 9.3 us -> 2.6 us  [body(): lax.all_to_all(requests, 'table', split_axis=0, concat_axis=0, tiled=True)]
    unnamed x37 -> x20, local copies, waits for them, and re-layouts: 12.1 us -> 5.7 us
    ppermute x9 -> x12, starting transfers between devices: 11.9 us -> 14.9 us  [turn(): lax.ppermute(value, 'batch', [(source, (source + by) % batch_count) for s...]
  transfers between devices with their start and end apart: 12 -> 14, of which waited for: 7 -> 6; matrix products, arithmetic and copies ran while one was open for 2% -> 4% of each run, Pallas kernels for 22% -> 12%
where the time goes in v1:
time: 138 us; the launch traced here: 137 us
  starting transfers between devices  35.8 us (26%)
  Pallas kernels  35.6 us (26%)
  blocking collectives  27.3 us (20%)
  waiting for transfers between devices  27.1 us (20%)
  local copies, waits for them, and re-layouts  7.69 us (6%)
  other arithmetic  3.2 us (2%)
    pallas_call x11, Pallas kernels, call(): pl.pallas_call(kernel, out_shape=outs, in_specs=[HBM if place in far else...  35.6 us
    all_to_all x1, blocking collectives, body(): lax.all_to_all(grads.reshape(table_count, -1, width), 'table', split_axis...  27.3 us
    ppermute x12, waiting for transfers between devices, turn(): lax.ppermute(value, 'batch', [(source, (source + by) % batch_count) for s...  18.4 us
    ppermute x12, starting transfers between devices, turn(): lax.ppermute(value, 'batch', [(source, (source + by) % batch_count) for s...  14.9 us
    all_to_all x1, starting transfers between devices, body(): lax.all_to_all(requests, 'table', split_axis=0, concat_axis=0, tiled=True)  13.2 us
    all_to_all x1, starting transfers between devices, body(): lax.all_to_all(fetched, 'table', split_axis=0, concat_axis=0, tiled=True)  7.71 us
    all_to_all x1, waiting for transfers between devices, body(): lax.all_to_all(fetched, 'table', split_axis=0, concat_axis=0, tiled=True)  6.11 us
    unnamed x20, local copies, waits for them, and re-layouts  5.7 us
  transfers between devices with their start and end apart: 14, of which 6 were waited for; matrix products, arithmetic and copies ran while one was open for 4% of the time, Pallas kernels for 12%

profile of v1, /device:TPU:1, one launch (start us, length us, event | category | flops | bytes accessed | tf_op | source)
XLA Modules:
  0.0 136.9 jit_solution(10682320202056008858)
XLA Ops:
  0.0 0.7 copy-done.8
  0.7 0.7 shard_map.91
  1.4 13.2 %all-to-all-start = ((s32[64,1,32]{2,1,0:T(1,128)}), s32[64,1,32]{2,1,0:T(1,128)S(1)}, u32[]{:S(2)}, u32[]{:S(2)}) async-start(s32[64,1,32]{2,1,0:T(1,128)} %bitcast.1), calls=%async_computation | async-start | bytes 65536 | tf_op jit(solution)/shard_map/all_to_all | solution.py:359
  14.6 0.9 fusion.16
  15.5 1.5 %convert_bitcast_fusion.kept_ref = f32[2,8,1024]{2,1,0:T(8,128)} fusion(s32[2,1024,8]{1,2,0:T(8,128)} %param.13), kind=kLoop, calls=%fused_computation | loop fusion | flops 16384 | bytes 131072 | tf_op jit(solution)/shard_map/convert_element_type | solution.py:392
  16.9 4.3 %shard_map.94.slots_ref = bf16[2048,1024]{1,0:T(8,128)(2,1)} custom-call(s32[2,1024]{1,0:T(2,128)} %bitcast.28), custom_call_target="tpu_custom_call" | custom-call | flops 10000000 | bytes 4194304 | tf_op jit(solution)/shard_map/pallas_call | solution.py:38
  21.3 2.6 %all-to-all-done = s32[64,1,32]{2,1,0:T(1,128)S(1)} async-done(((s32[64,1,32]{2,1,0:T(1,128)}), s32[64,1,32]{2,1,0:T(1,128)S(1)}, u32[]{:S(2)}, u32[]{:S(2)}) %all-to-all-start) | async-done | bytes 8224 | tf_op jit(solution)/shard_map/all_to_all | solution.py:359
  23.9 0.6 copy-done.9
  24.5 6.4 %shard_map.92 = bf16[64,32,128]{2,1,0:T(8,128)(2,1)} custom-call(s32[64,32]{1,0:T(8,128)} %bitcast.18, bf16[8192,128]{1,0:T(8,128)(2,1)} %table_far.1), custom_call_target="tpu_custom_call" | custom-call | flops 1000000 | bytes 6000000 | tf_op jit(solution)/shard_map/pallas_call | solution.py:38
  30.9 7.7 %all-to-all-start.1 = ((bf16[64,32,128]{2,1,0:T(8,128)(2,1)}), bf16[64,32,128]{2,1,0:T(8,128)(2,1)S(1)}, u32[]{:S(2)}, u32[]{:S(2)}) async-start(bf16[64,32,128]{2,1,0:T(8,128)(2,1)} %shard_map.92), calls=%async_computation.1 | async-start | bytes 1048576 | tf_op jit(solution)/shard_map/all_to_all | solution.py:377
  38.6 2.6 %collective-permute-start.2 = (s32[64,32]{1,0:T(8,128)}, s32[64,32]{1,0:T(8,128)S(1)}, u32[]{:S(2)}, u32[]{:S(2)}) collective-permute-start(s32[64,32]{1,0:T(8,128)} %bitcast.19), channel_id=1, source_target_pairs={{0,3},{1,0},{2,1},{3,2},{4,7},{5,4},{6,5},{7,6},{8,11},{9,8},{10,9... | collective-permute-start | bytes 24584 | tf_op jit(solution)/shard_map/ppermute | solution.py:355
  41.2 0.8 broadcast_subtract_fusion.3
  43.4 6.3 %shard_map.93.edges_ref = bf16[2,1024,1024]{2,1,0:T(8,128)(2,1)} custom-call(s32[8,1024]{1,0:T(8,128)} %bitcast.27, f32[2,8,1024]{2,1,0:T(8,128)} %convert_bitcast_fusion.kept_ref), custom_call_target="tpu_custom_call" | custom-call | flops 60000000 | bytes 4194304 | tf_op jit(solution)/shard_map/pallas_call | solution.py:38
  50.2 6.1 %all-to-all-done.1 = bf16[64,32,128]{2,1,0:T(8,128)(2,1)S(1)} async-done(((bf16[64,32,128]{2,1,0:T(8,128)(2,1)}), bf16[64,32,128]{2,1,0:T(8,128)(2,1)S(1)}, u32[]{:S(2)}, u32[]{:S(2)}) %all-to-all-start.1) | async-done | bytes 524320 | tf_op jit(solution)/shard_map/all_to_all | solution.py:377
  56.4 2.2 %copy-done = bf16[2048,1024]{1,0:T(8,128)(2,1)S(1)} copy-done((bf16[2048,1024]{1,0:T(8,128)(2,1)S(1)}, bf16[2048,1024]{1,0:T(8,128)(2,1)}, u32[]{:S(2)}) %copy-start) | copy-done | bytes 4194328
  58.6 2.2 %copy-done.2 = bf16[2,1024,1024]{2,1,0:T(8,128)(2,1)S(1)} copy-done((bf16[2,1024,1024]{2,1,0:T(8,128)(2,1)S(1)}, bf16[2,1024,1024]{2,1,0:T(8,128)(2,1)}, u32[]{:S(2)}) %copy-start.2) | copy-done | bytes 4194328
  60.7 4.1 %shard_map.95 = (bf16[256,512]{1,0:T(8,128)(2,1)S(1)}, f32[256,512]{1,0:T(8,128)S(1)}, bf16[2,256,1024]{2,1,0:T(8,128)(2,1)S(1)}, bf16[256,512]{1,0:T(8,128)(2,1)S(1)}, f32[256,512]{1,0:T(8,128)S(1)}) custom-call(bf16[2048,128]{1,0:T(8,128)(2,1)S(1)} %bitcast.16, bf16[2048,1024]{1,0:T(8,128)(2,1)S(1)} %copy-done, bf16[2,1024,1024]{2,1,0:T(8,128)(2,1)S(1)} %copy-done.2, ...), custom_call_target="tpu_custom_call" | custom-call | flops 2400000000 | bytes 10000000 | tf_op jit(solution)/shard_map/pallas_call | solution.py:38
  64.8 2.6 %collective-permute-start.4 = (bf16[256,512]{1,0:T(8,128)(2,1)S(1)}, bf16[256,512]{1,0:T(8,128)(2,1)S(1)}, u32[]{:S(2)}, u32[]{:S(2)}) collective-permute-start(bf16[256,512]{1,0:T(8,128)(2,1)S(1)} %get-tuple-element.65.key0_ref), channel_id=1, source_target_pairs={{0,3},{1,0},{2,1},{3,2},{4,7},{5,4},{6,5},{7,6},{8,11},{9,8},{10,9... | collective-permute-start | bytes 786440 | tf_op jit(solution)/shard_map/ppermute | solution.py:355
  67.4 1.7 %collective-permute-start.5 = (bf16[256,512]{1,0:T(8,128)(2,1)S(1)}, bf16[256,512]{1,0:T(8,128)(2,1)S(1)}, u32[]{:S(2)}, u32[]{:S(2)}) collective-permute-start(bf16[256,512]{1,0:T(8,128)(2,1)S(1)} %get-tuple-element.65.key0_ref), channel_id=1, source_target_pairs={{0,2},{1,3},{2,0},{3,1},{4,6},{5,7},{6,4},{7,5},{8,10},{9,11},{10,... | collective-permute-start | bytes 786440 | tf_op jit(solution)/shard_map/ppermute | solution.py:355
  69.1 9.0 %collective-permute-done.4.key3_ref = bf16[256,512]{1,0:T(8,128)(2,1)S(1)} collective-permute-done((bf16[256,512]{1,0:T(8,128)(2,1)S(1)}, bf16[256,512]{1,0:T(8,128)(2,1)S(1)}, u32[]{:S(2)}, u32[]{:S(2)}) %collective-permute-start.4) | collective-permute-done | bytes 262176 | tf_op jit(solution)/shard_map/ppermute | solution.py:355
  79.5 1.4 %shard_map.96 = (f32[1536,512]{1,0:T(8,128)S(1)}, f32[1,512]{1,0:T(1,128)S(1)}, f32[1024,1]{1,0:T(8,128)S(1)}) custom-call(bf16[256,512]{1,0:T(8,128)(2,1)S(1)} %get-tuple-element.65.key0_ref, bf16[256,512]{1,0:T(8,128)(2,1)S(1)} %collective-permute-done.3.key1_ref, bf16[256,512]{1,0:T(8,128)(2,1)S(1)} %collective-permute-done.4.key3_ref), custom_call_target="tpu_custom_call" | custom-call | flops 800000000 | bytes 4000000 | tf_op jit(solution)/shard_map/pallas_call | solution.py:38
  81.0 6.4 %shard_map.97 = bf16[2048,128]{1,0:T(8,128)(2,1)S(1)} custom-call(bf16[256,512]{1,0:T(8,128)(2,1)S(1)} %get-tuple-element.65.key0_ref, bf16[256,512]{1,0:T(8,128)(2,1)S(1)} %collective-permute-done.3.key1_ref, bf16[256,512]{1,0:T(8,128)(2,1)S(1)} %collective-permute-done.4.key3_ref, bf16[256,512]{1,0:T(8,128)(2,1)S(1)} %collective-permute-done.5.key2_ref, ...), custom_call_target="tpu_custom_call" | custom-call | flops 8000000000 | bytes 12000000 | tf_op jit(solution)/shard_map/pallas_call | solution.py:38
  87.4 27.3 %all_to_all.21 = bf16[64,32,128]{2,1,0:T(8,128)(2,1)S(1)} all-to-all(bf16[64,32,128]{2,1,0:T(8,128)(2,1)S(1)} %bitcast.17), channel_id=1, replica_groups=mesh['table'=64,'batch'=4] {'table'}, dimensions={0} | all-to-all | bytes 1048576 | tf_op jit(solution)/shard_map/all_to_all | solution.py:466
  114.7 2.7 %collective-permute-start.8 = (bf16[1024,128]{1,0:T(8,128)(2,1)S(1)}, bf16[1024,128]{1,0:T(8,128)(2,1)S(1)}, u32[]{:S(2)}, u32[]{:S(2)}) collective-permute-start(bf16[1024,128]{1,0:T(8,128)(2,1)S(1)} %bitcast.23), channel_id=1, source_target_pairs={{0,3},{1,0},{2,1},{3,2},{4,7},{5,4},{6,5},{7,6},{8,11},{9,8},{10,9... | collective-permute-start | bytes 786440 | tf_op jit(solution)/shard_map/ppermute | solution.py:355
  117.4 1.4 %collective-permute-start.10 = (bf16[1024,128]{1,0:T(8,128)(2,1)S(1)}, bf16[1024,128]{1,0:T(8,128)(2,1)S(1)}, u32[]{:S(2)}, u32[]{:S(2)}) collective-permute-start(bf16[1024,128]{1,0:T(8,128)(2,1)S(1)} %bitcast.24), channel_id=1, source_target_pairs={{0,1},{1,2},{2,3},{3,0},{4,5},{5,6},{6,7},{7,4},{8,9},{9,10},{10,1... | collective-permute-start | bytes 786440 | tf_op jit(solution)/shard_map/ppermute | solution.py:355
  118.9 4.6 %collective-permute-done.6.refs_2_ = bf16[1024,128]{1,0:T(8,128)(2,1)S(1)} collective-permute-done((bf16[1024,128]{1,0:T(8,128)(2,1)S(1)}, bf16[1024,128]{1,0:T(8,128)(2,1)S(1)}, u32[]{:S(2)}, u32[]{:S(2)}) %collective-permute-start.6) | collective-permute-done | bytes 262176 | tf_op jit(solution)/shard_map/ppermute | solution.py:355
  123.4 2.7 %collective-permute-start.9 = (bf16[1024,128]{1,0:T(8,128)(2,1)S(1)}, bf16[1024,128]{1,0:T(8,128)(2,1)S(1)}, u32[]{:S(2)}, u32[]{:S(2)}) collective-permute-start(bf16[1024,128]{1,0:T(8,128)(2,1)S(1)} %collective-permute-done.8.refs_5_), channel_id=1, source_target_pairs={{0,3},{1,0},{2,1},{3,2},{4,7},{5,4},{6,5},{7,6},{8,11},{9,8},{10,9... | collective-permute-start | bytes 786440 | tf_op jit(solution)/shard_map/ppermute | solution.py:355
  126.1 1.3 shard_map.98.refs_6_
  127.4 1.3 shard_map.99.refs_6_
  129.1 1.3 shard_map.100.refs_6_
  130.3 4.3 %collective-permute-done.7.refs_2_ = bf16[1024,128]{1,0:T(8,128)(2,1)S(1)} collective-permute-done((bf16[1024,128]{1,0:T(8,128)(2,1)S(1)}, bf16[1024,128]{1,0:T(8,128)(2,1)S(1)}, u32[]{:S(2)}, u32[]{:S(2)}) %collective-permute-start.7) | collective-permute-done | bytes 262176 | tf_op jit(solution)/shard_map/ppermute | solution.py:355
  134.7 2.2 %shard_map.101 = f32[2048,128]{1,0:T(8,128)} custom-call(s32[1,2048]{1,0:T(1,128)S(1)} %sub.98.refs_0_.refs_3_, bf16[2048,128]{1,0:T(8,128)(2,1)S(1)} %broadcast_in_dim.18.refs_1_.refs_4_, bf16[1024,128]{1,0:T(8,128)(2,1)S(1)} %collective-permute-done.7.refs_2_, s32[1,2048]{1,0:T(1,128)S(1)} %sub.98.refs_0_.refs_3_, ...), custom_call_target="tpu_custom_call" | custom-call | flops 1000000000 | bytes 4000000 | tf_op jit(solution)/shard_map/pallas_call | solution.py:38
  (52 shorter events, 3.8 us)
Async XLA Ops:
  0.0 0.7 copy-start.8
  1.4 22.5 %all-to-all-start = ((s32[64,1,32]{2,1,0:T(1,128)}), s32[64,1,32]{2,1,0:T(1,128)S(1)}, u32[]{:S(2)}, u32[]{:S(2)}) async-start(s32[64,1,32]{2,1,0:T(1,128)} %bitcast.1), calls=%async_computation | async-start | bytes 65536 | tf_op jit(solution)/shard_map/all_to_all | solution.py:359
  23.9 0.6 copy-start.9
  24.5 31.8 %copy-start.4 = (bf16[256,256]{1,0:T(8,128)(2,1)S(1)}, bf16[256,256]{1,0:T(8,128)(2,1)}, u32[]{:S(2)}) copy-start(bf16[256,256]{1,0:T(8,128)(2,1)} %two_ref.3) | copy-start | bytes 393220
  24.5 31.8 %copy-start.5 = (bf16[256,256]{1,0:T(8,128)(2,1)S(1)}, bf16[256,256]{1,0:T(8,128)(2,1)}, u32[]{:S(2)}) copy-start(bf16[256,256]{1,0:T(8,128)(2,1)} %first_ref.3) | copy-start | bytes 393220
  24.5 31.8 %copy-start.6 = (bf16[256,256]{1,0:T(8,128)(2,1)S(1)}, bf16[256,256]{1,0:T(8,128)(2,1)}, u32[]{:S(2)}) copy-start(bf16[256,256]{1,0:T(8,128)(2,1)} %second_ref.3) | copy-start | bytes 393220
  24.5 31.8 %copy-start.7 = (bf16[128,256]{1,0:T(8,128)(2,1)S(1)}, bf16[128,256]{1,0:T(8,128)(2,1)}, u32[]{:S(2)}) copy-start(bf16[128,256]{1,0:T(8,128)(2,1)} %one_ref.3) | copy-start | bytes 196612
  30.9 25.4 %all-to-all-start.1 = ((bf16[64,32,128]{2,1,0:T(8,128)(2,1)}), bf16[64,32,128]{2,1,0:T(8,128)(2,1)S(1)}, u32[]{:S(2)}, u32[]{:S(2)}) async-start(bf16[64,32,128]{2,1,0:T(8,128)(2,1)} %shard_map.92), calls=%async_computation.1 | async-start | bytes 1048576 | tf_op jit(solution)/shard_map/all_to_all | solution.py:377
  38.6 11.0 %collective-permute-start.2 = (s32[64,32]{1,0:T(8,128)}, s32[64,32]{1,0:T(8,128)S(1)}, u32[]{:S(2)}, u32[]{:S(2)}) collective-permute-start(s32[64,32]{1,0:T(8,128)} %bitcast.19), channel_id=1, source_target_pairs={{0,3},{1,0},{2,1},{3,2},{4,7},{5,4},{6,5},{7,6},{8,11},{9,8},{10,9... | collective-permute-start | bytes 24584 | tf_op jit(solution)/shard_map/ppermute | solution.py:355
  42.2 7.5 %collective-permute-start.1 = (s32[64,32]{1,0:T(8,128)}, s32[64,32]{1,0:T(8,128)S(1)}, u32[]{:S(2)}, u32[]{:S(2)}) collective-permute-start(s32[64,32]{1,0:T(8,128)} %bitcast.21), channel_id=1, source_target_pairs={{0,2},{1,3},{2,0},{3,1},{4,6},{5,7},{6,4},{7,5},{8,10},{9,11},{10,... | collective-permute-start | bytes 24584 | tf_op jit(solution)/shard_map/ppermute | solution.py:355
  42.8 7.2 %collective-permute-start = (s32[64,32]{1,0:T(8,128)}, s32[64,32]{1,0:T(8,128)S(1)}, u32[]{:S(2)}, u32[]{:S(2)}) collective-permute-start(s32[64,32]{1,0:T(8,128)} %bitcast.22), channel_id=1, source_target_pairs={{0,1},{1,2},{2,3},{3,0},{4,5},{5,6},{6,7},{7,4},{8,9},{9,10},{10,1... | collective-permute-start | bytes 24584 | tf_op jit(solution)/shard_map/ppermute | solution.py:355
  56.4 2.2 %copy-start = (bf16[2048,1024]{1,0:T(8,128)(2,1)S(1)}, bf16[2048,1024]{1,0:T(8,128)(2,1)}, u32[]{:S(2)}) copy-start(bf16[2048,1024]{1,0:T(8,128)(2,1)} %shard_map.94.slots_ref) | copy-start | bytes 12582916
  58.6 2.2 %copy-start.2 = (bf16[2,1024,1024]{2,1,0:T(8,128)(2,1)S(1)}, bf16[2,1024,1024]{2,1,0:T(8,128)(2,1)}, u32[]{:S(2)}) copy-start(bf16[2,1024,1024]{2,1,0:T(8,128)(2,1)} %shard_map.93.edges_ref) | copy-start | bytes 12582916
  60.7 20.2 %copy-start.3 = (bf16[2,1024,1024]{2,1,0:T(8,128)(2,1)S(1)}, bf16[2,1024,1024]{2,1,0:T(8,128)(2,1)}, u32[]{:S(2)}) copy-start(bf16[2,1024,1024]{2,1,0:T(8,128)(2,1)} %shard_map.93.edges_ref) | copy-start | bytes 12582916
  64.8 16.2 %copy-start.1 = (bf16[2048,1024]{1,0:T(8,128)(2,1)S(1)}, bf16[2048,1024]{1,0:T(8,128)(2,1)}, u32[]{:S(2)}) copy-start(bf16[2048,1024]{1,0:T(8,128)(2,1)} %shard_map.94.slots_ref) | copy-start | bytes 12582916
  64.8 13.3 %collective-permute-start.4 = (bf16[256,512]{1,0:T(8,128)(2,1)S(1)}, bf16[256,512]{1,0:T(8,128)(2,1)S(1)}, u32[]{:S(2)}, u32[]{:S(2)}) collective-permute-start(bf16[256,512]{1,0:T(8,128)(2,1)S(1)} %get-tuple-element.65.key0_ref), channel_id=1, source_target_pairs={{0,3},{1,0},{2,1},{3,2},{4,7},{5,4},{6,5},{7,6},{8,11},{9,8},{10,9... | collective-permute-start | bytes 786440 | tf_op jit(solution)/shard_map/ppermute | solution.py:355
  67.4 10.8 %collective-permute-start.3 = (bf16[256,512]{1,0:T(8,128)(2,1)S(1)}, bf16[256,512]{1,0:T(8,128)(2,1)S(1)}, u32[]{:S(2)}, u32[]{:S(2)}) collective-permute-start(bf16[256,512]{1,0:T(8,128)(2,1)S(1)} %get-tuple-element.65.key0_ref), channel_id=1, source_target_pairs={{0,1},{1,2},{2,3},{3,0},{4,5},{5,6},{6,7},{7,4},{8,9},{9,10},{10,1... | collective-permute-start | bytes 786440 | tf_op jit(solution)/shard_map/ppermute | solution.py:355
  67.4 13.6 %collective-permute-start.5 = (bf16[256,512]{1,0:T(8,128)(2,1)S(1)}, bf16[256,512]{1,0:T(8,128)(2,1)S(1)}, u32[]{:S(2)}, u32[]{:S(2)}) collective-permute-start(bf16[256,512]{1,0:T(8,128)(2,1)S(1)} %get-tuple-element.65.key0_ref), channel_id=1, source_target_pairs={{0,2},{1,3},{2,0},{3,1},{4,6},{5,7},{6,4},{7,5},{8,10},{9,11},{10,... | collective-permute-start | bytes 786440 | tf_op jit(solution)/shard_map/ppermute | solution.py:355
  114.7 8.8 %collective-permute-start.6 = (bf16[1024,128]{1,0:T(8,128)(2,1)S(1)}, bf16[1024,128]{1,0:T(8,128)(2,1)S(1)}, u32[]{:S(2)}, u32[]{:S(2)}) collective-permute-start(bf16[1024,128]{1,0:T(8,128)(2,1)S(1)} %bitcast.25), channel_id=1, source_target_pairs={{0,1},{1,2},{2,3},{3,0},{4,5},{5,6},{6,7},{7,4},{8,9},{9,10},{10,1... | collective-permute-start | bytes 786440 | tf_op jit(solution)/shard_map/ppermute | solution.py:355
  114.7 8.7 %collective-permute-start.8 = (bf16[1024,128]{1,0:T(8,128)(2,1)S(1)}, bf16[1024,128]{1,0:T(8,128)(2,1)S(1)}, u32[]{:S(2)}, u32[]{:S(2)}) collective-permute-start(bf16[1024,128]{1,0:T(8,128)(2,1)S(1)} %bitcast.23), channel_id=1, source_target_pairs={{0,3},{1,0},{2,1},{3,2},{4,7},{5,4},{6,5},{7,6},{8,11},{9,8},{10,9... | collective-permute-start | bytes 786440 | tf_op jit(solution)/shard_map/ppermute | solution.py:355
  117.4 11.2 %collective-permute-start.11 = (bf16[1024,128]{1,0:T(8,128)(2,1)S(1)}, bf16[1024,128]{1,0:T(8,128)(2,1)S(1)}, u32[]{:S(2)}, u32[]{:S(2)}) collective-permute-start(bf16[1024,128]{1,0:T(8,128)(2,1)S(1)} %bitcast.26), channel_id=1, source_target_pairs={{0,3},{1,0},{2,1},{3,2},{4,7},{5,4},{6,5},{7,6},{8,11},{9,8},{10,9... | collective-permute-start | bytes 786440 | tf_op jit(solution)/shard_map/ppermute | solution.py:355
  117.4 11.6 %collective-permute-start.10 = (bf16[1024,128]{1,0:T(8,128)(2,1)S(1)}, bf16[1024,128]{1,0:T(8,128)(2,1)S(1)}, u32[]{:S(2)}, u32[]{:S(2)}) collective-permute-start(bf16[1024,128]{1,0:T(8,128)(2,1)S(1)} %bitcast.24), channel_id=1, source_target_pairs={{0,1},{1,2},{2,3},{3,0},{4,5},{5,6},{6,7},{7,4},{8,9},{9,10},{10,1... | collective-permute-start | bytes 786440 | tf_op jit(solution)/shard_map/ppermute | solution.py:355
  123.4 11.2 %collective-permute-start.7 = (bf16[1024,128]{1,0:T(8,128)(2,1)S(1)}, bf16[1024,128]{1,0:T(8,128)(2,1)S(1)}, u32[]{:S(2)}, u32[]{:S(2)}) collective-permute-start(bf16[1024,128]{1,0:T(8,128)(2,1)S(1)} %collective-permute-done.6.refs_2_), channel_id=1, source_target_pairs={{0,1},{1,2},{2,3},{3,0},{4,5},{5,6},{6,7},{7,4},{8,9},{9,10},{10,1... | collective-permute-start | bytes 786440 | tf_op jit(solution)/shard_map/ppermute | solution.py:355
  123.4 11.2 %collective-permute-start.9 = (bf16[1024,128]{1,0:T(8,128)(2,1)S(1)}, bf16[1024,128]{1,0:T(8,128)(2,1)S(1)}, u32[]{:S(2)}, u32[]{:S(2)}) collective-permute-start(bf16[1024,128]{1,0:T(8,128)(2,1)S(1)} %collective-permute-done.8.refs_5_), channel_id=1, source_target_pairs={{0,3},{1,0},{2,1},{3,2},{4,7},{5,4},{6,5},{7,6},{8,11},{9,8},{10,9... | collective-permute-start | bytes 786440 | tf_op jit(solution)/shard_map/ppermute | solution.py:355

commit v2 on v1

--- a/solution.py
+++ b/solution.py
@@ -12,6 +12,7 @@
 EPSILON = 1e-06
 F32 = jnp.float32
 BF16 = jnp.bfloat16
+F8 = jnp.float8_e4m3fn
 VMEM = pl.BlockSpec(memory_space=pltpu.VMEM)
 HBM = pl.BlockSpec(memory_space=pltpu.HBM)
 
@@ -48,7 +49,7 @@
     )(*args)
 
 
-TILE, LANES, ROWS = 16, 128, 64
+TILE, LANES, ROWS = 32, 128, 64
 
 
 def spread(row, kind):
@@ -83,7 +84,7 @@
                     for view in range(views):
                         totals[view] = totals[view] + jnp.where(hit, kept[view][slot], none)
                 for view in range(views):
-                    edges_ref[view, pl.ds(start, TILE), span] = totals[view]
+                    edges_ref[view, pl.ds(start, TILE), span] = totals[view].astype(F8)
             return carry
 
         lax.fori_loop(0, nodes // ROWS, step, 0)
@@ -110,7 +111,7 @@
                 total = jnp.where(named[0] == ids, one, none)
                 for which in range(1, hashes):
                     total = total + jnp.where(named[which] == ids, one, none)
-                slots_ref[pl.ds(start, TILE), span] = total
+                slots_ref[pl.ds(start, TILE), span] = total.astype(F8)
             return carry
 
         lax.fori_loop(0, slots_ref.shape[0] // ROWS, step, 0)
@@ -134,13 +135,16 @@
 
 def forward_kernel(
     rows_ref, slots_ref, edges_ref, degree_ref, one_ref, two_ref, first_ref, second_ref,
-    keys_ref, raw_ref, hidden_ref, inner_ref, slope_ref,
+    keys_ref, raw_ref, hidden_ref, inner_ref, slope_ref, wide_slots_ref, wide_edges_ref,
 ):
     seeds = SEED_DEV
     width = rows_ref.shape[1]
-    features = split(tn(rows_ref[...], slots_ref[...]))
+    slots = slots_ref[...].astype(BF16)
+    wide_slots_ref[...] = slots
+    features = split(tn(rows_ref[...], slots))
     for view in range(2):
-        edges = edges_ref[view]
+        edges = edges_ref[view].astype(BF16)
+        wide_edges_ref[view] = edges
         degree = degree_ref[view : view + 1, :]
         summed = nn(features, edges)
         layer_in = ((summed[:width] + summed[width:]) / degree).astype(BF16)
@@ -275,10 +279,10 @@
 
 
 def fetch_kernel(
-    asked_ref, table_far, out_ref, table_ref, wide_ref, rows_ref, index_ref, sem, table_sem
+    asked_far, table_far, out_ref, table_ref, wide_ref, rows_ref, index_ref, sem, table_sem
 ):
     slabs, slots = index_ref.shape
-    copy = pltpu.make_async_copy(asked_ref, index_ref, sem)
+    copy = pltpu.make_async_copy(asked_far, index_ref, sem)
     copy.start()
     table_copies = slot_parts(table_far, table_ref, table_sem)
     for table_copy in table_copies:
@@ -372,37 +376,37 @@
             pltpu.SemaphoreType.DMA,
             pltpu.SemaphoreType.DMA((8,)),
         ],
-        far=(1,),
+        far=(0, 1),
     )
     arrived = lax.all_to_all(fetched, "table", split_axis=0, concat_axis=0, tiled=True)
 
     (slots,) = call(
         slots_kernel,
-        [jax.ShapeDtypeStruct((slot_count, nodes), BF16)],
+        [jax.ShapeDtypeStruct((slot_count, nodes), F8)],
         [node_slots.T],
         flops=10_000_000,
         moved=2 * nodes * slot_count,
         mib=60,
         scratch=[
-            pltpu.VMEM((slot_count, nodes), BF16),
+            pltpu.VMEM((slot_count, nodes), F8),
             pltpu.SemaphoreType.DMA((nodes // LANES,)),
         ],
         far_outs=(0,),
     )
-    kept = kept_edges.transpose(0, 2, 1).astype(F32)
+    fetched, received, near, kept = lax.optimization_barrier(
+        (fetched, received, neighbours.T, kept_edges)
+    )
+    kept = kept.transpose(0, 2, 1).astype(F32)
     degree = 1.0 + jnp.sum(kept, axis=1)
-    fetched, received, near, kept = lax.optimization_barrier(
-        (fetched, received, neighbours.T, kept)
-    )
     (edges,) = call(
         edges_kernel,
-        [jax.ShapeDtypeStruct((2, nodes, nodes), BF16)],
+        [jax.ShapeDtypeStruct((2, nodes, nodes), F8)],
         [near, kept],
         flops=60_000_000,
         moved=4 * nodes * nodes,
         mib=60,
         scratch=[
-            pltpu.VMEM((2, nodes, nodes), BF16),
+            pltpu.VMEM((2, nodes, nodes), F8),
             pltpu.SemaphoreType.DMA((nodes // LANES,)),
         ],
         far_outs=(0,),
@@ -421,7 +425,7 @@
     rows = arrived.reshape(slot_count, width)
 
     wide = weight_one.shape[1]
-    keys, raw, hidden, inner, slope = call(
+    keys, raw, hidden, inner, slope, slots, edges = call(
         forward_kernel,
         [
             jax.ShapeDtypeStruct((wide, 2 * seeds), BF16),
@@ -429,11 +433,13 @@
             jax.ShapeDtypeStruct((2, wide, nodes), BF16),
             jax.ShapeDtypeStruct((wide, 2 * seeds), BF16),
             jax.ShapeDtypeStruct((wide, 2 * seeds), F32),
+            jax.ShapeDtypeStruct((slot_count, nodes), BF16),
+            jax.ShapeDtypeStruct((2, nodes, nodes), BF16),
         ],
         [rows, slots, edges, degree, weight_one, weight_two, proj_first, proj_second],
         flops=2_400_000_000,
         moved=10_000_000,
-        mib=24,
+        mib=32,
     )
     ahead, far, behind = [turn(keys, by) for by in (1, 2, 3)]
     keys, owned = lax.optimization_barrier((keys, owned))

time: 138 us -> 132 us (0.957)
  local copies, waits for them, and re-layouts: 7.69 us -> 4.89 us
  starting transfers between devices: 35.8 us -> 33.1 us
  waiting for transfers between devices: 27.1 us -> 29.2 us
  other arithmetic: 3.2 us -> 1.49 us
    unnamed x20 -> x18, local copies, waits for them, and re-layouts: 5.7 us -> 2.91 us
    all_to_all x1, starting transfers between devices: 7.71 us -> 5.03 us  [body(): lax.all_to_all(fetched, 'table', split_axis=0, concat_axis=0, tiled=True)]
    all_to_all x1, waiting for transfers between devices: 2.6 us -> 5.28 us  [body(): lax.all_to_all(requests, 'table', split_axis=0, concat_axis=0, tiled=True)]
  transfers between devices with their start and end apart: 14 -> 14, of which waited for: 6 -> 8; matrix products, arithmetic and copies ran while one was open for 4% -> 3% of each run, Pallas kernels for 12% -> 11%
where the time goes in v2:
time: 132 us; the launch traced here: 131 us
  Pallas kernels  34.4 us (26%)
  starting transfers between devices  33.1 us (25%)
  waiting for transfers between devices  29.2 us (22%)
  blocking collectives  27.7 us (21%)
  local copies, waits for them, and re-layouts  4.89 us (4%)
  other arithmetic  1.49 us (1%)
    pallas_call x11, Pallas kernels, call(): pl.pallas_call(kernel, out_shape=outs, in_specs=[HBM if place in far else...  34.4 us
    all_to_all x1, blocking collectives, body(): lax.all_to_all(grads.reshape(table_count, -1, width), 'table', split_axis...  27.7 us
    ppermute x12, waiting for transfers between devices, turn(): lax.ppermute(value, 'batch', [(source, (source + by) % batch_count) for s...  17.9 us
    ppermute x12, starting transfers between devices, turn(): lax.ppermute(value, 'batch', [(source, (source + by) % batch_count) for s...  14.9 us
    all_to_all x1, starting transfers between devices, body(): lax.all_to_all(requests, 'table', split_axis=0, concat_axis=0, tiled=True)  13.2 us
    all_to_all x1, waiting for transfers between devices, body(): lax.all_to_all(fetched, 'table', split_axis=0, concat_axis=0, tiled=True)  6.04 us
    all_to_all x1, waiting for transfers between devices, body(): lax.all_to_all(requests, 'table', split_axis=0, concat_axis=0, tiled=True)  5.28 us
    all_to_all x1, starting transfers between devices, body(): lax.all_to_all(fetched, 'table', split_axis=0, concat_axis=0, tiled=True)  5.03 us
  transfers between devices with their start and end apart: 14, of which 8 were waited for; matrix products, arithmetic and copies ran while one was open for 3% of the time, Pallas kernels for 11%

profile of v2, /device:TPU:1, one launch (start us, length us, event | category | flops | bytes accessed | tf_op | source)
XLA Modules:
  0.0 131.1 jit_solution(18384510150763718958)
XLA Ops:
  0.0 0.7 copy-done.2
  0.7 0.7 shard_map.91
  1.4 13.2 %all-to-all-start = ((s32[64,1,32]{2,1,0:T(1,128)}), s32[64,1,32]{2,1,0:T(1,128)S(1)}, u32[]{:S(2)}, u32[]{:S(2)}) async-start(s32[64,1,32]{2,1,0:T(1,128)} %bitcast.1), calls=%async_computation | async-start | bytes 65536 | tf_op jit(solution)/shard_map/all_to_all | solution.py:363
  14.6 4.0 %shard_map.94.slots_ref = f8e4m3fn[2048,1024]{1,0:T(32,128)(4,1)} custom-call(s32[2,1024]{1,0:T(2,128)} %bitcast.28), custom_call_target="tpu_custom_call" | custom-call | flops 10000000 | bytes 4194304 | tf_op jit(solution)/shard_map/pallas_call | solution.py:39
  18.6 5.3 %all-to-all-done = s32[64,1,32]{2,1,0:T(1,128)S(1)} async-done(((s32[64,1,32]{2,1,0:T(1,128)}), s32[64,1,32]{2,1,0:T(1,128)S(1)}, u32[]{:S(2)}, u32[]{:S(2)}) %all-to-all-start) | async-done | bytes 8224 | tf_op jit(solution)/shard_map/all_to_all | solution.py:363
  24.5 5.7 %shard_map.92 = bf16[64,32,128]{2,1,0:T(8,128)(2,1)} custom-call(s32[64,32]{1,0:T(8,128)} %bitcast.18, bf16[8192,128]{1,0:T(8,128)(2,1)} %table_far.1), custom_call_target="tpu_custom_call" | custom-call | flops 1000000 | bytes 6000000 | tf_op jit(solution)/shard_map/pallas_call | solution.py:39
  30.3 5.0 %all-to-all-start.1 = ((bf16[64,32,128]{2,1,0:T(8,128)(2,1)}), bf16[64,32,128]{2,1,0:T(8,128)(2,1)S(1)}, u32[]{:S(2)}, u32[]{:S(2)}) async-start(bf16[64,32,128]{2,1,0:T(8,128)(2,1)} %shard_map.92), calls=%async_computation.1 | async-start | bytes 1048576 | tf_op jit(solution)/shard_map/all_to_all | solution.py:381
  35.3 0.8 broadcast_subtract_fusion.3
  36.2 2.6 %collective-permute-start.2 = (s32[64,32]{1,0:T(8,128)}, s32[64,32]{1,0:T(8,128)S(1)}, u32[]{:S(2)}, u32[]{:S(2)}) collective-permute-start(s32[64,32]{1,0:T(8,128)} %bitcast.20), channel_id=1, source_target_pairs={{0,3},{1,0},{2,1},{3,2},{4,7},{5,4},{6,5},{7,6},{8,11},{9,8},{10,9... | collective-permute-start | bytes 24584 | tf_op jit(solution)/shard_map/ppermute | solution.py:359
  39.3 0.6 collective-permute-start
  40.0 0.6 convert_bitcast_fusion.kept_ref
  40.6 5.8 %shard_map.93.edges_ref = f8e4m3fn[2,1024,1024]{2,1,0:T(32,128)(4,1)} custom-call(s32[8,1024]{1,0:T(8,128)} %bitcast.27, f32[2,8,1024]{2,1,0:T(8,128)} %convert_bitcast_fusion.kept_ref), custom_call_target="tpu_custom_call" | custom-call | flops 60000000 | bytes 4194304 | tf_op jit(solution)/shard_map/pallas_call | solution.py:39
  47.0 6.0 %all-to-all-done.1 = bf16[64,32,128]{2,1,0:T(8,128)(2,1)S(1)} async-done(((bf16[64,32,128]{2,1,0:T(8,128)(2,1)}), bf16[64,32,128]{2,1,0:T(8,128)(2,1)S(1)}, u32[]{:S(2)}, u32[]{:S(2)}) %all-to-all-start.1) | async-done | bytes 524320 | tf_op jit(solution)/shard_map/all_to_all | solution.py:381
  53.1 1.6 %copy-done.1 = f8e4m3fn[2,1024,1024]{2,1,0:T(32,128)(4,1)S(1)} copy-done((f8e4m3fn[2,1024,1024]{2,1,0:T(32,128)(4,1)S(1)}, f8e4m3fn[2,1024,1024]{2,1,0:T(32,128)(4,1)}, u32[]{:S(2)}) %copy-start.1) | copy-done | bytes 2097176
  54.6 4.1 %shard_map.95 = (bf16[256,512]{1,0:T(8,128)(2,1)S(1)}, f32[256,512]{1,0:T(8,128)S(1)}, bf16[2,256,1024]{2,1,0:T(8,128)(2,1)S(1)}, bf16[256,512]{1,0:T(8,128)(2,1...) custom-call(bf16[2048,128]{1,0:T(8,128)(2,1)S(1)} %bitcast.16, ...), custom_call_target="tpu_custom_call" | custom-call | flops 2400000000 | bytes 10000000 | tf_op jit(solution)/shard_map/pallas_call | solution.py:39
  58.8 2.6 %collective-permute-start.4 = (bf16[256,512]{1,0:T(8,128)(2,1)S(1)}, bf16[256,512]{1,0:T(8,128)(2,1)S(1)}, u32[]{:S(2)}, u32[]{:S(2)}) collective-permute-start(bf16[256,512]{1,0:T(8,128)(2,1)S(1)} %get-tuple-element.67.key0_ref), channel_id=1, source_target_pairs={{0,3},{1,0},{2,1},{3,2},{4,7},{5,4},{6,5},{7,6},{8,11},{9,8},{10,9... | collective-permute-start | bytes 786440 | tf_op jit(solution)/shard_map/ppermute | solution.py:359
  61.4 1.7 %collective-permute-start.5 = (bf16[256,512]{1,0:T(8,128)(2,1)S(1)}, bf16[256,512]{1,0:T(8,128)(2,1)S(1)}, u32[]{:S(2)}, u32[]{:S(2)}) collective-permute-start(bf16[256,512]{1,0:T(8,128)(2,1)S(1)} %get-tuple-element.67.key0_ref), channel_id=1, source_target_pairs={{0,2},{1,3},{2,0},{3,1},{4,6},{5,7},{6,4},{7,5},{8,10},{9,11},{10,... | collective-permute-start | bytes 786440 | tf_op jit(solution)/shard_map/ppermute | solution.py:359
  63.1 4.2 %collective-permute-done.4.key3_ref = bf16[256,512]{1,0:T(8,128)(2,1)S(1)} collective-permute-done((bf16[256,512]{1,0:T(8,128)(2,1)S(1)}, bf16[256,512]{1,0:T(8,128)(2,1)S(1)}, u32[]{:S(2)}, u32[]{:S(2)}) %collective-permute-start.4) | collective-permute-done | bytes 262176 | tf_op jit(solution)/shard_map/ppermute | solution.py:359
  67.3 3.3 %collective-permute-done.3.key1_ref = bf16[256,512]{1,0:T(8,128)(2,1)S(1)} collective-permute-done((bf16[256,512]{1,0:T(8,128)(2,1)S(1)}, bf16[256,512]{1,0:T(8,128)(2,1)S(1)}, u32[]{:S(2)}, u32[]{:S(2)}) %collective-permute-start.3) | collective-permute-done | bytes 262176 | tf_op jit(solution)/shard_map/ppermute | solution.py:359
  72.0 1.4 %shard_map.96 = (f32[1536,512]{1,0:T(8,128)S(1)}, f32[1,512]{1,0:T(1,128)S(1)}, f32[1024,1]{1,0:T(8,128)S(1)}) custom-call(bf16[256,512]{1,0:T(8,128)(2,1)S(1)} %get-tuple-element.67.key0_ref, bf16[256,512]{1,0:T(8,128)(2,1)S(1)} %collective-permute-done.3.key1_ref, bf16[256,512]{1,0:T(8,128)(2,1)S(1)} %collective-permute-done.4.key3_ref), custom_call_target="tpu_custom_call" | custom-call | flops 800000000 | bytes 4000000 | tf_op jit(solution)/shard_map/pallas_call | solution.py:39
  73.4 1.1 collective-permute-done.5.key2_ref
  74.5 6.6 %shard_map.97 = bf16[2048,128]{1,0:T(8,128)(2,1)S(1)} custom-call(bf16[256,512]{1,0:T(8,128)(2,1)S(1)} %get-tuple-element.67.key0_ref, bf16[256,512]{1,0:T(8,128)(2,1)S(1)} %collective-permute-done.3.key1_ref, bf16[256,512]{1,0:T(8,128)(2,1)S(1)} %collective-permute-done.4.key3_ref, bf16[256,512]{1,0:T(8,128)(2,1)S(1)} %collective-permute-done.5.key2_ref, ...), custom_call_target="tpu_custom_call" | custom-call | flops 8000000000 | bytes 12000000 | tf_op jit(solution)/shard_map/pallas_call | solution.py:39
  81.1 27.7 %all_to_all.21 = bf16[64,32,128]{2,1,0:T(8,128)(2,1)S(1)} all-to-all(bf16[64,32,128]{2,1,0:T(8,128)(2,1)S(1)} %bitcast.17), channel_id=1, replica_groups=mesh['table'=64,'batch'=4] {'table'}, dimensions={0} | all-to-all | bytes 1048576 | tf_op jit(solution)/shard_map/all_to_all | solution.py:472
  108.9 2.7 %collective-permute-start.8 = (bf16[1024,128]{1,0:T(8,128)(2,1)S(1)}, bf16[1024,128]{1,0:T(8,128)(2,1)S(1)}, u32[]{:S(2)}, u32[]{:S(2)}) collective-permute-start(bf16[1024,128]{1,0:T(8,128)(2,1)S(1)} %bitcast.23), channel_id=1, source_target_pairs={{0,3},{1,0},{2,1},{3,2},{4,7},{5,4},{6,5},{7,6},{8,11},{9,8},{10,9... | collective-permute-start | bytes 786440 | tf_op jit(solution)/shard_map/ppermute | solution.py:359
  111.6 1.4 %collective-permute-start.10 = (bf16[1024,128]{1,0:T(8,128)(2,1)S(1)}, bf16[1024,128]{1,0:T(8,128)(2,1)S(1)}, u32[]{:S(2)}, u32[]{:S(2)}) collective-permute-start(bf16[1024,128]{1,0:T(8,128)(2,1)S(1)} %bitcast.24), channel_id=1, source_target_pairs={{0,1},{1,2},{2,3},{3,0},{4,5},{5,6},{6,7},{7,4},{8,9},{9,10},{10,1... | collective-permute-start | bytes 786440 | tf_op jit(solution)/shard_map/ppermute | solution.py:359
  113.0 4.6 %collective-permute-done.6.refs_2_ = bf16[1024,128]{1,0:T(8,128)(2,1)S(1)} collective-permute-done((bf16[1024,128]{1,0:T(8,128)(2,1)S(1)}, bf16[1024,128]{1,0:T(8,128)(2,1)S(1)}, u32[]{:S(2)}, u32[]{:S(2)}) %collective-permute-start.6) | collective-permute-done | bytes 262176 | tf_op jit(solution)/shard_map/ppermute | solution.py:359
  117.6 2.7 %collective-permute-start.9 = (bf16[1024,128]{1,0:T(8,128)(2,1)S(1)}, bf16[1024,128]{1,0:T(8,128)(2,1)S(1)}, u32[]{:S(2)}, u32[]{:S(2)}) collective-permute-start(bf16[1024,128]{1,0:T(8,128)(2,1)S(1)} %collective-permute-done.8.refs_5_), channel_id=1, source_target_pairs={{0,3},{1,0},{2,1},{3,2},{4,7},{5,4},{6,5},{7,6},{8,11},{9,8},{10,9... | collective-permute-start | bytes 786440 | tf_op jit(solution)/shard_map/ppermute | solution.py:359
  120.3 1.3 shard_map.98.refs_6_
  121.5 1.3 shard_map.99.refs_6_
  123.2 1.3 shard_map.100.refs_6_
  124.5 4.3 %collective-permute-done.7.refs_2_ = bf16[1024,128]{1,0:T(8,128)(2,1)S(1)} collective-permute-done((bf16[1024,128]{1,0:T(8,128)(2,1)S(1)}, bf16[1024,128]{1,0:T(8,128)(2,1)S(1)}, u32[]{:S(2)}, u32[]{:S(2)}) %collective-permute-start.7) | collective-permute-done | bytes 262176 | tf_op jit(solution)/shard_map/ppermute | solution.py:359
  128.8 2.2 %shard_map.101 = f32[2048,128]{1,0:T(8,128)} custom-call(s32[1,2048]{1,0:T(1,128)S(1)} %sub.98.refs_0_.refs_3_, bf16[2048,128]{1,0:T(8,128)(2,1)S(1)} %broadcast_in_dim.18.refs_1_.refs_4_, bf16[1024,128]{1,0:T(8,128)(2,1)S(1)} %collective-permute-done.7.refs_2_, s32[1,2048]{1,0:T(1,128)S(1)} %sub.98.refs_0_.refs_3_, ...), custom_call_target="tpu_custom_call" | custom-call | flops 1000000000 | bytes 4000000 | tf_op jit(solution)/shard_map/pallas_call | solution.py:39
  (50 shorter events, 3.8 us)
Async XLA Ops:
  0.0 0.7 copy-start.2
  0.7 39.2 %copy-start.8 = (s32[2,1024,8]{1,2,0:T(8,128)S(1)}, s32[2,1024,8]{1,2,0:T(8,128)}, u32[]{:S(2)}) copy-start(s32[2,1024,8]{1,2,0:T(8,128)} %param.13) | copy-start | bytes 196612
  1.4 22.5 %all-to-all-start = ((s32[64,1,32]{2,1,0:T(1,128)}), s32[64,1,32]{2,1,0:T(1,128)S(1)}, u32[]{:S(2)}, u32[]{:S(2)}) async-start(s32[64,1,32]{2,1,0:T(1,128)} %bitcast.1), calls=%async_computation | async-start | bytes 65536 | tf_op jit(solution)/shard_map/all_to_all | solution.py:363
  23.9 0.6 copy-start.7
  24.5 28.5 %copy-start = (f8e4m3fn[2048,1024]{1,0:T(32,128)(4,1)S(1)}, f8e4m3fn[2048,1024]{1,0:T(32,128)(4,1)}, u32[]{:S(2)}) copy-start(f8e4m3fn[2048,1024]{1,0:T(32,128)(4,1)} %shard_map.94.slots_ref) | copy-start | bytes 6291460
  24.5 28.5 %copy-start.3 = (bf16[256,256]{1,0:T(8,128)(2,1)S(1)}, bf16[256,256]{1,0:T(8,128)(2,1)}, u32[]{:S(2)}) copy-start(bf16[256,256]{1,0:T(8,128)(2,1)} %two_ref.3) | copy-start | bytes 393220
  24.5 28.5 %copy-start.4 = (bf16[256,256]{1,0:T(8,128)(2,1)S(1)}, bf16[256,256]{1,0:T(8,128)(2,1)}, u32[]{:S(2)}) copy-start(bf16[256,256]{1,0:T(8,128)(2,1)} %first_ref.3) | copy-start | bytes 393220
  24.5 28.5 %copy-start.5 = (bf16[256,256]{1,0:T(8,128)(2,1)S(1)}, bf16[256,256]{1,0:T(8,128)(2,1)}, u32[]{:S(2)}) copy-start(bf16[256,256]{1,0:T(8,128)(2,1)} %second_ref.3) | copy-start | bytes 393220
  24.5 28.5 %copy-start.6 = (bf16[128,256]{1,0:T(8,128)(2,1)S(1)}, bf16[128,256]{1,0:T(8,128)(2,1)}, u32[]{:S(2)}) copy-start(bf16[128,256]{1,0:T(8,128)(2,1)} %one_ref.3) | copy-start | bytes 196612
  30.3 22.8 %all-to-all-start.1 = ((bf16[64,32,128]{2,1,0:T(8,128)(2,1)}), bf16[64,32,128]{2,1,0:T(8,128)(2,1)S(1)}, u32[]{:S(2)}, u32[]{:S(2)}) async-start(bf16[64,32,128]{2,1,0:T(8,128)(2,1)} %shard_map.92), calls=%async_computation.1 | async-start | bytes 1048576 | tf_op jit(solution)/shard_map/all_to_all | solution.py:381
  36.2 10.2 %collective-permute-start.2 = (s32[64,32]{1,0:T(8,128)}, s32[64,32]{1,0:T(8,128)S(1)}, u32[]{:S(2)}, u32[]{:S(2)}) collective-permute-start(s32[64,32]{1,0:T(8,128)} %bitcast.20), channel_id=1, source_target_pairs={{0,3},{1,0},{2,1},{3,2},{4,7},{5,4},{6,5},{7,6},{8,11},{9,8},{10,9... | collective-permute-start | bytes 24584 | tf_op jit(solution)/shard_map/ppermute | solution.py:359
  38.8 7.6 %collective-permute-start.1 = (s32[64,32]{1,0:T(8,128)}, s32[64,32]{1,0:T(8,128)S(1)}, u32[]{:S(2)}, u32[]{:S(2)}) collective-permute-start(s32[64,32]{1,0:T(8,128)} %bitcast.21), channel_id=1, source_target_pairs={{0,2},{1,3},{2,0},{3,1},{4,6},{5,7},{6,4},{7,5},{8,10},{9,11},{10,... | collective-permute-start | bytes 24584 | tf_op jit(solution)/shard_map/ppermute | solution.py:359
  39.3 7.4 %collective-permute-start = (s32[64,32]{1,0:T(8,128)}, s32[64,32]{1,0:T(8,128)S(1)}, u32[]{:S(2)}, u32[]{:S(2)}) collective-permute-start(s32[64,32]{1,0:T(8,128)} %bitcast.22), channel_id=1, source_target_pairs={{0,1},{1,2},{2,3},{3,0},{4,5},{5,6},{6,7},{7,4},{8,9},{9,10},{10,1... | collective-permute-start | bytes 24584 | tf_op jit(solution)/shard_map/ppermute | solution.py:359
  53.0 1.6 %copy-start.1 = (f8e4m3fn[2,1024,1024]{2,1,0:T(32,128)(4,1)S(1)}, f8e4m3fn[2,1024,1024]{2,1,0:T(32,128)(4,1)}, u32[]{:S(2)}) copy-start(f8e4m3fn[2,1024,1024]{2,1,0:T(32,128)(4,1)} %shard_map.93.edges_ref) | copy-start | bytes 6291460
  58.8 8.5 %collective-permute-start.4 = (bf16[256,512]{1,0:T(8,128)(2,1)S(1)}, bf16[256,512]{1,0:T(8,128)(2,1)S(1)}, u32[]{:S(2)}, u32[]{:S(2)}) collective-permute-start(bf16[256,512]{1,0:T(8,128)(2,1)S(1)} %get-tuple-element.67.key0_ref), channel_id=1, source_target_pairs={{0,3},{1,0},{2,1},{3,2},{4,7},{5,4},{6,5},{7,6},{8,11},{9,8},{10,9... | collective-permute-start | bytes 786440 | tf_op jit(solution)/shard_map/ppermute | solution.py:359
  61.3 9.3 %collective-permute-start.3 = (bf16[256,512]{1,0:T(8,128)(2,1)S(1)}, bf16[256,512]{1,0:T(8,128)(2,1)S(1)}, u32[]{:S(2)}, u32[]{:S(2)}) collective-permute-start(bf16[256,512]{1,0:T(8,128)(2,1)S(1)} %get-tuple-element.67.key0_ref), channel_id=1, source_target_pairs={{0,1},{1,2},{2,3},{3,0},{4,5},{5,6},{6,7},{7,4},{8,9},{9,10},{10,1... | collective-permute-start | bytes 786440 | tf_op jit(solution)/shard_map/ppermute | solution.py:359
  61.4 13.1 %collective-permute-start.5 = (bf16[256,512]{1,0:T(8,128)(2,1)S(1)}, bf16[256,512]{1,0:T(8,128)(2,1)S(1)}, u32[]{:S(2)}, u32[]{:S(2)}) collective-permute-start(bf16[256,512]{1,0:T(8,128)(2,1)S(1)} %get-tuple-element.67.key0_ref), channel_id=1, source_target_pairs={{0,2},{1,3},{2,0},{3,1},{4,6},{5,7},{6,4},{7,5},{8,10},{9,11},{10,... | collective-permute-start | bytes 786440 | tf_op jit(solution)/shard_map/ppermute | solution.py:359
  108.8 8.8 %collective-permute-start.6 = (bf16[1024,128]{1,0:T(8,128)(2,1)S(1)}, bf16[1024,128]{1,0:T(8,128)(2,1)S(1)}, u32[]{:S(2)}, u32[]{:S(2)}) collective-permute-start(bf16[1024,128]{1,0:T(8,128)(2,1)S(1)} %bitcast.25), channel_id=1, source_target_pairs={{0,1},{1,2},{2,3},{3,0},{4,5},{5,6},{6,7},{7,4},{8,9},{9,10},{10,1... | collective-permute-start | bytes 786440 | tf_op jit(solution)/shard_map/ppermute | solution.py:359
  108.9 8.7 %collective-permute-start.8 = (bf16[1024,128]{1,0:T(8,128)(2,1)S(1)}, bf16[1024,128]{1,0:T(8,128)(2,1)S(1)}, u32[]{:S(2)}, u32[]{:S(2)}) collective-permute-start(bf16[1024,128]{1,0:T(8,128)(2,1)S(1)} %bitcast.23), channel_id=1, source_target_pairs={{0,3},{1,0},{2,1},{3,2},{4,7},{5,4},{6,5},{7,6},{8,11},{9,8},{10,9... | collective-permute-start | bytes 786440 | tf_op jit(solution)/shard_map/ppermute | solution.py:359
  111.6 11.2 %collective-permute-start.11 = (bf16[1024,128]{1,0:T(8,128)(2,1)S(1)}, bf16[1024,128]{1,0:T(8,128)(2,1)S(1)}, u32[]{:S(2)}, u32[]{:S(2)}) collective-permute-start(bf16[1024,128]{1,0:T(8,128)(2,1)S(1)} %bitcast.26), channel_id=1, source_target_pairs={{0,3},{1,0},{2,1},{3,2},{4,7},{5,4},{6,5},{7,6},{8,11},{9,8},{10,9... | collective-permute-start | bytes 786440 | tf_op jit(solution)/shard_map/ppermute | solution.py:359
  111.6 11.6 %collective-permute-start.10 = (bf16[1024,128]{1,0:T(8,128)(2,1)S(1)}, bf16[1024,128]{1,0:T(8,128)(2,1)S(1)}, u32[]{:S(2)}, u32[]{:S(2)}) collective-permute-start(bf16[1024,128]{1,0:T(8,128)(2,1)S(1)} %bitcast.24), channel_id=1, source_target_pairs={{0,1},{1,2},{2,3},{3,0},{4,5},{5,6},{6,7},{7,4},{8,9},{9,10},{10,1... | collective-permute-start | bytes 786440 | tf_op jit(solution)/shard_map/ppermute | solution.py:359
  117.6 11.2 %collective-permute-start.7 = (bf16[1024,128]{1,0:T(8,128)(2,1)S(1)}, bf16[1024,128]{1,0:T(8,128)(2,1)S(1)}, u32[]{:S(2)}, u32[]{:S(2)}) collective-permute-start(bf16[1024,128]{1,0:T(8,128)(2,1)S(1)} %collective-permute-done.6.refs_2_), channel_id=1, source_target_pairs={{0,1},{1,2},{2,3},{3,0},{4,5},{5,6},{6,7},{7,4},{8,9},{9,10},{10,1... | collective-permute-start | bytes 786440 | tf_op jit(solution)/shard_map/ppermute | solution.py:359
  117.6 11.2 %collective-permute-start.9 = (bf16[1024,128]{1,0:T(8,128)(2,1)S(1)}, bf16[1024,128]{1,0:T(8,128)(2,1)S(1)}, u32[]{:S(2)}, u32[]{:S(2)}) collective-permute-start(bf16[1024,128]{1,0:T(8,128)(2,1)S(1)} %collective-permute-done.8.refs_5_), channel_id=1, source_target_pairs={{0,3},{1,0},{2,1},{3,2},{4,7},{5,4},{6,5},{7,6},{8,11},{9,8},{10,9... | collective-permute-start | bytes 786440 | tf_op jit(solution)/shard_map/ppermute | solution.py:359

commit v3 on v2

--- a/solution.py
+++ b/solution.py
@@ -49,7 +49,7 @@
     )(*args)
 
 
-TILE, LANES, ROWS = 32, 128, 64
+TILE, LANES, ROWS = 32, 128, 128
 
 
 def spread(row, kind):
@@ -98,6 +98,7 @@
 
 def slots_kernel(slot_ref, slots_far, slots_ref, sem):
     hashes, nodes = slot_ref.shape
+    rows = min(256, slots_ref.shape[0])
     one, none = jnp.ones((), BF16), jnp.zeros((), BF16)
     copies = []
     for part in range(nodes // LANES):
@@ -105,8 +106,8 @@
         named = [spread(slot_ref[which : which + 1, span], jnp.int16) for which in range(hashes)]
 
         def step(block, carry):
-            for tile in range(ROWS // TILE):
-                start = pl.multiple_of(block * ROWS + tile * TILE, TILE)
+            for tile in range(rows // TILE):
+                start = pl.multiple_of(block * rows + tile * TILE, TILE)
                 ids = (places(0) + start).astype(jnp.int16)
                 total = jnp.where(named[0] == ids, one, none)
                 for which in range(1, hashes):
@@ -114,23 +115,13 @@
                 slots_ref[pl.ds(start, TILE), span] = total.astype(F8)
             return carry
 
-        lax.fori_loop(0, slots_ref.shape[0] // ROWS, step, 0)
+        lax.fori_loop(0, slots_ref.shape[0] // rows, step, 0)
         copies.append(
             pltpu.make_async_copy(slots_ref.at[:, span], slots_far.at[:, span], sem.at[part])
         )
         copies[-1].start()
     for copy in copies:
         copy.wait()
-
-
-def slot_parts(source, target, sems):
-    count = sems.shape[0]
-    part = target.shape[0] // count
-    spans = [pl.ds(place * part, part) for place in range(count)]
-    return [
-        pltpu.make_async_copy(source.at[span], target.at[span], sems.at[place])
-        for place, span in enumerate(spans)
-    ]
 
 
 def forward_kernel(
@@ -279,29 +270,27 @@
 
 
 def fetch_kernel(
-    asked_far, table_far, out_ref, table_ref, wide_ref, rows_ref, index_ref, sem, table_sem
+    asked_ref, table_ref, out_ref, again_ref, wide_ref, rows_ref, row_ref, index_ref, sem
 ):
     slabs, slots = index_ref.shape
-    copy = pltpu.make_async_copy(asked_far, index_ref, sem)
+    asked = asked_ref[...]
+    row_ref[...] = jnp.maximum(asked, 0)
+    copy = pltpu.make_async_copy(row_ref, index_ref, sem)
     copy.start()
-    table_copies = slot_parts(table_far, table_ref, table_sem)
-    for table_copy in table_copies:
-        table_copy.start()
-    part = table_ref.shape[0] // len(table_copies)
-    for place, table_copy in enumerate(table_copies):
-        table_copy.wait()
-        span = slice(place * part, (place + 1) * part)
-        wide_ref[span, :] = table_ref[span, :].astype(F32)
+    again_ref[...] = asked
+    wide_ref[...] = table_ref[...].astype(F32)
     copy.wait()
 
-    def step(slab, carry):
-        start = pl.multiple_of(slab * slots, slots)
-        for slot in range(slots):
-            row = jnp.maximum(index_ref[slab, slot], 0)
-            rows_ref[pl.ds(start + slot, 1), :] = wide_ref[pl.ds(row, 1), :]
+    def step(pair, carry):
+        for which in range(2):
+            slab = 2 * pair + which
+            start = pl.multiple_of(slab * slots, slots)
+            for slot in range(slots):
+                row = index_ref[slab, slot]
+                rows_ref[pl.ds(start + slot, 1), :] = wide_ref[pl.ds(row, 1), :]
         return carry
 
-    lax.fori_loop(0, slabs, step, 0)
+    lax.fori_loop(0, slabs // 2, step, 0)
     out_ref[...] = rows_ref[...].astype(BF16).reshape(out_ref.shape)
 
 
@@ -361,25 +350,6 @@
         )
 
     received = lax.all_to_all(requests, "table", split_axis=0, concat_axis=0, tiled=True)
-    (fetched,) = call(
-        fetch_kernel,
-        [jax.ShapeDtypeStruct(requests.shape + (width,), BF16)],
-        [received, embedding_table],
-        flops=1_000_000,
-        moved=6_000_000,
-        mib=60,
-        scratch=[
-            pltpu.VMEM((shard_rows, width), BF16),
-            pltpu.VMEM((shard_rows, width), F32),
-            pltpu.VMEM((slot_count, width), F32),
-            pltpu.SMEM(requests.shape, jnp.int32),
-            pltpu.SemaphoreType.DMA,
-            pltpu.SemaphoreType.DMA((8,)),
-        ],
-        far=(0, 1),
-    )
-    arrived = lax.all_to_all(fetched, "table", split_axis=0, concat_axis=0, tiled=True)
-
     (slots,) = call(
         slots_kernel,
         [jax.ShapeDtypeStruct((slot_count, nodes), F8)],
@@ -393,6 +363,26 @@
         ],
         far_outs=(0,),
     )
+    fetched, received = call(
+        fetch_kernel,
+        [
+            jax.ShapeDtypeStruct(requests.shape + (width,), BF16),
+            jax.ShapeDtypeStruct(requests.shape, jnp.int32),
+        ],
+        [received, embedding_table],
+        flops=1_000_000,
+        moved=6_000_000,
+        mib=24,
+        scratch=[
+            pltpu.VMEM((shard_rows, width), F32),
+            pltpu.VMEM((slot_count, width), F32),
+            pltpu.VMEM(requests.shape, jnp.int32),
+            pltpu.SMEM(requests.shape, jnp.int32),
+            pltpu.SemaphoreType.DMA,
+        ],
+    )
+    arrived = lax.all_to_all(fetched, "table", split_axis=0, concat_axis=0, tiled=True)
+
     fetched, received, near, kept = lax.optimization_barrier(
         (fetched, received, neighbours.T, kept_edges)
     )
@@ -442,10 +432,6 @@
         mib=32,
     )
     ahead, far, behind = [turn(keys, by) for by in (1, 2, 3)]
-    keys, owned = lax.optimization_barrier((keys, owned))
-    lanes = [jnp.broadcast_to(part_of[:, None], (slot_count, width)) for _, part_of in owned]
-    ahead, behind, lanes = lax.optimization_barrier((ahead, behind, lanes))
-    owned = [(index, lane) for (index, _), lane in zip(owned, lanes)]
     expo, total0, totals = call(
         early_kernel,
         [
@@ -477,7 +463,12 @@
     upper, lower = slice(0, half), slice(half, slot_count)
     from_left = [turn(returned[upper], 1)]
     from_right = [turn(returned[lower], 3)]
+    from_left[0], owned = lax.optimization_barrier((from_left[0], owned))
+    owned = [
+        (index, jnp.broadcast_to(part_of[:, None], (slot_count, width))) for index, part_of in owned
+    ]
     from_left.append(turn(returned[lower], 1))
+    owned[0], owned[2] = lax.optimization_barrier((owned[0], owned[2]))
     from_right.append(turn(returned[upper], 3))
     from_far = [turn(from_left[0], 1), turn(from_right[0], 3)]
     rounds = (

time: 132 us -> 128 us (0.970)
  Pallas kernels: 34.4 us -> 31 us
  waiting for transfers between devices: 29.2 us -> 31 us
  blocking collectives: 27.7 us -> 26.3 us
    pallas_call x11, Pallas kernels: 34.4 us -> 31 us  [call(): pl.pallas_call(kernel, out_shape=outs, in_specs=[HBM if place in far else...]
    all_to_all x1, blocking collectives: 27.7 us -> 26.3 us  [body(): lax.all_to_all(grads.reshape(table_count, -1, width), 'table', split_axis...]
  transfers between devices with their start and end apart: 14 -> 14, of which waited for: 8 -> 6; matrix products, arithmetic and copies ran while one was open for 3% -> 2% of each run, Pallas kernels for 11% -> 11%
where the time goes in v3:
time: 128 us; the launch traced here: 127 us
  starting transfers between devices  33.2 us (26%)
  Pallas kernels  31 us (24%)
  waiting for transfers between devices  31 us (24%)
  blocking collectives  26.3 us (21%)
  local copies, waits for them, and re-layouts  4.45 us (3%)
    pallas_call x11, Pallas kernels, call(): pl.pallas_call(kernel, out_shape=outs, in_specs=[HBM if place in far else...  31 us
    all_to_all x1, blocking collectives, body(): lax.all_to_all(grads.reshape(table_count, -1, width), 'table', split_axis...  26.3 us
    ppermute x12, waiting for transfers between devices, turn(): lax.ppermute(value, 'batch', [(source, (source + by) % batch_count) for s...  17.6 us
    ppermute x12, starting transfers between devices, turn(): lax.ppermute(value, 'batch', [(source, (source + by) % batch_count) for s...  15.2 us
    all_to_all x1, starting transfers between devices, body(): lax.all_to_all(requests, 'table', split_axis=0, concat_axis=0, tiled=True)  13.2 us
    all_to_all x1, waiting for transfers between devices, body(): lax.all_to_all(fetched, 'table', split_axis=0, concat_axis=0, tiled=True)  7.29 us
    all_to_all x1, waiting for transfers between devices, body(): lax.all_to_all(requests, 'table', split_axis=0, concat_axis=0, tiled=True)  6.19 us
    all_to_all x1, starting transfers between devices, body(): lax.all_to_all(fetched, 'table', split_axis=0, concat_axis=0, tiled=True)  4.89 us
  transfers between devices with their start and end apart: 14, of which 6 were waited for; matrix products, arithmetic and copies ran while one was open for 2% of the time, Pallas kernels for 11%

profile of v3, /device:TPU:1, one launch (start us, length us, event | category | flops | bytes accessed | tf_op | source)
XLA Modules:
  0.0 127.1 jit_solution(15954163624329901966)
XLA Ops:
  0.0 0.8 copy-done.3
  0.9 0.7 shard_map.91
  1.6 13.2 %all-to-all-start = ((s32[64,1,32]{2,1,0:T(1,128)}), s32[64,1,32]{2,1,0:T(1,128)S(1)}, u32[]{:S(2)}, u32[]{:S(2)}) async-start(s32[64,1,32]{2,1,0:T(1,128)} %bitcast.1), calls=%async_computation | async-start | bytes 65536 | tf_op jit(solution)/shard_map/all_to_all | solution.py:352
  14.8 3.1 %shard_map.94.slots_ref = f8e4m3fn[2048,1024]{1,0:T(32,128)(4,1)} custom-call(s32[2,1024]{1,0:T(2,128)} %bitcast.24), custom_call_target="tpu_custom_call" | custom-call | flops 10000000 | bytes 4194304 | tf_op jit(solution)/shard_map/pallas_call | solution.py:39
  17.9 6.2 %all-to-all-done = s32[64,1,32]{2,1,0:T(1,128)S(1)} async-done(((s32[64,1,32]{2,1,0:T(1,128)}), s32[64,1,32]{2,1,0:T(1,128)S(1)}, u32[]{:S(2)}, u32[]{:S(2)}) %all-to-all-start) | async-done | bytes 8224 | tf_op jit(solution)/shard_map/all_to_all | solution.py:352
  24.1 3.7 %shard_map.92 = (bf16[64,32,128]{2,1,0:T(8,128)(2,1)}, s32[64,32]{1,0:T(8,128)S(1)}) custom-call(s32[64,32]{1,0:T(8,128)S(1)} %bitcast.18, bf16[8192,128]{1,0:T(8,128)(2,1)S(1)} %copy-done), custom_call_target="tpu_custom_call" | custom-call | flops 1000000 | bytes 6000000 | tf_op jit(solution)/shard_map/pallas_call | solution.py:39
  27.8 4.9 %all-to-all-start.1 = ((bf16[64,32,128]{2,1,0:T(8,128)(2,1)}), bf16[64,32,128]{2,1,0:T(8,128)(2,1)S(1)}, u32[]{:S(2)}, u32[]{:S(2)}) async-start(bf16[64,32,128]{2,1,0:T(8,128)(2,1)} %get-tuple-element.45), calls=%async_computation.1 | async-start | bytes 1048576 | tf_op jit(solution)/shard_map/all_to_all | solution.py:384
  32.8 2.6 %collective-permute-start.2 = (s32[64,32]{1,0:T(8,128)S(1)}, s32[64,32]{1,0:T(8,128)S(1)}, u32[]{:S(2)}, u32[]{:S(2)}) collective-permute-start(s32[64,32]{1,0:T(8,128)S(1)} %get-tuple-element.47), channel_id=1, source_target_pairs={{0,3},{1,0},{2,1},{3,2},{4,7},{5,4},{6,5},{7,6},{8,11},{9,8},{10,9... | collective-permute-start | bytes 24584 | tf_op jit(solution)/shard_map/ppermute | solution.py:348
  35.4 0.5 collective-permute-start.1
  35.9 0.6 collective-permute-start
  36.6 0.6 convert_bitcast_fusion.kept_ref
  37.2 5.4 %shard_map.93.edges_ref = f8e4m3fn[2,1024,1024]{2,1,0:T(32,128)(4,1)} custom-call(s32[8,1024]{1,0:T(8,128)} %bitcast.23, f32[2,8,1024]{2,1,0:T(8,128)} %convert_bitcast_fusion.kept_ref), custom_call_target="tpu_custom_call" | custom-call | flops 60000000 | bytes 4194304 | tf_op jit(solution)/shard_map/pallas_call | solution.py:39
  43.2 7.3 %all-to-all-done.1 = bf16[64,32,128]{2,1,0:T(8,128)(2,1)S(1)} async-done(((bf16[64,32,128]{2,1,0:T(8,128)(2,1)}), bf16[64,32,128]{2,1,0:T(8,128)(2,1)S(1)}, u32[]{:S(2)}, u32[]{:S(2)}) %all-to-all-start.1) | async-done | bytes 524320 | tf_op jit(solution)/shard_map/all_to_all | solution.py:384
  50.5 1.6 %copy-done.2 = f8e4m3fn[2,1024,1024]{2,1,0:T(32,128)(4,1)S(1)} copy-done((f8e4m3fn[2,1024,1024]{2,1,0:T(32,128)(4,1)S(1)}, f8e4m3fn[2,1024,1024]{2,1,0:T(32,128)(4,1)}, u32[]{:S(2)}) %copy-start.2) | copy-done | bytes 2097176
  52.1 4.1 %shard_map.95 = (bf16[256,512]{1,0:T(8,128)(2,1)S(1)}, f32[256,512]{1,0:T(8,128)S(1)}, bf16[2,256,1024]{2,1,0:T(8,128)(2,1)S(1)}, bf16[256,512]{1,0:T(8,128)(2,1...) custom-call(bf16[2048,128]{1,0:T(8,128)(2,1)S(1)} %bitcast.16, ...), custom_call_target="tpu_custom_call" | custom-call | flops 2400000000 | bytes 10000000 | tf_op jit(solution)/shard_map/pallas_call | solution.py:39
  56.2 2.6 %collective-permute-start.4 = (bf16[256,512]{1,0:T(8,128)(2,1)S(1)}, bf16[256,512]{1,0:T(8,128)(2,1)S(1)}, u32[]{:S(2)}, u32[]{:S(2)}) collective-permute-start(bf16[256,512]{1,0:T(8,128)(2,1)S(1)} %get-tuple-element.54.key0_ref), channel_id=1, source_target_pairs={{0,3},{1,0},{2,1},{3,2},{4,7},{5,4},{6,5},{7,6},{8,11},{9,8},{10,9... | collective-permute-start | bytes 786440 | tf_op jit(solution)/shard_map/ppermute | solution.py:348
  58.8 1.7 %collective-permute-start.5 = (bf16[256,512]{1,0:T(8,128)(2,1)S(1)}, bf16[256,512]{1,0:T(8,128)(2,1)S(1)}, u32[]{:S(2)}, u32[]{:S(2)}) collective-permute-start(bf16[256,512]{1,0:T(8,128)(2,1)S(1)} %get-tuple-element.54.key0_ref), channel_id=1, source_target_pairs={{0,2},{1,3},{2,0},{3,1},{4,6},{5,7},{6,4},{7,5},{8,10},{9,11},{10,... | collective-permute-start | bytes 786440 | tf_op jit(solution)/shard_map/ppermute | solution.py:348
  60.5 9.0 %collective-permute-done.4.key3_ref = bf16[256,512]{1,0:T(8,128)(2,1)S(1)} collective-permute-done((bf16[256,512]{1,0:T(8,128)(2,1)S(1)}, bf16[256,512]{1,0:T(8,128)(2,1)S(1)}, u32[]{:S(2)}, u32[]{:S(2)}) %collective-permute-start.4) | collective-permute-done | bytes 262176 | tf_op jit(solution)/shard_map/ppermute | solution.py:348
  69.6 1.4 %shard_map.96 = (f32[1536,512]{1,0:T(8,128)S(1)}, f32[1,512]{1,0:T(1,128)S(1)}, f32[1024,1]{1,0:T(8,128)S(1)}) custom-call(bf16[256,512]{1,0:T(8,128)(2,1)S(1)} %get-tuple-element.54.key0_ref, bf16[256,512]{1,0:T(8,128)(2,1)S(1)} %collective-permute-done.3.key1_ref, bf16[256,512]{1,0:T(8,128)(2,1)S(1)} %collective-permute-done.4.key3_ref), custom_call_target="tpu_custom_call" | custom-call | flops 800000000 | bytes 4000000 | tf_op jit(solution)/shard_map/pallas_call | solution.py:39
  71.0 0.9 collective-permute-done.5.key2_ref
  71.9 6.6 %shard_map.97 = bf16[2048,128]{1,0:T(8,128)(2,1)S(1)} custom-call(bf16[256,512]{1,0:T(8,128)(2,1)S(1)} %get-tuple-element.54.key0_ref, bf16[256,512]{1,0:T(8,128)(2,1)S(1)} %collective-permute-done.3.key1_ref, bf16[256,512]{1,0:T(8,128)(2,1)S(1)} %collective-permute-done.4.key3_ref, bf16[256,512]{1,0:T(8,128)(2,1)S(1)} %collective-permute-done.5.key2_ref, ...), custom_call_target="tpu_custom_call" | custom-call | flops 8000000000 | bytes 12000000 | tf_op jit(solution)/shard_map/pallas_call | solution.py:39
  78.5 26.3 %all_to_all.21 = bf16[64,32,128]{2,1,0:T(8,128)(2,1)S(1)} all-to-all(bf16[64,32,128]{2,1,0:T(8,128)(2,1)S(1)} %bitcast.17), channel_id=1, replica_groups=mesh['table'=64,'batch'=4] {'table'}, dimensions={0} | all-to-all | bytes 1048576 | tf_op jit(solution)/shard_map/all_to_all | solution.py:458
  105.0 2.7 %collective-permute-start.8 = (bf16[1024,128]{1,0:T(8,128)(2,1)S(1)}, bf16[1024,128]{1,0:T(8,128)(2,1)S(1)}, u32[]{:S(2)}, u32[]{:S(2)}) collective-permute-start(bf16[1024,128]{1,0:T(8,128)(2,1)S(1)} %bitcast.19), channel_id=1, source_target_pairs={{0,3},{1,0},{2,1},{3,2},{4,7},{5,4},{6,5},{7,6},{8,11},{9,8},{10,9... | collective-permute-start | bytes 786440 | tf_op jit(solution)/shard_map/ppermute | solution.py:348
  107.7 1.4 %collective-permute-start.10 = (bf16[1024,128]{1,0:T(8,128)(2,1)S(1)}, bf16[1024,128]{1,0:T(8,128)(2,1)S(1)}, u32[]{:S(2)}, u32[]{:S(2)}) collective-permute-start(bf16[1024,128]{1,0:T(8,128)(2,1)S(1)} %bitcast.20), channel_id=1, source_target_pairs={{0,1},{1,2},{2,3},{3,0},{4,5},{5,6},{6,7},{7,4},{8,9},{9,10},{10,1... | collective-permute-start | bytes 786440 | tf_op jit(solution)/shard_map/ppermute | solution.py:348
  109.1 4.6 %collective-permute-done.6.refs_2_ = bf16[1024,128]{1,0:T(8,128)(2,1)S(1)} collective-permute-done((bf16[1024,128]{1,0:T(8,128)(2,1)S(1)}, bf16[1024,128]{1,0:T(8,128)(2,1)S(1)}, u32[]{:S(2)}, u32[]{:S(2)}) %collective-permute-start.6) | collective-permute-done | bytes 262176 | tf_op jit(solution)/shard_map/ppermute | solution.py:348
  114.4 3.0 %collective-permute-start.9 = (bf16[1024,128]{1,0:T(8,128)(2,1)S(1)}, bf16[1024,128]{1,0:T(8,128)(2,1)S(1)}, u32[]{:S(2)}, u32[]{:S(2)}) collective-permute-start(bf16[1024,128]{1,0:T(8,128)(2,1)S(1)} %collective-permute-done.8.refs_5_), channel_id=1, source_target_pairs={{0,3},{1,0},{2,1},{3,2},{4,7},{5,4},{6,5},{7,6},{8,11},{9,8},{10,9... | collective-permute-start | bytes 786440 | tf_op jit(solution)/shard_map/ppermute | solution.py:348
  117.3 1.3 shard_map.98.refs_6_
  118.6 0.3 broadcast_in_dim.18.refs_1_
  119.3 1.3 shard_map.99.refs_6_
  120.6 1.3 shard_map.100.refs_6_
  121.8 3.1 %collective-permute-done.7.refs_2_ = bf16[1024,128]{1,0:T(8,128)(2,1)S(1)} collective-permute-done((bf16[1024,128]{1,0:T(8,128)(2,1)S(1)}, bf16[1024,128]{1,0:T(8,128)(2,1)S(1)}, u32[]{:S(2)}, u32[]{:S(2)}) %collective-permute-start.7) | collective-permute-done | bytes 262176 | tf_op jit(solution)/shard_map/ppermute | solution.py:348
  124.9 2.2 %shard_map.101 = f32[2048,128]{1,0:T(8,128)} custom-call(s32[1,2048]{1,0:T(1,128)S(1)} %sub.98.refs_0_.refs_3_, bf16[2048,128]{1,0:T(8,128)(2,1)S(1)} %broadcast_in_dim.17.refs_1_.refs_4_, bf16[1024,128]{1,0:T(8,128)(2,1)S(1)} %collective-permute-done.7.refs_2_, s32[1,2048]{1,0:T(1,128)S(1)} %sub.98.refs_0_.refs_3_, ...), custom_call_target="tpu_custom_call" | custom-call | flops 1000000000 | bytes 4000000 | tf_op jit(solution)/shard_map/pallas_call | solution.py:39
  (50 shorter events, 1.9 us)
Async XLA Ops:
  0.0 24.1 %copy-start = (bf16[8192,128]{1,0:T(8,128)(2,1)S(1)}, bf16[8192,128]{1,0:T(8,128)(2,1)}, u32[]{:S(2)}) copy-start(bf16[8192,128]{1,0:T(8,128)(2,1)} %table_ref.1) | copy-start | bytes 6291460
  0.0 0.8 copy-start.3
  0.8 35.7 %copy-start.8 = (s32[2,1024,8]{1,2,0:T(8,128)S(1)}, s32[2,1024,8]{1,2,0:T(8,128)}, u32[]{:S(2)}) copy-start(s32[2,1024,8]{1,2,0:T(8,128)} %param.13) | copy-start | bytes 196612
  1.6 22.5 %all-to-all-start = ((s32[64,1,32]{2,1,0:T(1,128)}), s32[64,1,32]{2,1,0:T(1,128)S(1)}, u32[]{:S(2)}, u32[]{:S(2)}) async-start(s32[64,1,32]{2,1,0:T(1,128)} %bitcast.1), calls=%async_computation | async-start | bytes 65536 | tf_op jit(solution)/shard_map/all_to_all | solution.py:352
  17.8 32.7 %copy-start.4 = (bf16[256,256]{1,0:T(8,128)(2,1)S(1)}, bf16[256,256]{1,0:T(8,128)(2,1)}, u32[]{:S(2)}) copy-start(bf16[256,256]{1,0:T(8,128)(2,1)} %two_ref.3) | copy-start | bytes 393220
  17.8 32.7 %copy-start.5 = (bf16[256,256]{1,0:T(8,128)(2,1)S(1)}, bf16[256,256]{1,0:T(8,128)(2,1)}, u32[]{:S(2)}) copy-start(bf16[256,256]{1,0:T(8,128)(2,1)} %first_ref.3) | copy-start | bytes 393220
  17.8 32.6 %copy-start.6 = (bf16[256,256]{1,0:T(8,128)(2,1)S(1)}, bf16[256,256]{1,0:T(8,128)(2,1)}, u32[]{:S(2)}) copy-start(bf16[256,256]{1,0:T(8,128)(2,1)} %second_ref.3) | copy-start | bytes 393220
  17.9 32.6 %copy-start.7 = (bf16[128,256]{1,0:T(8,128)(2,1)S(1)}, bf16[128,256]{1,0:T(8,128)(2,1)}, u32[]{:S(2)}) copy-start(bf16[128,256]{1,0:T(8,128)(2,1)} %one_ref.3) | copy-start | bytes 196612
  27.7 22.8 %copy-start.1 = (f8e4m3fn[2048,1024]{1,0:T(32,128)(4,1)S(1)}, f8e4m3fn[2048,1024]{1,0:T(32,128)(4,1)}, u32[]{:S(2)}) copy-start(f8e4m3fn[2048,1024]{1,0:T(32,128)(4,1)} %shard_map.94.slots_ref) | copy-start | bytes 6291460
  27.8 22.7 %all-to-all-start.1 = ((bf16[64,32,128]{2,1,0:T(8,128)(2,1)}), bf16[64,32,128]{2,1,0:T(8,128)(2,1)S(1)}, u32[]{:S(2)}, u32[]{:S(2)}) async-start(bf16[64,32,128]{2,1,0:T(8,128)(2,1)} %get-tuple-element.45), calls=%async_computation.1 | async-start | bytes 1048576 | tf_op jit(solution)/shard_map/all_to_all | solution.py:384
  32.8 9.8 %collective-permute-start.2 = (s32[64,32]{1,0:T(8,128)S(1)}, s32[64,32]{1,0:T(8,128)S(1)}, u32[]{:S(2)}, u32[]{:S(2)}) collective-permute-start(s32[64,32]{1,0:T(8,128)S(1)} %get-tuple-element.47), channel_id=1, source_target_pairs={{0,3},{1,0},{2,1},{3,2},{4,7},{5,4},{6,5},{7,6},{8,11},{9,8},{10,9... | collective-permute-start | bytes 24584 | tf_op jit(solution)/shard_map/ppermute | solution.py:348
  35.4 7.2 %collective-permute-start.1 = (s32[64,32]{1,0:T(8,128)S(1)}, s32[64,32]{1,0:T(8,128)S(1)}, u32[]{:S(2)}, u32[]{:S(2)}) collective-permute-start(s32[64,32]{1,0:T(8,128)S(1)} %get-tuple-element.47), channel_id=1, source_target_pairs={{0,2},{1,3},{2,0},{3,1},{4,6},{5,7},{6,4},{7,5},{8,10},{9,11},{10,... | collective-permute-start | bytes 24584 | tf_op jit(solution)/shard_map/ppermute | solution.py:348
  35.9 7.1 %collective-permute-start = (s32[64,32]{1,0:T(8,128)S(1)}, s32[64,32]{1,0:T(8,128)S(1)}, u32[]{:S(2)}, u32[]{:S(2)}) collective-permute-start(s32[64,32]{1,0:T(8,128)S(1)} %get-tuple-element.47), channel_id=1, source_target_pairs={{0,1},{1,2},{2,3},{3,0},{4,5},{5,6},{6,7},{7,4},{8,9},{9,10},{10,1... | collective-permute-start | bytes 24584 | tf_op jit(solution)/shard_map/ppermute | solution.py:348
  50.5 1.6 %copy-start.2 = (f8e4m3fn[2,1024,1024]{2,1,0:T(32,128)(4,1)S(1)}, f8e4m3fn[2,1024,1024]{2,1,0:T(32,128)(4,1)}, u32[]{:S(2)}) copy-start(f8e4m3fn[2,1024,1024]{2,1,0:T(32,128)(4,1)} %shard_map.93.edges_ref) | copy-start | bytes 6291460
  56.2 13.3 %collective-permute-start.4 = (bf16[256,512]{1,0:T(8,128)(2,1)S(1)}, bf16[256,512]{1,0:T(8,128)(2,1)S(1)}, u32[]{:S(2)}, u32[]{:S(2)}) collective-permute-start(bf16[256,512]{1,0:T(8,128)(2,1)S(1)} %get-tuple-element.54.key0_ref), channel_id=1, source_target_pairs={{0,3},{1,0},{2,1},{3,2},{4,7},{5,4},{6,5},{7,6},{8,11},{9,8},{10,9... | collective-permute-start | bytes 786440 | tf_op jit(solution)/shard_map/ppermute | solution.py:348
  58.8 10.8 %collective-permute-start.3 = (bf16[256,512]{1,0:T(8,128)(2,1)S(1)}, bf16[256,512]{1,0:T(8,128)(2,1)S(1)}, u32[]{:S(2)}, u32[]{:S(2)}) collective-permute-start(bf16[256,512]{1,0:T(8,128)(2,1)S(1)} %get-tuple-element.54.key0_ref), channel_id=1, source_target_pairs={{0,1},{1,2},{2,3},{3,0},{4,5},{5,6},{6,7},{7,4},{8,9},{9,10},{10,1... | collective-permute-start | bytes 786440 | tf_op jit(solution)/shard_map/ppermute | solution.py:348
  58.8 13.1 %collective-permute-start.5 = (bf16[256,512]{1,0:T(8,128)(2,1)S(1)}, bf16[256,512]{1,0:T(8,128)(2,1)S(1)}, u32[]{:S(2)}, u32[]{:S(2)}) collective-permute-start(bf16[256,512]{1,0:T(8,128)(2,1)S(1)} %get-tuple-element.54.key0_ref), channel_id=1, source_target_pairs={{0,2},{1,3},{2,0},{3,1},{4,6},{5,7},{6,4},{7,5},{8,10},{9,11},{10,... | collective-permute-start | bytes 786440 | tf_op jit(solution)/shard_map/ppermute | solution.py:348
  104.9 8.8 %collective-permute-start.6 = (bf16[1024,128]{1,0:T(8,128)(2,1)S(1)}, bf16[1024,128]{1,0:T(8,128)(2,1)S(1)}, u32[]{:S(2)}, u32[]{:S(2)}) collective-permute-start(bf16[1024,128]{1,0:T(8,128)(2,1)S(1)} %bitcast.21), channel_id=1, source_target_pairs={{0,1},{1,2},{2,3},{3,0},{4,5},{5,6},{6,7},{7,4},{8,9},{9,10},{10,1... | collective-permute-start | bytes 786440 | tf_op jit(solution)/shard_map/ppermute | solution.py:348
  105.0 9.4 %collective-permute-start.8 = (bf16[1024,128]{1,0:T(8,128)(2,1)S(1)}, bf16[1024,128]{1,0:T(8,128)(2,1)S(1)}, u32[]{:S(2)}, u32[]{:S(2)}) collective-permute-start(bf16[1024,128]{1,0:T(8,128)(2,1)S(1)} %bitcast.19), channel_id=1, source_target_pairs={{0,3},{1,0},{2,1},{3,2},{4,7},{5,4},{6,5},{7,6},{8,11},{9,8},{10,9... | collective-permute-start | bytes 786440 | tf_op jit(solution)/shard_map/ppermute | solution.py:348
  107.6 12.9 %collective-permute-start.11 = (bf16[1024,128]{1,0:T(8,128)(2,1)S(1)}, bf16[1024,128]{1,0:T(8,128)(2,1)S(1)}, u32[]{:S(2)}, u32[]{:S(2)}) collective-permute-start(bf16[1024,128]{1,0:T(8,128)(2,1)S(1)} %bitcast.22), channel_id=1, source_target_pairs={{0,3},{1,0},{2,1},{3,2},{4,7},{5,4},{6,5},{7,6},{8,11},{9,8},{10,9... | collective-permute-start | bytes 786440 | tf_op jit(solution)/shard_map/ppermute | solution.py:348
  107.7 12.9 %collective-permute-start.10 = (bf16[1024,128]{1,0:T(8,128)(2,1)S(1)}, bf16[1024,128]{1,0:T(8,128)(2,1)S(1)}, u32[]{:S(2)}, u32[]{:S(2)}) collective-permute-start(bf16[1024,128]{1,0:T(8,128)(2,1)S(1)} %bitcast.20), channel_id=1, source_target_pairs={{0,1},{1,2},{2,3},{3,0},{4,5},{5,6},{6,7},{7,4},{8,9},{9,10},{10,1... | collective-permute-start | bytes 786440 | tf_op jit(solution)/shard_map/ppermute | solution.py:348
  113.7 11.2 %collective-permute-start.7 = (bf16[1024,128]{1,0:T(8,128)(2,1)S(1)}, bf16[1024,128]{1,0:T(8,128)(2,1)S(1)}, u32[]{:S(2)}, u32[]{:S(2)}) collective-permute-start(bf16[1024,128]{1,0:T(8,128)(2,1)S(1)} %collective-permute-done.6.refs_2_), channel_id=1, source_target_pairs={{0,1},{1,2},{2,3},{3,0},{4,5},{5,6},{6,7},{7,4},{8,9},{9,10},{10,1... | collective-permute-start | bytes 786440 | tf_op jit(solution)/shard_map/ppermute | solution.py:348
  114.4 10.5 %collective-permute-start.9 = (bf16[1024,128]{1,0:T(8,128)(2,1)S(1)}, bf16[1024,128]{1,0:T(8,128)(2,1)S(1)}, u32[]{:S(2)}, u32[]{:S(2)}) collective-permute-start(bf16[1024,128]{1,0:T(8,128)(2,1)S(1)} %collective-permute-done.8.refs_5_), channel_id=1, source_target_pairs={{0,3},{1,0},{2,1},{3,2},{4,7},{5,4},{6,5},{7,6},{8,11},{9,8},{10,9... | collective-permute-start | bytes 786440 | tf_op jit(solution)/shard_map/ppermute | solution.py:348

commit v4 on v3

--- a/solution.py
+++ b/solution.py
@@ -126,7 +126,7 @@
 
 def forward_kernel(
     rows_ref, slots_ref, edges_ref, degree_ref, one_ref, two_ref, first_ref, second_ref,
-    keys_ref, raw_ref, hidden_ref, inner_ref, slope_ref, wide_slots_ref, wide_edges_ref,
+    keys_a_ref, keys_b_ref, raw_ref, hidden_ref, inner_ref, slope_ref, wide_slots_ref, wide_edges_ref,
 ):
     seeds = SEED_DEV
     width = rows_ref.shape[1]
@@ -151,7 +151,7 @@
         raw = tn(second_ref[...], projected)
         scale = lax.rsqrt(jnp.sum(raw * raw, axis=0, keepdims=True) + EPSILON)
         span = slice(view * seeds, (view + 1) * seeds)
-        keys_ref[:, span] = (raw * scale).astype(BF16)
+        (keys_a_ref, keys_b_ref)[view][...] = (raw * scale).astype(BF16)
         raw_ref[:, span] = raw
         inner_ref[:, span] = inner
         slope_ref[:, span] = jnp.where(before > 0.0, 1.0, grown)
@@ -179,8 +179,17 @@
     return jnp.sum(expo, axis=1, keepdims=True)
 
 
-def early_kernel(key0_ref, key1_ref, key3_ref, expo_ref, total0_ref, totals_ref):
-    own, ahead, behind = key0_ref[...], key1_ref[...], key3_ref[...]
+def joined(refs):
+    return jnp.concatenate([ref[...] for ref in refs], axis=1)
+
+
+def early_kernel(
+    key0a_ref, key0b_ref, key1a_ref, key1b_ref, key3a_ref, key3b_ref,
+    expo_ref, total0_ref, totals_ref,
+):
+    own = joined((key0a_ref, key0b_ref))
+    ahead = joined((key1a_ref, key1b_ref))
+    behind = joined((key3a_ref, key3b_ref))
     count = own.shape[1]
     same = diagonal(count)
     expo = pair_expo(own.T, own, same)
@@ -205,40 +214,43 @@
 
 
 def backward_kernel(
-    key0_ref, key1_ref, key3_ref, key2_ref, expo_ref, total0_ref, totals_ref,
+    key0a_ref, key0b_ref, key1a_ref, key1b_ref, key3a_ref, key3b_ref, key2a_ref, key2b_ref,
+    expo_ref, total0_ref, totals_ref,
     raw_ref, hidden_ref, inner_ref, slope_ref,
     slots_ref, edges_ref, degree_ref, one_ref, two_ref, first_ref, second_ref,
     grads_ref,
 ):
     seeds = SEED_DEV
-    far = key2_ref[...]
+    own = joined((key0a_ref, key0b_ref))
+    ahead = joined((key1a_ref, key1b_ref))
+    behind = joined((key3a_ref, key3b_ref))
+    far = joined((key2a_ref, key2b_ref))
     count = far.shape[1]
     left = far.T
-    last = pair_expo(left, key0_ref[...])
+    last = pair_expo(left, own)
     total0 = total0_ref[...] + down_sum(last)
     total2 = across_sum(last) + across_sum(pair_expo(left, far, diagonal(count)))
-    expo = pair_expo(left, key1_ref[...])
+    expo = pair_expo(left, ahead)
     total2 = total2 + across_sum(expo)
     total1 = totals_ref[:count, :] + flip(down_sum(expo))
-    expo = pair_expo(left, key3_ref[...])
+    expo = pair_expo(left, behind)
     total2 = total2 + across_sum(expo)
     total3 = totals_ref[count:, :] + flip(down_sum(expo))
     own_inverse = 1.0 / total0
     pulled = jnp.zeros(far.shape, F32)
     blocks = (
-        (key0_ref, expo_ref[:count, :], flip(total0)),
-        (key1_ref, expo_ref[count : 2 * count, :], total1),
-        (key3_ref, expo_ref[2 * count :, :], total3),
-        (key2_ref, last, total2),
-    )
-    for key_ref, expo, total in blocks:
+        (own, expo_ref[:count, :], flip(total0)),
+        (ahead, expo_ref[count : 2 * count, :], total1),
+        (behind, expo_ref[2 * count :, :], total3),
+        (far, last, total2),
+    )
+    for block, expo, total in blocks:
         weights = (expo * (own_inverse + 1.0 / total)).astype(BF16)
-        pulled = pulled + nn(key_ref[...], weights)
+        pulled = pulled + nn(block, weights)
     feature_grads = None
     for view in range(2):
         span = slice(view * seeds, (view + 1) * seeds)
-        other = slice((1 - view) * seeds, (2 - view) * seeds)
-        partner = key0_ref[:, other].astype(F32)
+        partner = (key0b_ref, key0a_ref)[view][...].astype(F32)
         key_grads = (pulled[:, span] - 2.0 * partner) * (1.0 / TEMPER)
         raw = raw_ref[:, span]
         scale = lax.rsqrt(jnp.sum(raw * raw, axis=0, keepdims=True) + EPSILON)
@@ -415,10 +427,11 @@
     rows = arrived.reshape(slot_count, width)
 
     wide = weight_one.shape[1]
-    keys, raw, hidden, inner, slope, slots, edges = call(
+    keys_a, keys_b, raw, hidden, inner, slope, slots, edges = call(
         forward_kernel,
         [
-            jax.ShapeDtypeStruct((wide, 2 * seeds), BF16),
+            jax.ShapeDtypeStruct((wide, seeds), BF16),
+            jax.ShapeDtypeStruct((wide, seeds), BF16),
             jax.ShapeDtypeStruct((wide, 2 * seeds), F32),
             jax.ShapeDtypeStruct((2, wide, nodes), BF16),
             jax.ShapeDtypeStruct((wide, 2 * seeds), BF16),
@@ -431,7 +444,9 @@
         moved=10_000_000,
         mib=32,
     )
-    ahead, far, behind = [turn(keys, by) for by in (1, 2, 3)]
+    ahead_b, behind_a = turn(keys_b, 1), turn(keys_a, 3)
+    ahead_a, behind_b = turn(keys_a, 1), turn(keys_b, 3)
+    far_b, far_a = turn(ahead_b, 1), turn(behind_a, 3)
     expo, total0, totals = call(
         early_kernel,
         [
@@ -439,7 +454,7 @@
             jax.ShapeDtypeStruct((1, 2 * seeds), F32),
             jax.ShapeDtypeStruct((4 * seeds, 1), F32),
         ],
-        [keys, ahead, behind],
+        [keys_a, keys_b, ahead_a, ahead_b, behind_a, behind_b],
         flops=800_000_000,
         moved=4_000_000,
         mib=16,
@@ -448,7 +463,8 @@
         backward_kernel,
         [jax.ShapeDtypeStruct((slot_count, width), BF16)],
         [
-            keys, ahead, behind, far, expo, total0, totals, raw, hidden, inner, slope,
+            keys_a, keys_b, ahead_a, ahead_b, behind_a, behind_b, far_a, far_b,
+            expo, total0, totals, raw, hidden, inner, slope,
             slots, edges, degree, weight_one, weight_two, proj_first, proj_second,
         ],
         flops=8_000_000_000,
@@ -463,7 +479,9 @@
     upper, lower = slice(0, half), slice(half, slot_count)
     from_left = [turn(returned[upper], 1)]
     from_right = [turn(returned[lower], 3)]
-    from_left[0], owned = lax.optimization_barrier((from_left[0], owned))
+    from_left[0], from_right[0], owned = lax.optimization_barrier(
+        (from_left[0], from_right[0], owned)
+    )
     owned = [
         (index, jnp.broadcast_to(part_of[:, None], (slot_count, width))) for index, part_of in owned
     ]

time: 128 us -> 125 us (0.977)
  waiting for transfers between devices: 31 us -> 25 us
  starting transfers between devices: 33.2 us -> 37.1 us
    ppermute x12 -> x15, waiting for transfers between devices: 17.6 us -> 11.5 us  [turn(): lax.ppermute(value, 'batch', [(source, (source + by) % batch_count) for s...]
    ppermute x12 -> x15, starting transfers between devices: 15.2 us -> 19 us  [turn(): lax.ppermute(value, 'batch', [(source, (source + by) % batch_count) for s...]
  transfers between devices with their start and end apart: 14 -> 17, of which waited for: 6 -> 6; matrix products, arithmetic and copies ran while one was open for 2% -> 2% of each run, Pallas kernels for 11% -> 11%
where the time goes in v4:
time: 125 us
  starting transfers between devices  37.1 us (30%)
  Pallas kernels  31.1 us (25%)
  blocking collectives  26.1 us (21%)
  waiting for transfers between devices  25 us (20%)
  local copies, waits for them, and re-layouts  4.45 us (4%)
    pallas_call x11, Pallas kernels, call(): pl.pallas_call(kernel, out_shape=outs, in_specs=[HBM if place in far else...  31.1 us
    all_to_all x1, blocking collectives, body(): lax.all_to_all(grads.reshape(table_count, -1, width), 'table', split_axis...  26.1 us
    ppermute x15, starting transfers between devices, turn(): lax.ppermute(value, 'batch', [(source, (source + by) % batch_count) for s...  19 us
    all_to_all x1, starting transfers between devices, body(): lax.all_to_all(requests, 'table', split_axis=0, concat_axis=0, tiled=True)  13.2 us
    ppermute x15, waiting for transfers between devices, turn(): lax.ppermute(value, 'batch', [(source, (source + by) % batch_count) for s...  11.5 us
    all_to_all x1, waiting for transfers between devices, body(): lax.all_to_all(fetched, 'table', split_axis=0, concat_axis=0, tiled=True)  7.32 us
    all_to_all x1, waiting for transfers between devices, body(): lax.all_to_all(requests, 'table', split_axis=0, concat_axis=0, tiled=True)  6.16 us
    all_to_all x1, starting transfers between devices, body(): lax.all_to_all(fetched, 'table', split_axis=0, concat_axis=0, tiled=True)  4.89 us
  transfers between devices with their start and end apart: 17, of which 6 were waited for; matrix products, arithmetic and copies ran while one was open for 2% of the time, Pallas kernels for 11%

profile of v4, /device:TPU:1, one launch (start us, length us, event | category | flops | bytes accessed | tf_op | source)
XLA Modules:
  0.0 124.7 jit_solution(14719317785316830075)
XLA Ops:
  0.0 0.8 copy-done.3
  0.9 0.7 shard_map.91
  1.6 13.2 %all-to-all-start = ((s32[64,1,32]{2,1,0:T(1,128)}), s32[64,1,32]{2,1,0:T(1,128)S(1)}, u32[]{:S(2)}, u32[]{:S(2)}) async-start(s32[64,1,32]{2,1,0:T(1,128)} %bitcast.1), calls=%async_computation | async-start | bytes 65536 | tf_op jit(solution)/shard_map/all_to_all | solution.py:364
  14.8 3.1 %shard_map.94.slots_ref = f8e4m3fn[2048,1024]{1,0:T(32,128)(4,1)} custom-call(s32[2,1024]{1,0:T(2,128)} %bitcast.24), custom_call_target="tpu_custom_call" | custom-call | flops 10000000 | bytes 4194304 | tf_op jit(solution)/shard_map/pallas_call | solution.py:39
  17.9 6.2 %all-to-all-done = s32[64,1,32]{2,1,0:T(1,128)S(1)} async-done(((s32[64,1,32]{2,1,0:T(1,128)}), s32[64,1,32]{2,1,0:T(1,128)S(1)}, u32[]{:S(2)}, u32[]{:S(2)}) %all-to-all-start) | async-done | bytes 8224 | tf_op jit(solution)/shard_map/all_to_all | solution.py:364
  24.1 3.7 %shard_map.92 = (bf16[64,32,128]{2,1,0:T(8,128)(2,1)}, s32[64,32]{1,0:T(8,128)S(1)}) custom-call(s32[64,32]{1,0:T(8,128)S(1)} %bitcast.18, bf16[8192,128]{1,0:T(8,128)(2,1)S(1)} %copy-done), custom_call_target="tpu_custom_call" | custom-call | flops 1000000 | bytes 6000000 | tf_op jit(solution)/shard_map/pallas_call | solution.py:39
  27.8 4.9 %all-to-all-start.1 = ((bf16[64,32,128]{2,1,0:T(8,128)(2,1)}), bf16[64,32,128]{2,1,0:T(8,128)(2,1)S(1)}, u32[]{:S(2)}, u32[]{:S(2)}) async-start(bf16[64,32,128]{2,1,0:T(8,128)(2,1)} %get-tuple-element.47), calls=%async_computation.1 | async-start | bytes 1048576 | tf_op jit(solution)/shard_map/all_to_all | solution.py:396
  32.8 2.6 %collective-permute-start.2 = (s32[64,32]{1,0:T(8,128)S(1)}, s32[64,32]{1,0:T(8,128)S(1)}, u32[]{:S(2)}, u32[]{:S(2)}) collective-permute-start(s32[64,32]{1,0:T(8,128)S(1)} %get-tuple-element.49), channel_id=1, source_target_pairs={{0,3},{1,0},{2,1},{3,2},{4,7},{5,4},{6,5},{7,6},{8,11},{9,8},{10,9... | collective-permute-start | bytes 24584 | tf_op jit(solution)/shard_map/ppermute | solution.py:360
  35.4 0.5 collective-permute-start.1
  35.9 0.6 collective-permute-start
  36.6 0.6 convert_bitcast_fusion.kept_ref
  37.2 5.4 %shard_map.93.edges_ref = f8e4m3fn[2,1024,1024]{2,1,0:T(32,128)(4,1)} custom-call(s32[8,1024]{1,0:T(8,128)} %bitcast.23, f32[2,8,1024]{2,1,0:T(8,128)} %convert_bitcast_fusion.kept_ref), custom_call_target="tpu_custom_call" | custom-call | flops 60000000 | bytes 4194304 | tf_op jit(solution)/shard_map/pallas_call | solution.py:39
  43.2 7.3 %all-to-all-done.1 = bf16[64,32,128]{2,1,0:T(8,128)(2,1)S(1)} async-done(((bf16[64,32,128]{2,1,0:T(8,128)(2,1)}), bf16[64,32,128]{2,1,0:T(8,128)(2,1)S(1)}, u32[]{:S(2)}, u32[]{:S(2)}) %all-to-all-start.1) | async-done | bytes 524320 | tf_op jit(solution)/shard_map/all_to_all | solution.py:396
  50.5 1.6 %copy-done.2 = f8e4m3fn[2,1024,1024]{2,1,0:T(32,128)(4,1)S(1)} copy-done((f8e4m3fn[2,1024,1024]{2,1,0:T(32,128)(4,1)S(1)}, f8e4m3fn[2,1024,1024]{2,1,0:T(32,128)(4,1)}, u32[]{:S(2)}) %copy-start.2) | copy-done | bytes 2097176
  52.1 4.1 %shard_map.95 = (bf16[256,256]{1,0:T(8,128)(2,1)S(1)}, bf16[256,256]{1,0:T(8,128)(2,1)S(1)}, f32[256,512]{1,0:T(8,128)S(1)}, bf16[2,256,1024]{2,1,0:T(8,128)(2,1...) custom-call(bf16[2048,128]{1,0:T(8,128)(2,1)S(1)} %bitcast.16, ...), custom_call_target="tpu_custom_call" | custom-call | flops 2400000000 | bytes 10000000 | tf_op jit(solution)/shard_map/pallas_call | solution.py:39
  56.2 2.6 %collective-permute-start.5 = (bf16[256,256]{1,0:T(8,128)(2,1)S(1)}, bf16[256,256]{1,0:T(8,128)(2,1)S(1)}, u32[]{:S(2)}, u32[]{:S(2)}) collective-permute-start(bf16[256,256]{1,0:T(8,128)(2,1)S(1)} %get-tuple-element.56.key0a_ref), channel_id=1, source_target_pairs={{0,3},{1,0},{2,1},{3,2},{4,7},{5,4},{6,5},{7,6},{8,11},{9,8},{10,9... | collective-permute-start | bytes 393224 | tf_op jit(solution)/shard_map/ppermute | solution.py:360
  59.0 2.5 %collective-permute-start.6 = (bf16[256,256]{1,0:T(8,128)(2,1)S(1)}, bf16[256,256]{1,0:T(8,128)(2,1)S(1)}, u32[]{:S(2)}, u32[]{:S(2)}) collective-permute-start(bf16[256,256]{1,0:T(8,128)(2,1)S(1)} %get-tuple-element.57.key0b_ref), channel_id=1, source_target_pairs={{0,3},{1,0},{2,1},{3,2},{4,7},{5,4},{6,5},{7,6},{8,11},{9,8},{10,9... | collective-permute-start | bytes 393224 | tf_op jit(solution)/shard_map/ppermute | solution.py:360
  61.5 3.2 %collective-permute-start.7 = (bf16[256,256]{1,0:T(8,128)(2,1)S(1)}, bf16[256,256]{1,0:T(8,128)(2,1)S(1)}, u32[]{:S(2)}, u32[]{:S(2)}) collective-permute-start(bf16[256,256]{1,0:T(8,128)(2,1)S(1)} %collective-permute-done.5.key3a_ref), channel_id=1, source_target_pairs={{0,3},{1,0},{2,1},{3,2},{4,7},{5,4},{6,5},{7,6},{8,11},{9,8},{10,9... | collective-permute-start | bytes 393224 | tf_op jit(solution)/shard_map/ppermute | solution.py:360
  64.7 2.5 %collective-permute-done.3.key1a_ref = bf16[256,256]{1,0:T(8,128)(2,1)S(1)} collective-permute-done((bf16[256,256]{1,0:T(8,128)(2,1)S(1)}, bf16[256,256]{1,0:T(8,128)(2,1)S(1)}, u32[]{:S(2)}, u32[]{:S(2)}) %collective-permute-start.3) | collective-permute-done | bytes 131104 | tf_op jit(solution)/shard_map/ppermute | solution.py:360
  67.2 1.4 %shard_map.96 = (f32[1536,512]{1,0:T(8,128)S(1)}, f32[1,512]{1,0:T(1,128)S(1)}, f32[1024,1]{1,0:T(8,128)S(1)}) custom-call(bf16[256,256]{1,0:T(8,128)(2,1)S(1)} %get-tuple-element.56.key0a_ref, bf16[256,256]{1,0:T(8,128)(2,1)S(1)} %get-tuple-element.57.key0b_ref, bf16[256,256]{1,0:T(8,128)(2,1)S(1)} %collective-permute-done.3.key1a_ref, ...), custom_call_target="tpu_custom_call" | custom-call | flops 800000000 | bytes 4000000 | tf_op jit(solution)/shard_map/pallas_call | solution.py:39
  68.6 1.1 collective-permute-done.8.key2b_ref
  69.7 6.7 %shard_map.97 = bf16[2048,128]{1,0:T(8,128)(2,1)S(1)} custom-call(bf16[256,256]{1,0:T(8,128)(2,1)S(1)} %get-tuple-element.56.key0a_ref, bf16[256,256]{1,0:T(8,128)(2,1)S(1)} %get-tuple-element.57.key0b_ref, bf16[256,256]{1,0:T(8,128)(2,1)S(1)} %collective-permute-done.3.key1a_ref, bf16[256,256]{1,0:T(8,128)(2,1)S(1)} %collective-permute-done.4.key1b_ref, ...), custom_call_target="tpu_custom_call" | custom-call | flops 8000000000 | bytes 12000000 | tf_op jit(solution)/shard_map/pallas_call | solution.py:39
  76.4 26.1 %all_to_all.21 = bf16[64,32,128]{2,1,0:T(8,128)(2,1)S(1)} all-to-all(bf16[64,32,128]{2,1,0:T(8,128)(2,1)S(1)} %bitcast.17), channel_id=1, replica_groups=mesh['table'=64,'batch'=4] {'table'}, dimensions={0} | all-to-all | bytes 1048576 | tf_op jit(solution)/shard_map/all_to_all | solution.py:474
  102.6 2.7 %collective-permute-start.10 = (bf16[1024,128]{1,0:T(8,128)(2,1)S(1)}, bf16[1024,128]{1,0:T(8,128)(2,1)S(1)}, u32[]{:S(2)}, u32[]{:S(2)}) collective-permute-start(bf16[1024,128]{1,0:T(8,128)(2,1)S(1)} %bitcast.19), channel_id=1, source_target_pairs={{0,3},{1,0},{2,1},{3,2},{4,7},{5,4},{6,5},{7,6},{8,11},{9,8},{10,9... | collective-permute-start | bytes 786440 | tf_op jit(solution)/shard_map/ppermute | solution.py:360
  105.3 1.4 %collective-permute-start.13 = (bf16[1024,128]{1,0:T(8,128)(2,1)S(1)}, bf16[1024,128]{1,0:T(8,128)(2,1)S(1)}, u32[]{:S(2)}, u32[]{:S(2)}) collective-permute-start(bf16[1024,128]{1,0:T(8,128)(2,1)S(1)} %bitcast.20), channel_id=1, source_target_pairs={{0,1},{1,2},{2,3},{3,0},{4,5},{5,6},{6,7},{7,4},{8,9},{9,10},{10,1... | collective-permute-start | bytes 786440 | tf_op jit(solution)/shard_map/ppermute | solution.py:360
  106.7 4.6 %collective-permute-done.9.refs_2_ = bf16[1024,128]{1,0:T(8,128)(2,1)S(1)} collective-permute-done((bf16[1024,128]{1,0:T(8,128)(2,1)S(1)}, bf16[1024,128]{1,0:T(8,128)(2,1)S(1)}, u32[]{:S(2)}, u32[]{:S(2)}) %collective-permute-start.9) | collective-permute-done | bytes 262176 | tf_op jit(solution)/shard_map/ppermute | solution.py:360
  111.3 2.7 %collective-permute-start.12 = (bf16[1024,128]{1,0:T(8,128)(2,1)S(1)}, bf16[1024,128]{1,0:T(8,128)(2,1)S(1)}, u32[]{:S(2)}, u32[]{:S(2)}) collective-permute-start(bf16[1024,128]{1,0:T(8,128)(2,1)S(1)} %collective-permute-done.10.refs_5_), channel_id=1, source_target_pairs={{0,3},{1,0},{2,1},{3,2},{4,7},{5,4},{6,5},{7,6},{8,11},{9,8},{10,9... | collective-permute-start | bytes 786440 | tf_op jit(solution)/shard_map/ppermute | solution.py:360
  114.6 1.3 %shard_map.98.refs_6_ = f32[2048,128]{1,0:T(8,128)S(1)} custom-call(s32[1,2048]{1,0:T(1,128)S(1)} %sub.90.refs_0_, bf16[2048,128]{1,0:T(8,128)(2,1)S(1)} %broadcast_in_dim.16.refs_1_, bf16[2048,128]{1,0:T(8,128)(2,1)S(1)} %bitcast.15), custom_call_target="tpu_custom_call" | custom-call | flops 1000000000 | bytes 4000000 | tf_op jit(solution)/shard_map/pallas_call | solution.py:39
  116.6 1.3 %shard_map.99.refs_6_ = f32[2048,128]{1,0:T(8,128)S(1)} custom-call(s32[1,2048]{1,0:T(1,128)S(1)} %sub.94.refs_0_, bf16[2048,128]{1,0:T(8,128)(2,1)S(1)} %broadcast_in_dim.18.refs_1_, bf16[1024,128]{1,0:T(8,128)(2,1)S(1)} %collective-permute-done.9.refs_2_, s32[1,2048]{1,0:T(1,128)S(1)} %sub.102.refs_3_, bf16[2048,128]{1,0:T(8,128)(2,1)S(1)} %broadcast_in_dim.19.refs_4_, ...), custom_call_target="tpu_custom_call" | custom-call | flops 1000000000 | bytes 4000000 | tf_op jit(solution)/shard_map/pallas_call | solution.py:39
  117.9 1.3 %shard_map.100.refs_6_ = f32[2048,128]{1,0:T(8,128)S(1)} custom-call(s32[1,2048]{1,0:T(1,128)S(1)} %sub.94.refs_0_, bf16[2048,128]{1,0:T(8,128)(2,1)S(1)} %broadcast_in_dim.18.refs_1_, bf16[1024,128]{1,0:T(8,128)(2,1)S(1)} %collective-permute-done.13.refs_2_, s32[1,2048]{1,0:T(1,128)S(1)} %sub.102.refs_3_, bf16[2048,128]{1,0:T(8,128)(2,1)S(1)} %broadcast_in_dim.19.refs_4_, ...), custom_call_target="tpu_custom_call" | custom-call | flops 1000000000 | bytes 4000000 | tf_op jit(solution)/shard_map/pallas_call | solution.py:39
  119.1 3.4 %collective-permute-done.11.refs_2_ = bf16[1024,128]{1,0:T(8,128)(2,1)S(1)} collective-permute-done((bf16[1024,128]{1,0:T(8,128)(2,1)S(1)}, bf16[1024,128]{1,0:T(8,128)(2,1)S(1)}, u32[]{:S(2)}, u32[]{:S(2)}) %collective-permute-start.11) | collective-permute-done | bytes 262176 | tf_op jit(solution)/shard_map/ppermute | solution.py:360
  122.5 2.2 %shard_map.101 = f32[2048,128]{1,0:T(8,128)} custom-call(s32[1,2048]{1,0:T(1,128)S(1)} %sub.98.refs_0_.refs_3_, bf16[2048,128]{1,0:T(8,128)(2,1)S(1)} %broadcast_in_dim.17.refs_1_.refs_4_, bf16[1024,128]{1,0:T(8,128)(2,1)S(1)} %collective-permute-done.11.refs_2_, s32[1,2048]{1,0:T(1,128)S(1)} %sub.98.refs_0_.refs_3_, ...), custom_call_target="tpu_custom_call" | custom-call | flops 1000000000 | bytes 4000000 | tf_op jit(solution)/shard_map/pallas_call | solution.py:39
  (56 shorter events, 2.5 us)
Async XLA Ops:
  0.0 24.1 %copy-start = (bf16[8192,128]{1,0:T(8,128)(2,1)S(1)}, bf16[8192,128]{1,0:T(8,128)(2,1)}, u32[]{:S(2)}) copy-start(bf16[8192,128]{1,0:T(8,128)(2,1)} %table_ref.1) | copy-start | bytes 6291460
  0.0 0.8 copy-start.3
  0.8 35.7 %copy-start.8 = (s32[2,1024,8]{1,2,0:T(8,128)S(1)}, s32[2,1024,8]{1,2,0:T(8,128)}, u32[]{:S(2)}) copy-start(s32[2,1024,8]{1,2,0:T(8,128)} %param.13) | copy-start | bytes 196612
  1.6 22.5 %all-to-all-start = ((s32[64,1,32]{2,1,0:T(1,128)}), s32[64,1,32]{2,1,0:T(1,128)S(1)}, u32[]{:S(2)}, u32[]{:S(2)}) async-start(s32[64,1,32]{2,1,0:T(1,128)} %bitcast.1), calls=%async_computation | async-start | bytes 65536 | tf_op jit(solution)/shard_map/all_to_all | solution.py:364
  17.8 32.6 %copy-start.4 = (bf16[256,256]{1,0:T(8,128)(2,1)S(1)}, bf16[256,256]{1,0:T(8,128)(2,1)}, u32[]{:S(2)}) copy-start(bf16[256,256]{1,0:T(8,128)(2,1)} %two_ref.3) | copy-start | bytes 393220
  17.9 32.6 %copy-start.5 = (bf16[256,256]{1,0:T(8,128)(2,1)S(1)}, bf16[256,256]{1,0:T(8,128)(2,1)}, u32[]{:S(2)}) copy-start(bf16[256,256]{1,0:T(8,128)(2,1)} %first_ref.3) | copy-start | bytes 393220
  17.9 32.6 %copy-start.6 = (bf16[256,256]{1,0:T(8,128)(2,1)S(1)}, bf16[256,256]{1,0:T(8,128)(2,1)}, u32[]{:S(2)}) copy-start(bf16[256,256]{1,0:T(8,128)(2,1)} %second_ref.3) | copy-start | bytes 393220
  17.9 32.6 %copy-start.7 = (bf16[128,256]{1,0:T(8,128)(2,1)S(1)}, bf16[128,256]{1,0:T(8,128)(2,1)}, u32[]{:S(2)}) copy-start(bf16[128,256]{1,0:T(8,128)(2,1)} %one_ref.3) | copy-start | bytes 196612
  27.7 22.8 %copy-start.1 = (f8e4m3fn[2048,1024]{1,0:T(32,128)(4,1)S(1)}, f8e4m3fn[2048,1024]{1,0:T(32,128)(4,1)}, u32[]{:S(2)}) copy-start(f8e4m3fn[2048,1024]{1,0:T(32,128)(4,1)} %shard_map.94.slots_ref) | copy-start | bytes 6291460
  27.8 22.7 %all-to-all-start.1 = ((bf16[64,32,128]{2,1,0:T(8,128)(2,1)}), bf16[64,32,128]{2,1,0:T(8,128)(2,1)S(1)}, u32[]{:S(2)}, u32[]{:S(2)}) async-start(bf16[64,32,128]{2,1,0:T(8,128)(2,1)} %get-tuple-element.47), calls=%async_computation.1 | async-start | bytes 1048576 | tf_op jit(solution)/shard_map/all_to_all | solution.py:396
  32.8 9.7 %collective-permute-start.2 = (s32[64,32]{1,0:T(8,128)S(1)}, s32[64,32]{1,0:T(8,128)S(1)}, u32[]{:S(2)}, u32[]{:S(2)}) collective-permute-start(s32[64,32]{1,0:T(8,128)S(1)} %get-tuple-element.49), channel_id=1, source_target_pairs={{0,3},{1,0},{2,1},{3,2},{4,7},{5,4},{6,5},{7,6},{8,11},{9,8},{10,9... | collective-permute-start | bytes 24584 | tf_op jit(solution)/shard_map/ppermute | solution.py:360
  35.4 7.2 %collective-permute-start.1 = (s32[64,32]{1,0:T(8,128)S(1)}, s32[64,32]{1,0:T(8,128)S(1)}, u32[]{:S(2)}, u32[]{:S(2)}) collective-permute-start(s32[64,32]{1,0:T(8,128)S(1)} %get-tuple-element.49), channel_id=1, source_target_pairs={{0,2},{1,3},{2,0},{3,1},{4,6},{5,7},{6,4},{7,5},{8,10},{9,11},{10,... | collective-permute-start | bytes 24584 | tf_op jit(solution)/shard_map/ppermute | solution.py:360
  35.9 7.0 %collective-permute-start = (s32[64,32]{1,0:T(8,128)S(1)}, s32[64,32]{1,0:T(8,128)S(1)}, u32[]{:S(2)}, u32[]{:S(2)}) collective-permute-start(s32[64,32]{1,0:T(8,128)S(1)} %get-tuple-element.49), channel_id=1, source_target_pairs={{0,1},{1,2},{2,3},{3,0},{4,5},{5,6},{6,7},{7,4},{8,9},{9,10},{10,1... | collective-permute-start | bytes 24584 | tf_op jit(solution)/shard_map/ppermute | solution.py:360
  50.5 1.6 %copy-start.2 = (f8e4m3fn[2,1024,1024]{2,1,0:T(32,128)(4,1)S(1)}, f8e4m3fn[2,1024,1024]{2,1,0:T(32,128)(4,1)}, u32[]{:S(2)}) copy-start(f8e4m3fn[2,1024,1024]{2,1,0:T(32,128)(4,1)} %shard_map.93.edges_ref) | copy-start | bytes 6291460
  56.2 5.3 %collective-permute-start.5 = (bf16[256,256]{1,0:T(8,128)(2,1)S(1)}, bf16[256,256]{1,0:T(8,128)(2,1)S(1)}, u32[]{:S(2)}, u32[]{:S(2)}) collective-permute-start(bf16[256,256]{1,0:T(8,128)(2,1)S(1)} %get-tuple-element.56.key0a_ref), channel_id=1, source_target_pairs={{0,3},{1,0},{2,1},{3,2},{4,7},{5,4},{6,5},{7,6},{8,11},{9,8},{10,9... | collective-permute-start | bytes 393224 | tf_op jit(solution)/shard_map/ppermute | solution.py:360
  58.8 5.9 %collective-permute-start.4 = (bf16[256,256]{1,0:T(8,128)(2,1)S(1)}, bf16[256,256]{1,0:T(8,128)(2,1)S(1)}, u32[]{:S(2)}, u32[]{:S(2)}) collective-permute-start(bf16[256,256]{1,0:T(8,128)(2,1)S(1)} %get-tuple-element.57.key0b_ref), channel_id=1, source_target_pairs={{0,1},{1,2},{2,3},{3,0},{4,5},{5,6},{6,7},{7,4},{8,9},{9,10},{10,1... | collective-permute-start | bytes 393224 | tf_op jit(solution)/shard_map/ppermute | solution.py:360
  58.8 8.4 %collective-permute-start.3 = (bf16[256,256]{1,0:T(8,128)(2,1)S(1)}, bf16[256,256]{1,0:T(8,128)(2,1)S(1)}, u32[]{:S(2)}, u32[]{:S(2)}) collective-permute-start(bf16[256,256]{1,0:T(8,128)(2,1)S(1)} %get-tuple-element.56.key0a_ref), channel_id=1, source_target_pairs={{0,1},{1,2},{2,3},{3,0},{4,5},{5,6},{6,7},{7,4},{8,9},{9,10},{10,1... | collective-permute-start | bytes 393224 | tf_op jit(solution)/shard_map/ppermute | solution.py:360
  59.0 8.2 %collective-permute-start.6 = (bf16[256,256]{1,0:T(8,128)(2,1)S(1)}, bf16[256,256]{1,0:T(8,128)(2,1)S(1)}, u32[]{:S(2)}, u32[]{:S(2)}) collective-permute-start(bf16[256,256]{1,0:T(8,128)(2,1)S(1)} %get-tuple-element.57.key0b_ref), channel_id=1, source_target_pairs={{0,3},{1,0},{2,1},{3,2},{4,7},{5,4},{6,5},{7,6},{8,11},{9,8},{10,9... | collective-permute-start | bytes 393224 | tf_op jit(solution)/shard_map/ppermute | solution.py:360
  61.5 7.1 %collective-permute-start.7 = (bf16[256,256]{1,0:T(8,128)(2,1)S(1)}, bf16[256,256]{1,0:T(8,128)(2,1)S(1)}, u32[]{:S(2)}, u32[]{:S(2)}) collective-permute-start(bf16[256,256]{1,0:T(8,128)(2,1)S(1)} %collective-permute-done.5.key3a_ref), channel_id=1, source_target_pairs={{0,3},{1,0},{2,1},{3,2},{4,7},{5,4},{6,5},{7,6},{8,11},{9,8},{10,9... | collective-permute-start | bytes 393224 | tf_op jit(solution)/shard_map/ppermute | solution.py:360
  64.7 5.0 %collective-permute-start.8 = (bf16[256,256]{1,0:T(8,128)(2,1)S(1)}, bf16[256,256]{1,0:T(8,128)(2,1)S(1)}, u32[]{:S(2)}, u32[]{:S(2)}) collective-permute-start(bf16[256,256]{1,0:T(8,128)(2,1)S(1)} %collective-permute-done.4.key1b_ref), channel_id=1, source_target_pairs={{0,1},{1,2},{2,3},{3,0},{4,5},{5,6},{6,7},{7,4},{8,9},{9,10},{10,1... | collective-permute-start | bytes 393224 | tf_op jit(solution)/shard_map/ppermute | solution.py:360
  102.5 8.8 %collective-permute-start.9 = (bf16[1024,128]{1,0:T(8,128)(2,1)S(1)}, bf16[1024,128]{1,0:T(8,128)(2,1)S(1)}, u32[]{:S(2)}, u32[]{:S(2)}) collective-permute-start(bf16[1024,128]{1,0:T(8,128)(2,1)S(1)} %bitcast.21), channel_id=1, source_target_pairs={{0,1},{1,2},{2,3},{3,0},{4,5},{5,6},{6,7},{7,4},{8,9},{9,10},{10,1... | collective-permute-start | bytes 786440 | tf_op jit(solution)/shard_map/ppermute | solution.py:360
  102.6 8.7 %collective-permute-start.10 = (bf16[1024,128]{1,0:T(8,128)(2,1)S(1)}, bf16[1024,128]{1,0:T(8,128)(2,1)S(1)}, u32[]{:S(2)}, u32[]{:S(2)}) collective-permute-start(bf16[1024,128]{1,0:T(8,128)(2,1)S(1)} %bitcast.19), channel_id=1, source_target_pairs={{0,3},{1,0},{2,1},{3,2},{4,7},{5,4},{6,5},{7,6},{8,11},{9,8},{10,9... | collective-permute-start | bytes 786440 | tf_op jit(solution)/shard_map/ppermute | solution.py:360
  105.2 12.6 %collective-permute-start.14 = (bf16[1024,128]{1,0:T(8,128)(2,1)S(1)}, bf16[1024,128]{1,0:T(8,128)(2,1)S(1)}, u32[]{:S(2)}, u32[]{:S(2)}) collective-permute-start(bf16[1024,128]{1,0:T(8,128)(2,1)S(1)} %bitcast.22), channel_id=1, source_target_pairs={{0,3},{1,0},{2,1},{3,2},{4,7},{5,4},{6,5},{7,6},{8,11},{9,8},{10,9... | collective-permute-start | bytes 786440 | tf_op jit(solution)/shard_map/ppermute | solution.py:360
  105.3 12.6 %collective-permute-start.13 = (bf16[1024,128]{1,0:T(8,128)(2,1)S(1)}, bf16[1024,128]{1,0:T(8,128)(2,1)S(1)}, u32[]{:S(2)}, u32[]{:S(2)}) collective-permute-start(bf16[1024,128]{1,0:T(8,128)(2,1)S(1)} %bitcast.20), channel_id=1, source_target_pairs={{0,1},{1,2},{2,3},{3,0},{4,5},{5,6},{6,7},{7,4},{8,9},{9,10},{10,1... | collective-permute-start | bytes 786440 | tf_op jit(solution)/shard_map/ppermute | solution.py:360
  111.3 11.2 %collective-permute-start.11 = (bf16[1024,128]{1,0:T(8,128)(2,1)S(1)}, bf16[1024,128]{1,0:T(8,128)(2,1)S(1)}, u32[]{:S(2)}, u32[]{:S(2)}) collective-permute-start(bf16[1024,128]{1,0:T(8,128)(2,1)S(1)} %collective-permute-done.9.refs_2_), channel_id=1, source_target_pairs={{0,1},{1,2},{2,3},{3,0},{4,5},{5,6},{6,7},{7,4},{8,9},{9,10},{10,1... | collective-permute-start | bytes 786440 | tf_op jit(solution)/shard_map/ppermute | solution.py:360
  111.3 11.2 %collective-permute-start.12 = (bf16[1024,128]{1,0:T(8,128)(2,1)S(1)}, bf16[1024,128]{1,0:T(8,128)(2,1)S(1)}, u32[]{:S(2)}, u32[]{:S(2)}) collective-permute-start(bf16[1024,128]{1,0:T(8,128)(2,1)S(1)} %collective-permute-done.10.refs_5_), channel_id=1, source_target_pairs={{0,3},{1,0},{2,1},{3,2},{4,7},{5,4},{6,5},{7,6},{8,11},{9,8},{10,9... | collective-permute-start | bytes 786440 | tf_op jit(solution)/shard_map/ppermute | solution.py:360

commit v5 on v4

--- a/solution.py
+++ b/solution.py
@@ -49,7 +49,7 @@
     )(*args)
 
 
-TILE, LANES, ROWS = 32, 128, 128
+TILE, LANES, ROWS = 32, 128, 256
 
 
 def spread(row, kind):
@@ -98,7 +98,7 @@
 
 def slots_kernel(slot_ref, slots_far, slots_ref, sem):
     hashes, nodes = slot_ref.shape
-    rows = min(256, slots_ref.shape[0])
+    rows = min(512, slots_ref.shape[0])
     one, none = jnp.ones((), BF16), jnp.zeros((), BF16)
     copies = []
     for part in range(nodes // LANES):
@@ -493,7 +493,8 @@
         ((0, slice(0, slot_count), returned),),
         ((1, upper, from_left[0]), (3, lower, from_right[0])),
         ((1, lower, from_left[1]), (3, upper, from_right[1])),
-        ((2, upper, from_far[0]), (2, lower, from_far[1])),
+        ((2, upper, from_far[0]),),
+        ((2, lower, from_far[1]),),
     )
     total = None
     for pieces in rounds:

time: 125 us -> 125 us (level); the launches traced: 125 us -> 123 us
  waiting for transfers between devices: 25 us -> 23.7 us
    ppermute x15, waiting for transfers between devices: 11.5 us -> 10 us  [turn(): lax.ppermute(value, 'batch', [(source, (source + by) % batch_count) for s...]
    pallas_call x11 -> x12, Pallas kernels: 31.1 us -> 31.1 us  [call(): pl.pallas_call(kernel, out_shape=outs, in_specs=[HBM if place in far else...]
  transfers between devices with their start and end apart: 17 -> 17, of which waited for: 6 -> 7; matrix products, arithmetic and copies ran while one was open for 2% -> 2% of each run, Pallas kernels for 11% -> 12%
where the time goes in v5:
time: 125 us; the launch traced here: 123 us
  starting transfers between devices  36.7 us (29%)
  Pallas kernels  31.1 us (25%)
  blocking collectives  26.1 us (21%)
  waiting for transfers between devices  23.7 us (19%)
  local copies, waits for them, and re-layouts  4.45 us (4%)
    pallas_call x12, Pallas kernels, call(): pl.pallas_call(kernel, out_shape=outs, in_specs=[HBM if place in far else...  31.1 us
    all_to_all x1, blocking collectives, body(): lax.all_to_all(grads.reshape(table_count, -1, width), 'table', split_axis...  26.1 us
    ppermute x15, starting transfers between devices, turn(): lax.ppermute(value, 'batch', [(source, (source + by) % batch_count) for s...  18.7 us
    all_to_all x1, starting transfers between devices, body(): lax.all_to_all(requests, 'table', split_axis=0, concat_axis=0, tiled=True)  13.2 us
    ppermute x15, waiting for transfers between devices, turn(): lax.ppermute(value, 'batch', [(source, (source + by) % batch_count) for s...  10 us
    all_to_all x1, waiting for transfers between devices, body(): lax.all_to_all(fetched, 'table', split_axis=0, concat_axis=0, tiled=True)  7.31 us
    all_to_all x1, waiting for transfers between devices, body(): lax.all_to_all(requests, 'table', split_axis=0, concat_axis=0, tiled=True)  6.33 us
    all_to_all x1, starting transfers between devices, body(): lax.all_to_all(fetched, 'table', split_axis=0, concat_axis=0, tiled=True)  4.89 us
  transfers between devices with their start and end apart: 17, of which 7 were waited for; matrix products, arithmetic and copies ran while one was open for 2% of the time, Pallas kernels for 12%

profile of v5, /device:TPU:1, one launch (start us, length us, event | category | flops | bytes accessed | tf_op | source)
XLA Modules:
  0.0 123.2 jit_solution(2520054101428207003)
XLA Ops:
  0.0 0.8 copy-done.3
  0.9 0.7 shard_map.91
  1.6 13.2 %all-to-all-start = ((s32[64,1,32]{2,1,0:T(1,128)}), s32[64,1,32]{2,1,0:T(1,128)S(1)}, u32[]{:S(2)}, u32[]{:S(2)}) async-start(s32[64,1,32]{2,1,0:T(1,128)} %bitcast.1), calls=%async_computation | async-start | bytes 65536 | tf_op jit(solution)/shard_map/all_to_all | solution.py:364
  14.8 2.9 %shard_map.94.slots_ref = f8e4m3fn[2048,1024]{1,0:T(32,128)(4,1)} custom-call(s32[2,1024]{1,0:T(2,128)} %bitcast.24), custom_call_target="tpu_custom_call" | custom-call | flops 10000000 | bytes 4194304 | tf_op jit(solution)/shard_map/pallas_call | solution.py:39
  17.7 6.3 %all-to-all-done = s32[64,1,32]{2,1,0:T(1,128)S(1)} async-done(((s32[64,1,32]{2,1,0:T(1,128)}), s32[64,1,32]{2,1,0:T(1,128)S(1)}, u32[]{:S(2)}, u32[]{:S(2)}) %all-to-all-start) | async-done | bytes 8224 | tf_op jit(solution)/shard_map/all_to_all | solution.py:364
  24.1 3.7 %shard_map.92 = (bf16[64,32,128]{2,1,0:T(8,128)(2,1)}, s32[64,32]{1,0:T(8,128)S(1)}) custom-call(s32[64,32]{1,0:T(8,128)S(1)} %bitcast.18, bf16[8192,128]{1,0:T(8,128)(2,1)S(1)} %copy-done), custom_call_target="tpu_custom_call" | custom-call | flops 1000000 | bytes 6000000 | tf_op jit(solution)/shard_map/pallas_call | solution.py:39
  27.8 4.9 %all-to-all-start.1 = ((bf16[64,32,128]{2,1,0:T(8,128)(2,1)}), bf16[64,32,128]{2,1,0:T(8,128)(2,1)S(1)}, u32[]{:S(2)}, u32[]{:S(2)}) async-start(bf16[64,32,128]{2,1,0:T(8,128)(2,1)} %get-tuple-element.47), calls=%async_computation.1 | async-start | bytes 1048576 | tf_op jit(solution)/shard_map/all_to_all | solution.py:396
  32.8 2.6 %collective-permute-start.2 = (s32[64,32]{1,0:T(8,128)S(1)}, s32[64,32]{1,0:T(8,128)S(1)}, u32[]{:S(2)}, u32[]{:S(2)}) collective-permute-start(s32[64,32]{1,0:T(8,128)S(1)} %get-tuple-element.49), channel_id=1, source_target_pairs={{0,3},{1,0},{2,1},{3,2},{4,7},{5,4},{6,5},{7,6},{8,11},{9,8},{10,9... | collective-permute-start | bytes 24584 | tf_op jit(solution)/shard_map/ppermute | solution.py:360
  35.9 0.6 collective-permute-start
  36.6 0.6 convert_bitcast_fusion.kept_ref
  37.2 5.4 %shard_map.93.edges_ref = f8e4m3fn[2,1024,1024]{2,1,0:T(32,128)(4,1)} custom-call(s32[8,1024]{1,0:T(8,128)} %bitcast.23, f32[2,8,1024]{2,1,0:T(8,128)} %convert_bitcast_fusion.kept_ref), custom_call_target="tpu_custom_call" | custom-call | flops 60000000 | bytes 4194304 | tf_op jit(solution)/shard_map/pallas_call | solution.py:39
  43.2 7.3 %all-to-all-done.1 = bf16[64,32,128]{2,1,0:T(8,128)(2,1)S(1)} async-done(((bf16[64,32,128]{2,1,0:T(8,128)(2,1)}), bf16[64,32,128]{2,1,0:T(8,128)(2,1)S(1)}, u32[]{:S(2)}, u32[]{:S(2)}) %all-to-all-start.1) | async-done | bytes 524320 | tf_op jit(solution)/shard_map/all_to_all | solution.py:396
  50.5 1.6 %copy-done.2 = f8e4m3fn[2,1024,1024]{2,1,0:T(32,128)(4,1)S(1)} copy-done((f8e4m3fn[2,1024,1024]{2,1,0:T(32,128)(4,1)S(1)}, f8e4m3fn[2,1024,1024]{2,1,0:T(32,128)(4,1)}, u32[]{:S(2)}) %copy-start.2) | copy-done | bytes 2097176
  52.1 4.1 %shard_map.95 = (bf16[256,256]{1,0:T(8,128)(2,1)S(1)}, bf16[256,256]{1,0:T(8,128)(2,1)S(1)}, f32[256,512]{1,0:T(8,128)S(1)}, bf16[2,256,1024]{2,1,0:T(8,128)(2,1...) custom-call(bf16[2048,128]{1,0:T(8,128)(2,1)S(1)} %bitcast.16, ...), custom_call_target="tpu_custom_call" | custom-call | flops 2400000000 | bytes 10000000 | tf_op jit(solution)/shard_map/pallas_call | solution.py:39
  56.2 2.6 %collective-permute-start.5 = (bf16[256,256]{1,0:T(8,128)(2,1)S(1)}, bf16[256,256]{1,0:T(8,128)(2,1)S(1)}, u32[]{:S(2)}, u32[]{:S(2)}) collective-permute-start(bf16[256,256]{1,0:T(8,128)(2,1)S(1)} %get-tuple-element.56.key0a_ref), channel_id=1, source_target_pairs={{0,3},{1,0},{2,1},{3,2},{4,7},{5,4},{6,5},{7,6},{8,11},{9,8},{10,9... | collective-permute-start | bytes 393224 | tf_op jit(solution)/shard_map/ppermute | solution.py:360
  59.0 2.5 %collective-permute-start.6 = (bf16[256,256]{1,0:T(8,128)(2,1)S(1)}, bf16[256,256]{1,0:T(8,128)(2,1)S(1)}, u32[]{:S(2)}, u32[]{:S(2)}) collective-permute-start(bf16[256,256]{1,0:T(8,128)(2,1)S(1)} %get-tuple-element.57.key0b_ref), channel_id=1, source_target_pairs={{0,3},{1,0},{2,1},{3,2},{4,7},{5,4},{6,5},{7,6},{8,11},{9,8},{10,9... | collective-permute-start | bytes 393224 | tf_op jit(solution)/shard_map/ppermute | solution.py:360
  61.5 3.2 %collective-permute-start.7 = (bf16[256,256]{1,0:T(8,128)(2,1)S(1)}, bf16[256,256]{1,0:T(8,128)(2,1)S(1)}, u32[]{:S(2)}, u32[]{:S(2)}) collective-permute-start(bf16[256,256]{1,0:T(8,128)(2,1)S(1)} %collective-permute-done.5.key3a_ref), channel_id=1, source_target_pairs={{0,3},{1,0},{2,1},{3,2},{4,7},{5,4},{6,5},{7,6},{8,11},{9,8},{10,9... | collective-permute-start | bytes 393224 | tf_op jit(solution)/shard_map/ppermute | solution.py:360
  64.7 2.5 %collective-permute-done.3.key1a_ref = bf16[256,256]{1,0:T(8,128)(2,1)S(1)} collective-permute-done((bf16[256,256]{1,0:T(8,128)(2,1)S(1)}, bf16[256,256]{1,0:T(8,128)(2,1)S(1)}, u32[]{:S(2)}, u32[]{:S(2)}) %collective-permute-start.3) | collective-permute-done | bytes 131104 | tf_op jit(solution)/shard_map/ppermute | solution.py:360
  67.2 1.4 %shard_map.96 = (f32[1536,512]{1,0:T(8,128)S(1)}, f32[1,512]{1,0:T(1,128)S(1)}, f32[1024,1]{1,0:T(8,128)S(1)}) custom-call(bf16[256,256]{1,0:T(8,128)(2,1)S(1)} %get-tuple-element.56.key0a_ref, bf16[256,256]{1,0:T(8,128)(2,1)S(1)} %get-tuple-element.57.key0b_ref, bf16[256,256]{1,0:T(8,128)(2,1)S(1)} %collective-permute-done.3.key1a_ref, ...), custom_call_target="tpu_custom_call" | custom-call | flops 800000000 | bytes 4000000 | tf_op jit(solution)/shard_map/pallas_call | solution.py:39
  68.6 1.1 collective-permute-done.8.key2b_ref
  69.7 6.7 %shard_map.97 = bf16[2048,128]{1,0:T(8,128)(2,1)S(1)} custom-call(bf16[256,256]{1,0:T(8,128)(2,1)S(1)} %get-tuple-element.56.key0a_ref, bf16[256,256]{1,0:T(8,128)(2,1)S(1)} %get-tuple-element.57.key0b_ref, bf16[256,256]{1,0:T(8,128)(2,1)S(1)} %collective-permute-done.3.key1a_ref, bf16[256,256]{1,0:T(8,128)(2,1)S(1)} %collective-permute-done.4.key1b_ref, ...), custom_call_target="tpu_custom_call" | custom-call | flops 8000000000 | bytes 12000000 | tf_op jit(solution)/shard_map/pallas_call | solution.py:39
  76.4 26.1 %all_to_all.21 = bf16[64,32,128]{2,1,0:T(8,128)(2,1)S(1)} all-to-all(bf16[64,32,128]{2,1,0:T(8,128)(2,1)S(1)} %bitcast.17), channel_id=1, replica_groups=mesh['table'=64,'batch'=4] {'table'}, dimensions={0} | all-to-all | bytes 1048576 | tf_op jit(solution)/shard_map/all_to_all | solution.py:474
  102.6 2.7 %collective-permute-start.10 = (bf16[1024,128]{1,0:T(8,128)(2,1)S(1)}, bf16[1024,128]{1,0:T(8,128)(2,1)S(1)}, u32[]{:S(2)}, u32[]{:S(2)}) collective-permute-start(bf16[1024,128]{1,0:T(8,128)(2,1)S(1)} %bitcast.19), channel_id=1, source_target_pairs={{0,3},{1,0},{2,1},{3,2},{4,7},{5,4},{6,5},{7,6},{8,11},{9,8},{10,9... | collective-permute-start | bytes 786440 | tf_op jit(solution)/shard_map/ppermute | solution.py:360
  105.3 1.4 %collective-permute-start.13 = (bf16[1024,128]{1,0:T(8,128)(2,1)S(1)}, bf16[1024,128]{1,0:T(8,128)(2,1)S(1)}, u32[]{:S(2)}, u32[]{:S(2)}) collective-permute-start(bf16[1024,128]{1,0:T(8,128)(2,1)S(1)} %bitcast.20), channel_id=1, source_target_pairs={{0,1},{1,2},{2,3},{3,0},{4,5},{5,6},{6,7},{7,4},{8,9},{9,10},{10,1... | collective-permute-start | bytes 786440 | tf_op jit(solution)/shard_map/ppermute | solution.py:360
  106.7 4.6 %collective-permute-done.9.refs_2_ = bf16[1024,128]{1,0:T(8,128)(2,1)S(1)} collective-permute-done((bf16[1024,128]{1,0:T(8,128)(2,1)S(1)}, bf16[1024,128]{1,0:T(8,128)(2,1)S(1)}, u32[]{:S(2)}, u32[]{:S(2)}) %collective-permute-start.9) | collective-permute-done | bytes 262176 | tf_op jit(solution)/shard_map/ppermute | solution.py:360
  111.3 2.4 %collective-permute-start.11 = (bf16[1024,128]{1,0:T(8,128)(2,1)S(1)}, bf16[1024,128]{1,0:T(8,128)(2,1)S(1)}, u32[]{:S(2)}, u32[]{:S(2)}) collective-permute-start(bf16[1024,128]{1,0:T(8,128)(2,1)S(1)} %collective-permute-done.10.refs_5_), channel_id=1, source_target_pairs={{0,3},{1,0},{2,1},{3,2},{4,7},{5,4},{6,5},{7,6},{8,11},{9,8},{10,9... | collective-permute-start | bytes 786440 | tf_op jit(solution)/shard_map/ppermute | solution.py:360
  114.3 1.3 %shard_map.98.refs_6_ = f32[2048,128]{1,0:T(8,128)S(1)} custom-call(s32[1,2048]{1,0:T(1,128)S(1)} %sub.90.refs_0_, bf16[2048,128]{1,0:T(8,128)(2,1)S(1)} %broadcast_in_dim.16.refs_1_, bf16[2048,128]{1,0:T(8,128)(2,1)S(1)} %bitcast.15), custom_call_target="tpu_custom_call" | custom-call | flops 1000000000 | bytes 4000000 | tf_op jit(solution)/shard_map/pallas_call | solution.py:39
  116.3 1.3 %shard_map.99.refs_6_ = f32[2048,128]{1,0:T(8,128)S(1)} custom-call(s32[1,2048]{1,0:T(1,128)S(1)} %sub.94.refs_0_, bf16[2048,128]{1,0:T(8,128)(2,1)S(1)} %broadcast_in_dim.18.refs_1_, bf16[1024,128]{1,0:T(8,128)(2,1)S(1)} %collective-permute-done.9.refs_2_, s32[1,2048]{1,0:T(1,128)S(1)} %sub.102.refs_3_, bf16[2048,128]{1,0:T(8,128)(2,1)S(1)} %broadcast_in_dim.19.refs_4_, ...), custom_call_target="tpu_custom_call" | custom-call | flops 1000000000 | bytes 4000000 | tf_op jit(solution)/shard_map/pallas_call | solution.py:39
  117.6 1.3 %shard_map.100.refs_3_ = f32[2048,128]{1,0:T(8,128)S(1)} custom-call(s32[1,2048]{1,0:T(1,128)S(1)} %sub.94.refs_0_, bf16[2048,128]{1,0:T(8,128)(2,1)S(1)} %broadcast_in_dim.18.refs_1_, bf16[1024,128]{1,0:T(8,128)(2,1)S(1)} %collective-permute-done.13.refs_2_, s32[1,2048]{1,0:T(1,128)S(1)} %sub.102.refs_3_, bf16[2048,128]{1,0:T(8,128)(2,1)S(1)} %broadcast_in_dim.19.refs_4_, ...), custom_call_target="tpu_custom_call" | custom-call | flops 1000000000 | bytes 4000000 | tf_op jit(solution)/shard_map/pallas_call | solution.py:39
  118.8 1.4 %collective-permute-done.12.refs_2_ = bf16[1024,128]{1,0:T(8,128)(2,1)S(1)} collective-permute-done((bf16[1024,128]{1,0:T(8,128)(2,1)S(1)}, bf16[1024,128]{1,0:T(8,128)(2,1)S(1)}, u32[]{:S(2)}, u32[]{:S(2)}) %collective-permute-start.12) | collective-permute-done | bytes 262176 | tf_op jit(solution)/shard_map/ppermute | solution.py:360
  120.2 0.7 shard_map.101.refs_3_
  121.5 1.7 %shard_map.102 = f32[2048,128]{1,0:T(8,128)} custom-call(s32[1,2048]{1,0:T(1,128)S(1)} %sub.98.refs_0_, bf16[2048,128]{1,0:T(8,128)(2,1)S(1)} %broadcast_in_dim.17.refs_1_, bf16[1024,128]{1,0:T(8,128)(2,1)S(1)} %collective-permute-done.11.refs_2_, f32[2048,128]{1,0:T(8,128)S(1)} %shard_map.101.refs_3_), custom_call_target="tpu_custom_call" | custom-call | flops 1000000000 | bytes 4000000 | tf_op jit(solution)/shard_map/pallas_call | solution.py:39
  (57 shorter events, 3.5 us)
Async XLA Ops:
  0.0 24.1 %copy-start = (bf16[8192,128]{1,0:T(8,128)(2,1)S(1)}, bf16[8192,128]{1,0:T(8,128)(2,1)}, u32[]{:S(2)}) copy-start(bf16[8192,128]{1,0:T(8,128)(2,1)} %table_ref.1) | copy-start | bytes 6291460
  0.0 0.8 copy-start.3
  0.8 35.7 %copy-start.8 = (s32[2,1024,8]{1,2,0:T(8,128)S(1)}, s32[2,1024,8]{1,2,0:T(8,128)}, u32[]{:S(2)}) copy-start(s32[2,1024,8]{1,2,0:T(8,128)} %param.13) | copy-start | bytes 196612
  1.6 22.5 %all-to-all-start = ((s32[64,1,32]{2,1,0:T(1,128)}), s32[64,1,32]{2,1,0:T(1,128)S(1)}, u32[]{:S(2)}, u32[]{:S(2)}) async-start(s32[64,1,32]{2,1,0:T(1,128)} %bitcast.1), calls=%async_computation | async-start | bytes 65536 | tf_op jit(solution)/shard_map/all_to_all | solution.py:364
  17.7 32.8 %copy-start.4 = (bf16[256,256]{1,0:T(8,128)(2,1)S(1)}, bf16[256,256]{1,0:T(8,128)(2,1)}, u32[]{:S(2)}) copy-start(bf16[256,256]{1,0:T(8,128)(2,1)} %two_ref.3) | copy-start | bytes 393220
  17.7 32.8 %copy-start.5 = (bf16[256,256]{1,0:T(8,128)(2,1)S(1)}, bf16[256,256]{1,0:T(8,128)(2,1)}, u32[]{:S(2)}) copy-start(bf16[256,256]{1,0:T(8,128)(2,1)} %first_ref.3) | copy-start | bytes 393220
  17.7 32.8 %copy-start.6 = (bf16[256,256]{1,0:T(8,128)(2,1)S(1)}, bf16[256,256]{1,0:T(8,128)(2,1)}, u32[]{:S(2)}) copy-start(bf16[256,256]{1,0:T(8,128)(2,1)} %second_ref.3) | copy-start | bytes 393220
  17.7 32.8 %copy-start.7 = (bf16[128,256]{1,0:T(8,128)(2,1)S(1)}, bf16[128,256]{1,0:T(8,128)(2,1)}, u32[]{:S(2)}) copy-start(bf16[128,256]{1,0:T(8,128)(2,1)} %one_ref.3) | copy-start | bytes 196612
  27.7 22.8 %copy-start.1 = (f8e4m3fn[2048,1024]{1,0:T(32,128)(4,1)S(1)}, f8e4m3fn[2048,1024]{1,0:T(32,128)(4,1)}, u32[]{:S(2)}) copy-start(f8e4m3fn[2048,1024]{1,0:T(32,128)(4,1)} %shard_map.94.slots_ref) | copy-start | bytes 6291460
  27.8 22.7 %all-to-all-start.1 = ((bf16[64,32,128]{2,1,0:T(8,128)(2,1)}), bf16[64,32,128]{2,1,0:T(8,128)(2,1)S(1)}, u32[]{:S(2)}, u32[]{:S(2)}) async-start(bf16[64,32,128]{2,1,0:T(8,128)(2,1)} %get-tuple-element.47), calls=%async_computation.1 | async-start | bytes 1048576 | tf_op jit(solution)/shard_map/all_to_all | solution.py:396
  32.8 9.8 %collective-permute-start.2 = (s32[64,32]{1,0:T(8,128)S(1)}, s32[64,32]{1,0:T(8,128)S(1)}, u32[]{:S(2)}, u32[]{:S(2)}) collective-permute-start(s32[64,32]{1,0:T(8,128)S(1)} %get-tuple-element.49), channel_id=1, source_target_pairs={{0,3},{1,0},{2,1},{3,2},{4,7},{5,4},{6,5},{7,6},{8,11},{9,8},{10,9... | collective-permute-start | bytes 24584 | tf_op jit(solution)/shard_map/ppermute | solution.py:360
  35.4 7.2 %collective-permute-start.1 = (s32[64,32]{1,0:T(8,128)S(1)}, s32[64,32]{1,0:T(8,128)S(1)}, u32[]{:S(2)}, u32[]{:S(2)}) collective-permute-start(s32[64,32]{1,0:T(8,128)S(1)} %get-tuple-element.49), channel_id=1, source_target_pairs={{0,2},{1,3},{2,0},{3,1},{4,6},{5,7},{6,4},{7,5},{8,10},{9,11},{10,... | collective-permute-start | bytes 24584 | tf_op jit(solution)/shard_map/ppermute | solution.py:360
  35.9 7.0 %collective-permute-start = (s32[64,32]{1,0:T(8,128)S(1)}, s32[64,32]{1,0:T(8,128)S(1)}, u32[]{:S(2)}, u32[]{:S(2)}) collective-permute-start(s32[64,32]{1,0:T(8,128)S(1)} %get-tuple-element.49), channel_id=1, source_target_pairs={{0,1},{1,2},{2,3},{3,0},{4,5},{5,6},{6,7},{7,4},{8,9},{9,10},{10,1... | collective-permute-start | bytes 24584 | tf_op jit(solution)/shard_map/ppermute | solution.py:360
  50.5 1.6 %copy-start.2 = (f8e4m3fn[2,1024,1024]{2,1,0:T(32,128)(4,1)S(1)}, f8e4m3fn[2,1024,1024]{2,1,0:T(32,128)(4,1)}, u32[]{:S(2)}) copy-start(f8e4m3fn[2,1024,1024]{2,1,0:T(32,128)(4,1)} %shard_map.93.edges_ref) | copy-start | bytes 6291460
  56.2 5.3 %collective-permute-start.5 = (bf16[256,256]{1,0:T(8,128)(2,1)S(1)}, bf16[256,256]{1,0:T(8,128)(2,1)S(1)}, u32[]{:S(2)}, u32[]{:S(2)}) collective-permute-start(bf16[256,256]{1,0:T(8,128)(2,1)S(1)} %get-tuple-element.56.key0a_ref), channel_id=1, source_target_pairs={{0,3},{1,0},{2,1},{3,2},{4,7},{5,4},{6,5},{7,6},{8,11},{9,8},{10,9... | collective-permute-start | bytes 393224 | tf_op jit(solution)/shard_map/ppermute | solution.py:360
  58.8 5.9 %collective-permute-start.4 = (bf16[256,256]{1,0:T(8,128)(2,1)S(1)}, bf16[256,256]{1,0:T(8,128)(2,1)S(1)}, u32[]{:S(2)}, u32[]{:S(2)}) collective-permute-start(bf16[256,256]{1,0:T(8,128)(2,1)S(1)} %get-tuple-element.57.key0b_ref), channel_id=1, source_target_pairs={{0,1},{1,2},{2,3},{3,0},{4,5},{5,6},{6,7},{7,4},{8,9},{9,10},{10,1... | collective-permute-start | bytes 393224 | tf_op jit(solution)/shard_map/ppermute | solution.py:360
  58.8 8.4 %collective-permute-start.3 = (bf16[256,256]{1,0:T(8,128)(2,1)S(1)}, bf16[256,256]{1,0:T(8,128)(2,1)S(1)}, u32[]{:S(2)}, u32[]{:S(2)}) collective-permute-start(bf16[256,256]{1,0:T(8,128)(2,1)S(1)} %get-tuple-element.56.key0a_ref), channel_id=1, source_target_pairs={{0,1},{1,2},{2,3},{3,0},{4,5},{5,6},{6,7},{7,4},{8,9},{9,10},{10,1... | collective-permute-start | bytes 393224 | tf_op jit(solution)/shard_map/ppermute | solution.py:360
  59.0 8.2 %collective-permute-start.6 = (bf16[256,256]{1,0:T(8,128)(2,1)S(1)}, bf16[256,256]{1,0:T(8,128)(2,1)S(1)}, u32[]{:S(2)}, u32[]{:S(2)}) collective-permute-start(bf16[256,256]{1,0:T(8,128)(2,1)S(1)} %get-tuple-element.57.key0b_ref), channel_id=1, source_target_pairs={{0,3},{1,0},{2,1},{3,2},{4,7},{5,4},{6,5},{7,6},{8,11},{9,8},{10,9... | collective-permute-start | bytes 393224 | tf_op jit(solution)/shard_map/ppermute | solution.py:360
  61.5 7.1 %collective-permute-start.7 = (bf16[256,256]{1,0:T(8,128)(2,1)S(1)}, bf16[256,256]{1,0:T(8,128)(2,1)S(1)}, u32[]{:S(2)}, u32[]{:S(2)}) collective-permute-start(bf16[256,256]{1,0:T(8,128)(2,1)S(1)} %collective-permute-done.5.key3a_ref), channel_id=1, source_target_pairs={{0,3},{1,0},{2,1},{3,2},{4,7},{5,4},{6,5},{7,6},{8,11},{9,8},{10,9... | collective-permute-start | bytes 393224 | tf_op jit(solution)/shard_map/ppermute | solution.py:360
  64.7 5.0 %collective-permute-start.8 = (bf16[256,256]{1,0:T(8,128)(2,1)S(1)}, bf16[256,256]{1,0:T(8,128)(2,1)S(1)}, u32[]{:S(2)}, u32[]{:S(2)}) collective-permute-start(bf16[256,256]{1,0:T(8,128)(2,1)S(1)} %collective-permute-done.4.key1b_ref), channel_id=1, source_target_pairs={{0,1},{1,2},{2,3},{3,0},{4,5},{5,6},{6,7},{7,4},{8,9},{9,10},{10,1... | collective-permute-start | bytes 393224 | tf_op jit(solution)/shard_map/ppermute | solution.py:360
  102.5 8.8 %collective-permute-start.9 = (bf16[1024,128]{1,0:T(8,128)(2,1)S(1)}, bf16[1024,128]{1,0:T(8,128)(2,1)S(1)}, u32[]{:S(2)}, u32[]{:S(2)}) collective-permute-start(bf16[1024,128]{1,0:T(8,128)(2,1)S(1)} %bitcast.21), channel_id=1, source_target_pairs={{0,1},{1,2},{2,3},{3,0},{4,5},{5,6},{6,7},{7,4},{8,9},{9,10},{10,1... | collective-permute-start | bytes 786440 | tf_op jit(solution)/shard_map/ppermute | solution.py:360
  102.6 8.7 %collective-permute-start.10 = (bf16[1024,128]{1,0:T(8,128)(2,1)S(1)}, bf16[1024,128]{1,0:T(8,128)(2,1)S(1)}, u32[]{:S(2)}, u32[]{:S(2)}) collective-permute-start(bf16[1024,128]{1,0:T(8,128)(2,1)S(1)} %bitcast.19), channel_id=1, source_target_pairs={{0,3},{1,0},{2,1},{3,2},{4,7},{5,4},{6,5},{7,6},{8,11},{9,8},{10,9... | collective-permute-start | bytes 786440 | tf_op jit(solution)/shard_map/ppermute | solution.py:360
  105.2 12.3 %collective-permute-start.14 = (bf16[1024,128]{1,0:T(8,128)(2,1)S(1)}, bf16[1024,128]{1,0:T(8,128)(2,1)S(1)}, u32[]{:S(2)}, u32[]{:S(2)}) collective-permute-start(bf16[1024,128]{1,0:T(8,128)(2,1)S(1)} %bitcast.22), channel_id=1, source_target_pairs={{0,3},{1,0},{2,1},{3,2},{4,7},{5,4},{6,5},{7,6},{8,11},{9,8},{10,9... | collective-permute-start | bytes 786440 | tf_op jit(solution)/shard_map/ppermute | solution.py:360
  105.3 12.3 %collective-permute-start.13 = (bf16[1024,128]{1,0:T(8,128)(2,1)S(1)}, bf16[1024,128]{1,0:T(8,128)(2,1)S(1)}, u32[]{:S(2)}, u32[]{:S(2)}) collective-permute-start(bf16[1024,128]{1,0:T(8,128)(2,1)S(1)} %bitcast.20), channel_id=1, source_target_pairs={{0,1},{1,2},{2,3},{3,0},{4,5},{5,6},{6,7},{7,4},{8,9},{9,10},{10,1... | collective-permute-start | bytes 786440 | tf_op jit(solution)/shard_map/ppermute | solution.py:360
  111.3 10.2 %collective-permute-start.11 = (bf16[1024,128]{1,0:T(8,128)(2,1)S(1)}, bf16[1024,128]{1,0:T(8,128)(2,1)S(1)}, u32[]{:S(2)}, u32[]{:S(2)}) collective-permute-start(bf16[1024,128]{1,0:T(8,128)(2,1)S(1)} %collective-permute-done.10.refs_5_), channel_id=1, source_target_pairs={{0,3},{1,0},{2,1},{3,2},{4,7},{5,4},{6,5},{7,6},{8,11},{9,8},{10,9... | collective-permute-start | bytes 786440 | tf_op jit(solution)/shard_map/ppermute | solution.py:360
  113.6 6.6 %collective-permute-start.12 = (bf16[1024,128]{1,0:T(8,128)(2,1)S(1)}, bf16[1024,128]{1,0:T(8,128)(2,1)S(1)}, u32[]{:S(2)}, u32[]{:S(2)}) collective-permute-start(bf16[1024,128]{1,0:T(8,128)(2,1)S(1)} %collective-permute-done.9.refs_2_), channel_id=1, source_target_pairs={{0,1},{1,2},{2,3},{3,0},{4,5},{5,6},{6,7},{7,4},{8,9},{9,10},{10,1... | collective-permute-start | bytes 786440 | tf_op jit(solution)/shard_map/ppermute | solution.py:360
